TPU v7x, 32 devices: a whole 2x2x4 slice. The times are simulated.
32 devices in a mesh: row: 8 (over z, x), grp: 4 (over y, core).
Axes of the slice: x: 2, y: 2, z: 4, core: 2. Of those that a mesh axis runs over, the one named last changes fastest.
Arguments:
- features: bfloat16 [32768, 256], P(('row', 'grp')), may hold values from -6 to 6
- weight: bfloat16 [256, 256], replicated, may hold values from -0.375 to 0.375
- cotangent: bfloat16 [32768, 256], P(('row', 'grp')), may hold values from -6 to 6
- adjacency_tiles: bfloat16 [2048, 128, 128], P(('row', 'grp')), may hold values from -0.25 to 0.25
- tile_rows: int32 [2048], P(('row', 'grp')), may hold values from 0 to 7
- tile_cols: int32 [2048], P(('row', 'grp')), may hold values from 0 to 31
- tile_counts: int32 [32], P(('row', 'grp')), may hold values from 1 to 64, 1024 in all
Outputs:
- activated: bfloat16 [32768, 256], P(('row', 'grp'))
- feature_grad: bfloat16 [32768, 256], P(('row', 'grp'))
- weight_grad: float32 [256, 256], replicated
Inputs may be any that keep to these rules, and one draw needn't show every extreme that they name: `tile_counts`: some device has all 64 slots live.
All inputs are finite; a program needn't handle non-finite values.
Results may differ from a plain program's by a relative error of at most 0.009.
Values may be sent and summed in bfloat16 or wider, within the bound.
No kernel may reach another device: no remote copies, remote signals or barrier semaphores. Data moves between devices by JAX's collectives and lax.ppermute only.
A program may use at most 64 MiB of HBM per device.

v0:
```python
import math

import jax
import jax.numpy as jnp
from jax import lax
from jax.sharding import PartitionSpec as P

HID = 256
TILE = 128


def local(features, weight, cotangent, adjacency_tiles, tile_rows, tile_cols, tile_counts):
    node_dev = features.shape[0]
    blocks_dev = node_dev // TILE
    members = lax.axis_size("grp")
    group_blocks = blocks_dev * members
    slot_count = adjacency_tiles.shape[0]
    block_size = math.gcd(16, slot_count)
    live_count = tile_counts[0]
    block_count = (live_count + block_size - 1) // block_size
    offsets = jnp.arange(block_size, dtype=jnp.int32)

    def slot_block(block):
        first_slot = block * block_size
        tile_vals = lax.dynamic_slice_in_dim(adjacency_tiles, first_slot, block_size, 0)
        row_index = lax.dynamic_slice_in_dim(tile_rows, first_slot, block_size, 0)
        col_index = lax.dynamic_slice_in_dim(tile_cols, first_slot, block_size, 0)
        live_mask = (first_slot + offsets < live_count).astype(jnp.float32)
        return (tile_vals, row_index, col_index, live_mask)

    projected = jnp.dot(features, weight, preferred_element_type=jnp.float32).astype(jnp.bfloat16)
    preact_zero = jnp.zeros((blocks_dev, TILE, HID), jnp.float32)
    panels = lax.all_gather(projected, "grp", axis=0, tiled=True).reshape(group_blocks, TILE, HID)

    def advance(block, preact):
        tile_vals, row_index, col_index, live_mask = slot_block(block)
        products = jnp.einsum(
            "tik,tkj->tij", tile_vals, panels[col_index], preferred_element_type=jnp.float32
        )
        return preact.at[row_index].add(products * live_mask[:, None, None])

    preact = lax.fori_loop(0, block_count, advance, preact_zero)
    sigmoid_z = jax.nn.sigmoid(preact)
    activated = (preact * sigmoid_z).astype(jnp.bfloat16).reshape(node_dev, HID)
    own_cot = cotangent.reshape(blocks_dev, TILE, HID).astype(jnp.float32)
    slope = (own_cot * sigmoid_z * (1.0 + preact * (1.0 - sigmoid_z))).astype(jnp.bfloat16)

    def backward_block(block, partial_sum):
        tile_vals, row_index, col_index, live_mask = slot_block(block)
        contrib = jnp.einsum(
            "tki,tkj->tij", tile_vals, slope[row_index], preferred_element_type=jnp.float32
        )
        return partial_sum.at[col_index].add(contrib * live_mask[:, None, None])

    partial_sum = lax.fori_loop(
        0, block_count, backward_block, jnp.zeros((group_blocks, TILE, HID), jnp.float32)
    )
    partial_bf = partial_sum.astype(jnp.bfloat16)
    partial_rows = partial_bf.reshape(group_blocks * TILE, HID)
    panel_sum = lax.psum_scatter(
        partial_rows.astype(jnp.float32).astype(jnp.bfloat16),
        "grp",
        scatter_dimension=0,
        tiled=True,
    )
    feature_grad = lax.dot_general(
        panel_sum, weight, (((1,), (1,)), ((), ())), preferred_element_type=jnp.float32
    ).astype(jnp.bfloat16)
    weight_part = lax.dot_general(
        features, panel_sum, (((0,), (0,)), ((), ())), preferred_element_type=jnp.float32
    )
    weight_grad = lax.psum(weight_part, ("row", "grp"))
    return (activated, feature_grad, weight_grad)


def solution(mesh):
    placed = (
        P(("row", "grp"), None),
        P(),
        P(("row", "grp"), None),
        P(("row", "grp"), None, None),
        P(("row", "grp")),
        P(("row", "grp")),
        P(("row", "grp")),
    )
    return jax.shard_map(
        local,
        mesh=mesh,
        in_specs=placed,
        out_specs=(P(("row", "grp"), None), P(("row", "grp"), None), P()),
        check_vma=False,
    )
```

profile of v0, /device:TPU:0, one launch (start us, length us, event | category | flops | bytes accessed | tf_op | source)
XLA Modules:
  0.0 292.8 jit_solution(1288798040956321759)
XLA Ops:
  7.2 0.0 copy-start
  7.2 0.0 copy-start.3
  7.2 0.0 copy-start.2
  7.2 0.0 all-gather.2.cloned.1.call-start
  7.2 1.0 copy-done
  8.2 2.0 convolution_convert_fusion.1
  10.2 0.0 all-gather.2.cloned.1.call-update
  10.2 0.0 reduce-scatter.2.cloned.1.call-start
  11.0 24.7 %all-gather.2.cloned.1.call-done = bf16[4096,256]{1,0:T(8,128)(2,1)} async-done(((bf16[1024,256]{1,0:T(8,128)(2,1)}), bf16[4096,256]{1,0:T(8,128)(2,1)}) %all-gather.2.cloned.1.call-update) | async-done | bytes 2097168 | tf_op jit(solution)/shard_map/all_gather | solution.py:33
  35.7 1.1 broadcast_in_dim.20
  36.8 0.0 copy-done.3
  36.8 0.0 copy-done.2
  36.8 30.3 %while.22 = (s32[]{:T(128)}, f32[8,128,256]{2,1,0:T(8,128)}, s32[]{:T(128)}, s32[64]{0:T(128)S(1)}, bf16[64,128,128]{2,1,0:T(8,128)(2,1)}, /*index=5*/s32[64]{0:...) while((s32[]{:T(128)}, f32[8,128,256]{2,1,0:T(8,128)}, ...), condition=%wide.region_2.3_spmd.clone, body=%wide.region_0.2_spmd.clone.sunk | while | flops 135267472 | bytes 12063475 | solution.py:42
  36.8 0.6 compare_convert_fusion.4
  37.4 0.1 compare_select_fusion.6
  37.5 3.2 %gather_fusion = bf16[16,128,256]{2,1,0:T(8,128)(2,1)} fusion(bf16[32,128,256]{2,1,0:T(8,128)(2,1)} %get-tuple-element.326, s32[1024]{0:T(1024)S(1)} %pad_clamp_fusion.4), kind=kCustom, calls=%fused_computation.clone.clone.1 | custom fusion | bytes 2097216 | tf_op jit(solution)/shard_map/while/body/gather | solution.py:38
  40.7 1.8 convolution_multiply_fusion.4
  42.5 4.3 %scatter_fusion = f32[8,128,256]{2,1,0:T(8,128)} fusion(f32[8,128,256]{2,1,0:T(8,128)} %get-tuple-element.309, s32[16]{0:T(128)S(1)} %get-tuple-element.284, f32[16,128,256]{2,1,0:T(8,128)S(1)} %convolution_multiply_fusion.4), kind=kCustom, calls=%fused_computation.2.clone.clone.1 | custom fusion | flops 524288 | bytes 6291520 | tf_op jit(solution)/shard_map/while/body/scatter-add | solution.py:40
  46.9 0.6 compare_convert_fusion.4
  47.5 0.1 compare_select_fusion.6
  47.6 3.2 %gather_fusion = bf16[16,128,256]{2,1,0:T(8,128)(2,1)} fusion(bf16[32,128,256]{2,1,0:T(8,128)(2,1)} %get-tuple-element.326, s32[1024]{0:T(1024)S(1)} %pad_clamp_fusion.4), kind=kCustom, calls=%fused_computation.clone.clone.1 | custom fusion | bytes 2097216 | tf_op jit(solution)/shard_map/while/body/gather | solution.py:38
  50.8 1.8 convolution_multiply_fusion.4
  52.6 4.3 %scatter_fusion = f32[8,128,256]{2,1,0:T(8,128)} fusion(f32[8,128,256]{2,1,0:T(8,128)} %get-tuple-element.309, s32[16]{0:T(128)S(1)} %get-tuple-element.284, f32[16,128,256]{2,1,0:T(8,128)S(1)} %convolution_multiply_fusion.4), kind=kCustom, calls=%fused_computation.2.clone.clone.1 | custom fusion | flops 524288 | bytes 6291520 | tf_op jit(solution)/shard_map/while/body/scatter-add | solution.py:40
  56.9 0.6 compare_convert_fusion.4
  57.6 0.1 compare_select_fusion.6
  57.7 3.2 %gather_fusion = bf16[16,128,256]{2,1,0:T(8,128)(2,1)} fusion(bf16[32,128,256]{2,1,0:T(8,128)(2,1)} %get-tuple-element.326, s32[1024]{0:T(1024)S(1)} %pad_clamp_fusion.4), kind=kCustom, calls=%fused_computation.clone.clone.1 | custom fusion | bytes 2097216 | tf_op jit(solution)/shard_map/while/body/gather | solution.py:38
  60.9 1.8 convolution_multiply_fusion.4
  62.7 4.4 %scatter_fusion = f32[8,128,256]{2,1,0:T(8,128)} fusion(f32[8,128,256]{2,1,0:T(8,128)} %get-tuple-element.309, s32[16]{0:T(128)S(1)} %get-tuple-element.284, f32[16,128,256]{2,1,0:T(8,128)S(1)} %convolution_multiply_fusion.4), kind=kCustom, calls=%fused_computation.2.clone.clone.1 | custom fusion | flops 524288 | bytes 6291520 | tf_op jit(solution)/shard_map/while/body/scatter-add | solution.py:40
  67.1 2.6 fusion.9
  69.7 2.4 broadcast_in_dim.21
  72.1 26.1 %while.23 = (s32[]{:T(128)}, f32[32,128,256]{2,1,0:T(8,128)}, s32[]{:T(128)}, s32[64]{0:T(128)S(1)}, bf16[64,128,128]{2,1,0:T(8,128)(2,1)}, /*index=5*/s32[64]{0...) while((s32[]{:T(128)}, f32[32,128,256]{2,1,0:T(8,128)}, ...), condition=%wide.region_5.6_spmd.clone, body=%wide.region_3.5_spmd.clone.sunk | while | flops 135267472 | bytes 12063475 | solution.py:55
  72.1 0.6 compare_convert_fusion.5
  72.8 0.1 compare_select_fusion.7
  72.9 1.6 gather_fusion.1
  74.5 1.9 convolution_multiply_fusion.5
  76.4 4.5 %scatter_fusion.1 = f32[32,128,256]{2,1,0:T(8,128)} fusion(f32[32,128,256]{2,1,0:T(8,128)} %get-tuple-element.345, s32[16]{0:T(128)S(1)} %get-tuple-element.294, f32[16,128,256]{2,1,0:T(8,128)S(1)} %convolution_multiply_fusion.5), kind=kCustom, calls=%fused_computation.3.clone.clone.1 | custom fusion | flops 524288 | bytes 6291520 | tf_op jit(solution)/shard_map/while/body/scatter-add | solution.py:53
  80.8 0.6 compare_convert_fusion.5
  81.5 0.1 compare_select_fusion.7
  81.5 1.6 gather_fusion.1
  83.1 1.9 convolution_multiply_fusion.5
  85.0 4.5 %scatter_fusion.1 = f32[32,128,256]{2,1,0:T(8,128)} fusion(f32[32,128,256]{2,1,0:T(8,128)} %get-tuple-element.345, s32[16]{0:T(128)S(1)} %get-tuple-element.294, f32[16,128,256]{2,1,0:T(8,128)S(1)} %convolution_multiply_fusion.5), kind=kCustom, calls=%fused_computation.3.clone.clone.1 | custom fusion | flops 524288 | bytes 6291520 | tf_op jit(solution)/shard_map/while/body/scatter-add | solution.py:53
  89.5 0.6 compare_convert_fusion.5
  90.2 0.1 compare_select_fusion.7
  90.3 1.6 gather_fusion.1
  91.9 1.9 convolution_multiply_fusion.5
  93.7 4.5 %scatter_fusion.1 = f32[32,128,256]{2,1,0:T(8,128)} fusion(f32[32,128,256]{2,1,0:T(8,128)} %get-tuple-element.345, s32[16]{0:T(128)S(1)} %get-tuple-element.294, f32[16,128,256]{2,1,0:T(8,128)S(1)} %convolution_multiply_fusion.5), kind=kCustom, calls=%fused_computation.3.clone.clone.1 | custom fusion | flops 524288 | bytes 6291520 | tf_op jit(solution)/shard_map/while/body/scatter-add | solution.py:53
  98.2 3.8 %convert_element_type.42 = bf16[32,128,256]{2,1,0:T(8,128)(2,1)} convert(f32[32,128,256]{2,1,0:T(8,128)} %get-tuple-element.100) | non-fusion elementwise | flops 1048576 | bytes 6291456 | tf_op jit(solution)/shard_map/convert_element_type | solution.py:58
  102.0 0.0 copy-start.1
  102.0 0.0 reduce-scatter.2.cloned.1.call-update
  102.0 0.0 all-reduce.2.cloned.1.call-start
  102.1 50.3 %reduce-scatter.2.cloned.1.call-done = bf16[1024,256]{1,0:T(8,128)(2,1)} async-done(((bf16[4096,256]{1,0:T(8,128)(2,1)}), bf16[1024,256]{1,0:T(8,128)(2,1)}) %reduce-scatter.2.cloned.1.call-update) | async-done | bytes 524304 | tf_op jit(solution)/shard_map/reduce_scatter | solution.py:60
  152.4 2.1 convolution_bitcast_fusion
  154.5 0.0 all-reduce.2.cloned.1.call-update
  154.5 0.0 copy-done.1
  154.5 2.2 convolution_convert_fusion
  156.7 127.7 %all-reduce.2.cloned.1.call-done = f32[256,256]{0,1:T(8,128)} async-done(((f32[256,256]{0,1:T(8,128)}), f32[256,256]{0,1:T(8,128)}) %all-reduce.2.cloned.1.call-update) | async-done | bytes 262160 | tf_op jit(solution)/shard_map/psum | solution.py:72
  284.4 1.8 copy.11
  (6 shorter events, 0.0 us)
Async XLA Ops:
  7.2 1.0 copy-start
  7.2 29.6 %copy-start.3 = (s32[64]{0:T(128)S(1)}, s32[64]{0:T(128)}, u32[]{:S(2)}) copy-start(s32[64]{0:T(128)} %param.16) | copy-start | bytes 772
  7.2 29.6 %copy-start.2 = (s32[64]{0:T(128)S(1)}, s32[64]{0:T(128)}, u32[]{:S(2)}) copy-start(s32[64]{0:T(128)} %param.15) | copy-start | bytes 772
  7.2 28.5 %all-gather.2.cloned.1.call-start = ((), (), s32[]{:S(2)}) async-start(), calls=%async_computation.1 | async-start | bytes 2621440 | tf_op jit(solution)/shard_map/all_gather | solution.py:33
  10.2 142.2 %reduce-scatter.2.cloned.1.call-start = ((), (), s32[]{:S(2)}) async-start(), calls=%async_computation.2 | async-start | bytes 2621440 | tf_op jit(solution)/shard_map/reduce_scatter | solution.py:60
  102.0 52.5 %copy-start.1 = (bf16[256,256]{1,0:T(8,128)(2,1)S(1)}, bf16[256,256]{1,0:T(8,128)(2,1)}, u32[]{:S(2)}) copy-start(bf16[256,256]{1,0:T(8,128)(2,1)} %param.12) | copy-start | bytes 393220
  102.0 182.4 %all-reduce.2.cloned.1.call-start = ((), (), s32[]{:S(2)}) async-start(), calls=%async_computation.3 | async-start | bytes 524288 | tf_op jit(solution)/shard_map/psum | solution.py:72
Sparse Core Ops, SparseCore 0:
  10.4 25.2 all-gather.1
  102.2 50.2 reduce-scatter.1
  159.4 124.9 all-reduce.1
where the time goes:
time: 294 us; the launch traced here: 293 us
  waiting for transfers between devices  203 us (69%)
  other arithmetic  37.3 us (13%)
  local copies, waits for them, and re-layouts  20.6 us (7%)
  matrix products  17.3 us (6%)
  between operations  14.4 us (5%)
    psum x1, waiting for transfers between devices, local(): weight_grad = lax.psum(weight_part, ('row', 'grp'))  128 us
    reduce_scatter x1, waiting for transfers between devices, local(): lax.psum_scatter(partial_rows.astype(jnp.float32).astype(jnp.bfloat16), '...  50.3 us
    all_gather x1, waiting for transfers between devices, local(): lax.all_gather(projected, 'grp', axis=0, tiled=True)  24.7 us
    scatter-add x3, other arithmetic, backward_block(): return partial_sum.at[col_index].add(contrib * live_mask[:, None, None])  13.4 us
    scatter-add x3, other arithmetic, advance(): return preact.at[row_index].add(products * live_mask[:, None, None])  13 us
    gather x3, local copies, waits for them, and re-layouts, advance(): panels[col_index]  9.58 us
  transfers between devices with their start and end apart: 3, of which 3 were waited for; matrix products, arithmetic and copies ran while one was open for 1% of the time, Pallas kernels for 0%

commit v1 on v0

v1 whole, which is shorter than its diff:
```python
import functools

import jax
import jax.numpy as jnp
from jax import lax
from jax.experimental import pallas as pl
from jax.experimental.pallas import tpu as pltpu
from jax.sharding import PartitionSpec as P

TILE = 128
UNROLL = 4
F32 = jnp.float32
BF16 = jnp.bfloat16

SMEM = pl.BlockSpec(memory_space=pltpu.SMEM)
VMEM = pl.BlockSpec(memory_space=pltpu.VMEM)


def params(mib):
    return pltpu.CompilerParams(vmem_limit_bytes=mib << 20)


def prep_body(cats, blocks_dev, cnt_ref, rows_ref, cols_ref, me_ref, list_ref, offs_ref, pos):
    live = cnt_ref[0]
    me = me_ref[0]
    half = blocks_dev // 2
    if cats == 1:
        pad_col = 0
        pad_acc = me_ref[1]
    else:
        pad_col = 0
        pad_acc = half
    pad = (blocks_dev << 8) | (pad_col << 16) | (pad_acc << 23)
    for k in range(cats):
        pos[k] = 0

    def blank(i, carry):
        list_ref[i] = pad
        return carry

    lax.fori_loop(0, list_ref.shape[0], blank, 0)

    def category(s):
        col = cols_ref[s]
        if cats == 1:
            return 0, col, col
        rel = lax.bitwise_xor(col // blocks_dev, me)
        local = lax.rem(col, blocks_dev)
        part = local // half
        return rel * 2 + part, local, local - part * half

    def count(s, carry):
        k = category(s)[0]
        pos[k] = pos[k] + 1
        return carry

    lax.fori_loop(0, live, count, 0)
    group = jnp.int32(0)
    for k in range(cats):
        n = pos[k]
        offs_ref[k] = group
        pos[k] = group * UNROLL
        group = group + (n + UNROLL - 1) // UNROLL
    offs_ref[cats] = group

    def place(s, carry):
        k, local, acc = category(s)
        p = pos[k]
        pos[k] = p + 1
        list_ref[p] = s | (rows_ref[s] << 8) | (local << 16) | (acc << 23)
        return carry

    lax.fori_loop(0, live, place, 0)


def tile_of(e):
    return e & 255


def row_of(e):
    return (e >> 8) & 255


def col_of(e):
    return (e >> 16) & 127


def acc_of(e):
    return e >> 23


def rows_at(block, n=TILE):
    return pl.ds(pl.multiple_of(block * TILE, TILE), n)


def forward_groups(list_ref, lo, hi, tiles_ref, x_ref, acc, mask):
    def step(g, carry):
        es = [list_ref[g * UNROLL + u] for u in range(UNROLL)]
        ds = [
            jnp.dot(
                tiles_ref[tile_of(e)],
                x_ref[rows_at(col_of(e) & mask), :],
                preferred_element_type=F32,
            )
            for e in es
        ]
        for e, d in zip(es, ds):
            acc[row_of(e)] += d
        return carry

    lax.fori_loop(lo, hi, step, 0)


def backward_groups(list_ref, lo, hi, tiles_ref, s_ref, acc, row_mask, by_half):
    def step(g, carry):
        es = [list_ref[g * UNROLL + u] for u in range(UNROLL)]
        ds = [
            lax.dot_general(
                tiles_ref[tile_of(e)],
                s_ref[rows_at(row_of(e) & row_mask), :],
                (((0,), (0,)), ((), ())),
                preferred_element_type=F32,
            )
            for e in es
        ]
        for e, d in zip(es, ds):
            acc[acc_of(e)] += d
        return carry

    lax.fori_loop(lo, hi, step, 0)


def forward_body(phases, masks, final, blocks_dev, first, refs):
    refs = list(refs)
    list_ref, offs_ref, tiles_ref = refs[:3]
    refs = refs[3:]
    xs = refs[: len(phases)]
    refs = refs[len(phases):]
    if not first:
        acc_in = refs.pop(0)
    if final:
        w_ref, cot_ref, core_ref = refs[:3]
        act_ref, sw_ref, keep_ref, send_ref = refs[3:7]
        refs = refs[7:]
        acc, wg = refs
    else:
        acc_out = refs[0]
        acc = refs[1]
    if first:
        acc[...] = jnp.zeros_like(acc)
    else:
        acc[0:blocks_dev] = acc_in[...]
    for (lo, hi), x_ref, mask in zip(phases, xs, masks):
        forward_groups(list_ref, offs_ref[lo], offs_ref[hi], tiles_ref, x_ref, acc, mask)
    if not final:
        acc_out[...] = acc[0:blocks_dev]
        return
    hid = w_ref.shape[0]
    w = w_ref[...]
    step_blocks = 4
    for b in range(0, blocks_dev, step_blocks):
        n = step_blocks * TILE
        agg = acc[b:b + step_blocks].reshape(n, hid).astype(BF16)
        pre = jnp.dot(agg, w, preferred_element_type=F32)
        sig = jax.nn.sigmoid(pre)
        act_ref[b * TILE:b * TILE + n, :] = (pre * sig).astype(BF16)
        cot = cot_ref[b * TILE:b * TILE + n, :].astype(F32)
        slope = (cot * sig * (1.0 + pre * (1.0 - sig))).astype(BF16)
        sw_ref[b * TILE:b * TILE + n, :] = lax.dot_general(
            slope, w, (((1,), (1,)), ((), ())), preferred_element_type=F32
        ).astype(BF16)
        part = lax.dot_general(agg, slope, (((0,), (0,)), ((), ())), preferred_element_type=F32)
        if b == 0:
            wg[...] = part
        else:
            wg[...] += part
    rows = keep_ref.shape[0]
    core = core_ref[0]
    keep_ref[...] = wg[pl.ds(pl.multiple_of(core * rows, rows), rows), :]
    send_ref[...] = wg[pl.ds(pl.multiple_of((1 - core) * rows, rows), rows), :]


def forward(lst, offs, tiles, xs, phases, masks, acc=None, tail=None):
    hid = xs[0].shape[1]
    first = acc is None
    final = tail is not None
    blocks_dev = 8 if acc is None else acc.shape[0]
    if tail is not None:
        blocks_dev = tail[1].shape[0] // TILE
    args = [lst, offs, tiles, *xs] + ([] if first else [acc])
    specs = [SMEM, SMEM] + [VMEM] * (len(args) - 2)
    scratch = [pltpu.VMEM((blocks_dev + 1, TILE, hid), F32)]
    if final:
        args += list(tail)
        specs += [VMEM, VMEM, SMEM]
        nodes = blocks_dev * TILE
        out = (
            jax.ShapeDtypeStruct((nodes, hid), BF16),
            jax.ShapeDtypeStruct((nodes, hid), BF16),
            jax.ShapeDtypeStruct((hid // 2, hid), F32),
            jax.ShapeDtypeStruct((hid // 2, hid), F32),
        )
        out_specs = (VMEM,) * 4
        scratch.append(pltpu.VMEM((hid, hid), F32))
    else:
        out = jax.ShapeDtypeStruct((blocks_dev, TILE, hid), F32)
        out_specs = VMEM

    def body(*refs):
        forward_body(phases, masks, final, blocks_dev, first, refs)

    return pl.pallas_call(
        body,
        out_shape=out,
        in_specs=specs,
        out_specs=out_specs,
        scratch_shapes=scratch,
        compiler_params=params(24),
    )(*args)


def backward(lst, offs, tiles, sw, cats, half, extra=None, dtype=BF16):
    nodes, hid = sw.shape
    row_mask = nodes // TILE - 1
    args = [lst, offs, tiles, sw] + ([] if extra is None else [extra])
    specs = [SMEM, SMEM] + [VMEM] * (len(args) - 2)
    span = half * TILE

    def body(*refs):
        list_ref, offs_ref, tiles_ref, sw_ref = refs[:4]
        extra_ref = None if extra is None else refs[4]
        out_ref, acc = refs[-2:]
        for i, k in enumerate(cats):
            if extra_ref is None:
                acc[...] = jnp.zeros_like(acc)
            else:
                acc[0:half] = (
                    extra_ref[i * span:(i + 1) * span, :].astype(F32).reshape(half, TILE, hid)
                )
            backward_groups(
                list_ref, offs_ref[k], offs_ref[k + 1], tiles_ref, sw_ref, acc, row_mask, True
            )
            out_ref[i * span:(i + 1) * span, :] = acc[0:half].reshape(span, hid).astype(dtype)

    return pl.pallas_call(
        body,
        out_shape=jax.ShapeDtypeStruct((len(cats) * span, hid), dtype),
        in_specs=specs,
        out_specs=VMEM,
        scratch_shapes=[pltpu.VMEM((half + 1, TILE, hid), F32)],
        compiler_params=params(40 if half > 8 else 24),
    )(*args)


def prepare(tile_counts, tile_rows, tile_cols, me, group_blocks, cats, blocks_dev):
    slots = tile_rows.shape[0]
    length = (slots + cats * UNROLL + 31) // 32 * 32
    info = jnp.stack([me, jnp.int32(group_blocks)]).astype(jnp.int32)
    return pl.pallas_call(
        functools.partial(prep_body, cats, blocks_dev),
        out_shape=(
            jax.ShapeDtypeStruct((length,), jnp.int32),
            jax.ShapeDtypeStruct((cats + 1,), jnp.int32),
        ),
        in_specs=[SMEM] * 4,
        out_specs=(SMEM, SMEM),
        scratch_shapes=[pltpu.SMEM((cats,), jnp.int32)],
    )(tile_counts, tile_rows, tile_cols, info)


def local_four(row_size, features, weight, cotangent, tiles, tile_rows, tile_cols, tile_counts):
    nodes, hid = features.shape
    blocks_dev = nodes // TILE
    half = blocks_dev // 2
    cut = half * TILE
    me = lax.axis_index("grp").astype(jnp.int32)
    core = lax.bitwise_and(me, 1)

    def swap(x, bit):
        return lax.ppermute(x, "grp", [(i, i ^ bit) for i in range(4)])

    ya = swap(features[:cut], 2)
    yb = swap(features[cut:], 2)
    sib = swap(features, 1)
    lst, offs = prepare(tile_counts, tile_rows, tile_cols, me, 4 * blocks_dev, 8, blocks_dev)
    acc = forward(lst, offs, tiles, [features, sib], [(0, 2), (2, 4)], [7, 7])
    za = swap(ya, 1)
    zb = swap(yb, 1)
    acc = forward(lst, offs, tiles, [ya, za], [(4, 5), (6, 7)], [3, 3], acc)
    activated, sw, keep, send = forward(
        lst, offs, tiles, [yb, zb], [(5, 6), (7, 8)], [3, 3], acc,
        (weight, cotangent, core.reshape(1)),
    )
    p3 = backward(lst, offs, tiles, sw, (6, 7), half)
    r3 = swap(p3, 1)
    p1 = backward(lst, offs, tiles, sw, (2, 3), half)
    q = backward(lst, offs, tiles, sw, (4, 5), half, r3)
    qr = swap(q, 2)
    r1 = swap(p1, 1)
    p0 = backward(lst, offs, tiles, sw, (0, 1), half, r1, F32)
    feature_grad = (p0 + qr.astype(F32)).astype(BF16)

    w = keep + swap(send, 1)

    def fold(w, axis, size, bit):
        mine = w.astype(BF16)
        other = lax.ppermute(mine, axis, [(i, i ^ bit) for i in range(size)])
        return mine.astype(F32) + other.astype(F32)

    bit = 1
    while bit < row_size:
        w = fold(w, "row", row_size, bit)
        bit *= 2
    w = fold(w, "grp", 4, 2)
    other = swap(w, 1)
    weight_grad = jnp.where(
        core == 0, jnp.concatenate([w, other]), jnp.concatenate([other, w])
    )
    return activated, feature_grad, weight_grad


def local_any(features, weight, cotangent, tiles, tile_rows, tile_cols, tile_counts):
    nodes, hid = features.shape
    blocks_dev = nodes // TILE
    members = lax.axis_size("grp")
    group_blocks = blocks_dev * members
    me = lax.axis_index("grp").astype(jnp.int32)
    panel = lax.all_gather(features, "grp", axis=0, tiled=True)
    lst, offs = prepare(tile_counts, tile_rows, tile_cols, me, group_blocks, 1, blocks_dev)
    activated, sw, keep, send = forward(
        lst, offs, tiles, [panel], [(0, 1)], [127], None,
        (weight, cotangent, jnp.zeros((1,), jnp.int32)),
    )
    partial = backward(lst, offs, tiles, sw, (0,), group_blocks)
    feature_grad = lax.psum_scatter(partial, "grp", scatter_dimension=0, tiled=True)
    weight_grad = lax.psum(jnp.concatenate([keep, send]), ("row", "grp"))
    return activated, feature_grad, weight_grad


def solution(mesh):
    rows, members = mesh.shape["row"], mesh.shape["grp"]
    split = P(("row", "grp"))
    if members == 4 and rows & (rows - 1) == 0:
        local = functools.partial(local_four, rows)
    else:
        local = local_any
    return jax.shard_map(
        local,
        mesh=mesh,
        in_specs=(split, P(), split, split, split, split, split),
        out_specs=(split, split, P()),
        check_vma=False,
    )
```

time: 294 us -> 71.8 us (0.24)
  waiting for transfers between devices: 203 us -> 29.3 us
  other arithmetic: 37.3 us -> 3.4 us
  matrix products: 17.3 us -> 0 us
  starting transfers between devices: 0.12 us -> 16.3 us
  Pallas kernels: 0 us -> 15.8 us
  local copies, waits for them, and re-layouts: 20.6 us -> 4.99 us
  between operations: 14.4 us -> 1.5 us
    psum x1 -> x0, waiting for transfers between devices: 128 us -> none  [local(): weight_grad = lax.psum(weight_part, ('row', 'grp'))]
    reduce_scatter x1 -> x0, waiting for transfers between devices: 50.3 us -> none  [local(): lax.psum_scatter(partial_rows.astype(jnp.float32).astype(jnp.bfloat16), '...]
    ppermute x0 -> x14, waiting for transfers between devices: none -> 29.3 us  [the longest x10 24.3 us: swap(): return lax.ppermute(x, 'grp', [(i, i ^ bit) for i in range(4)])]
    scatter-add x6 -> x0, other arithmetic: 26.5 us -> none  [the longest x3 13.4 us: backward_block(): return partial_sum.at[col_index].add(contrib * live_mask[:, None, None])]
    all_gather x1 -> x0, waiting for transfers between devices: 24.7 us -> none  [local(): lax.all_gather(projected, 'grp', axis=0, tiled=True)]
    dot_general x9 -> x0, matrix products: 17.3 us -> none  [the longest x3 5.64 us: backward_block(): jnp.einsum('tki,tkj->tij', tile_vals, slope[row_index], preferred_element...]
    ppermute x0 -> x14, starting transfers between devices: none -> 16.3 us  [the longest x4 8.9 us: fold(): other = lax.ppermute(mine, axis, [(i, i ^ bit) for i in range(size)])]
    pallas_call x0 -> x8, Pallas kernels: none -> 15.8 us  [the longest x4 7 us: backward(): pl.pallas_call(body, out_shape=jax.ShapeDtypeStruct((len(cats) * span, hi...]
  transfers between devices with their start and end apart: 3 -> 14, of which waited for: 3 -> 7; matrix products, arithmetic and copies ran while one was open for 1% -> 3% of each run, Pallas kernels for 0% -> 18%
where the time goes in v1:
time: 71.8 us; the launch traced here: 71.3 us
  waiting for transfers between devices  29.3 us (41%)
  starting transfers between devices  16.3 us (23%)
  Pallas kernels  15.8 us (22%)
  local copies, waits for them, and re-layouts  4.99 us (7%)
  other arithmetic  3.4 us (5%)
  between operations  1.5 us (2%)
    ppermute x10, waiting for transfers between devices, swap(): return lax.ppermute(x, 'grp', [(i, i ^ bit) for i in range(4)])  24.3 us
    ppermute x4, starting transfers between devices, fold(): other = lax.ppermute(mine, axis, [(i, i ^ bit) for i in range(size)])  8.9 us
    ppermute x10, starting transfers between devices, swap(): return lax.ppermute(x, 'grp', [(i, i ^ bit) for i in range(4)])  7.45 us
    pallas_call x4, Pallas kernels, backward(): pl.pallas_call(body, out_shape=jax.ShapeDtypeStruct((len(cats) * span, hi...  7 us
    pallas_call x3, Pallas kernels, forward(): pl.pallas_call(body, out_shape=out, in_specs=specs, out_specs=out_specs,...  5.92 us
    ppermute x4, waiting for transfers between devices, fold(): other = lax.ppermute(mine, axis, [(i, i ^ bit) for i in range(size)])  5.03 us
    unnamed x18, local copies, waits for them, and re-layouts  3.92 us
    pallas_call x1, Pallas kernels, prepare(): pl.pallas_call(functools.partial(prep_body, cats, blocks_dev), out_shape=...  2.84 us
  transfers between devices with their start and end apart: 14, of which 7 were waited for; matrix products, arithmetic and copies ran while one was open for 3% of the time, Pallas kernels for 18%

profile of v1, /device:TPU:0, one launch (start us, length us, event | category | flops | bytes accessed | tf_op | source)
XLA Modules:
  0.0 71.3 jit_solution(18083203693690130795)
XLA Ops:
  0.6 0.5 collective-permute-start.4
  1.1 1.1 %fusion = (bf16[512,256]{1,0:T(8,128)(2,1)S(1)}, bf16[512,256]{1,0:T(8,128)(2,1)S(1)}) fusion(bf16[1024,256]{1,0:T(8,128)(2,1)} %refs_3_.1), kind=kLoop, calls=%fused_computation.8 | loop fusion | bytes 1048576 | tf_op jit(solution)/shard_map/slice | solution.py:282
  2.2 2.6 %collective-permute-start.2 = (bf16[512,256]{1,0:T(8,128)(2,1)S(1)}, bf16[512,256]{1,0:T(8,128)(2,1)S(1)}, u32[]{:S(2)}, u32[]{:S(2)}) collective-permute-start(bf16[512,256]{1,0:T(8,128)(2,1)S(1)} %get-tuple-element.15), channel_id=1, source_target_pairs={{0,2},{1,3},{2,0},{3,1},{4,6},{5,7},{6,4},{7,5},{8,10},{9,11},{10,... | collective-permute-start | bytes 786440 | tf_op jit(solution)/shard_map/ppermute | solution.py:280
  4.8 0.1 collective-permute-start
  4.9 7.1 %collective-permute-done.2.refs_3_ = bf16[512,256]{1,0:T(8,128)(2,1)S(1)} collective-permute-done((bf16[512,256]{1,0:T(8,128)(2,1)S(1)}, bf16[512,256]{1,0:T(8,128)(2,1)S(1)}, u32[]{:S(2)}, u32[]{:S(2)}) %collective-permute-start.2) | collective-permute-done | bytes 262176 | tf_op jit(solution)/shard_map/ppermute | solution.py:280
  12.0 0.0 collective-permute-start.3
  12.0 5.4 %collective-permute-done.refs_3_ = bf16[512,256]{1,0:T(8,128)(2,1)S(1)} collective-permute-done((bf16[512,256]{1,0:T(8,128)(2,1)S(1)}, bf16[512,256]{1,0:T(8,128)(2,1)S(1)}, u32[]{:S(2)}, u32[]{:S(2)}) %collective-permute-start) | collective-permute-done | bytes 262176 | tf_op jit(solution)/shard_map/ppermute | solution.py:280
  17.4 0.0 collective-permute-start.1
  18.0 0.6 pad_add_fusion.me_ref
  18.6 2.8 %shard_map.94 = (s32[96]{0:T(128)}, s32[9]{0:T(128)}) custom-call(s32[1]{0:T(128)S(6)} %copy.10.cnt_ref, s32[64]{0:T(128)} %rows_ref.1, s32[64]{0:T(128)} %cols_ref.1, s32[2]{0:T(128)} %pad_add_fusion.me_ref), custom_call_target="tpu_custom_call" | custom-call | tf_op jit(solution)/shard_map/pallas_call | solution.py:259
  21.5 0.0 collective-permute-done.4.refs_4_
  21.5 0.0 copy-start
  21.5 1.6 %copy-done = bf16[64,128,128]{2,1,0:T(8,128)(2,1)S(1)} copy-done((bf16[64,128,128]{2,1,0:T(8,128)(2,1)S(1)}, bf16[64,128,128]{2,1,0:T(8,128)(2,1)}, u32[]{:S(2)}) %copy-start) | copy-done | bytes 2097176
  23.1 0.0 copy-start.2
  23.1 1.0 %copy-done.2 = bf16[1024,256]{1,0:T(8,128)(2,1)S(1)} copy-done((bf16[1024,256]{1,0:T(8,128)(2,1)S(1)}, bf16[1024,256]{1,0:T(8,128)(2,1)}, u32[]{:S(2)}) %copy-start.2) | copy-done | bytes 524312
  24.1 0.0 copy-start.5
  24.1 0.7 copy-done.5
  24.8 0.0 copy-start.7
  24.8 0.6 copy-done.7
  25.4 1.9 %shard_map.95.refs_5_ = f32[8,128,256]{2,1,0:T(8,128)S(1)} custom-call(s32[96]{0:T(128)S(1)} %copy-done.5, s32[9]{0:T(128)S(1)} %copy-done.7, bf16[64,128,128]{2,1,0:T(8,128)(2,1)S(1)} %copy-done, bf16[1024,256]{1,0:T(8,128)(2,1)S(1)} %copy-done.2, bf16[1024,256]{1,0:T(8,128)(2,1)S(1)} %collective-permute-done.4.refs_4_), custom_call_target="tpu_custom_call" | custom-call | tf_op jit(solution)/shard_map/pallas_call | solution.py:212
  27.3 0.0 copy-start.3
  27.3 0.0 copy-start.4
  27.3 0.0 collective-permute-done.3.refs_4_
  27.3 1.2 %shard_map.96.refs_5_ = f32[8,128,256]{2,1,0:T(8,128)S(1)} custom-call(s32[96]{0:T(128)S(1)} %copy-done.5, s32[9]{0:T(128)S(1)} %copy-done.7, bf16[64,128,128]{2,1,0:T(8,128)(2,1)S(1)} %copy-done, bf16[512,256]{1,0:T(8,128)(2,1)S(1)} %collective-permute-done.2.refs_3_, bf16[512,256]{1,0:T(8,128)(2,1)S(1)} %collective-permute-done.3.refs_4_, ...), custom_call_target="tpu_custom_call" | custom-call | tf_op jit(solution)/shard_map/pallas_call | solution.py:212
  28.5 0.0 collective-permute-done.1.refs_4_
  28.5 0.0 copy-done.3
  28.5 0.0 copy-done.4
  28.5 2.9 %shard_map.97 = (bf16[1024,256]{1,0:T(8,128)(2,1)}, bf16[1024,256]{1,0:T(8,128)(2,1)S(1)}, f32[128,256]{1,0:T(8,128)S(1)}, f32[128,256]{1,0:T(8,128)S(1)}) custom-call(s32[96]{0:T(128)S(1)} %copy-done.5, s32[9]{0:T(128)S(1)} %copy-done.7, bf16[64,128,128]{2,1,0:T(8,128)(2,1)S(1)} %copy-done, bf16[512,256]{1,0:T(8,128)(2,1)S(1)} %collective-permute-done.refs_3_, ...), custom_call_target="tpu_custom_call" | custom-call | tf_op jit(solution)/shard_map/pallas_call | solution.py:212
  31.4 2.7 %collective-permute-start.8 = (f32[128,256]{1,0:T(8,128)S(1)}, f32[128,256]{1,0:T(8,128)S(1)}, u32[]{:S(2)}, u32[]{:S(2)}) collective-permute-start(f32[128,256]{1,0:T(8,128)S(1)} %get-tuple-element.14), channel_id=1, source_target_pairs={{0,1},{1,0},{2,3},{3,2},{4,5},{5,4},{6,7},{7,6},{8,9},{9,8},{10,11... | collective-permute-start | bytes 393224 | tf_op jit(solution)/shard_map/ppermute | solution.py:280
  34.1 1.0 %collective-permute-done.8 = f32[128,256]{1,0:T(8,128)S(1)} collective-permute-done((f32[128,256]{1,0:T(8,128)S(1)}, f32[128,256]{1,0:T(8,128)S(1)}, u32[]{:S(2)}, u32[]{:S(2)}) %collective-permute-start.8) | collective-permute-done | bytes 131104 | tf_op jit(solution)/shard_map/ppermute | solution.py:280
  35.1 0.1 collective-permute-start.9
  35.2 4.3 %collective-permute-done.9 = bf16[128,256]{1,0:T(8,128)(2,1)S(1)} collective-permute-done((bf16[128,256]{1,0:T(8,128)(2,1)S(1)}, bf16[128,256]{1,0:T(8,128)(2,1)S(1)}, u32[]{:S(2)}, u32[]{:S(2)}) %collective-permute-start.9) | collective-permute-done | bytes 65568 | tf_op jit(solution)/shard_map/ppermute | solution.py:307
  39.6 2.5 %collective-permute-start.10 = (bf16[128,256]{1,0:T(8,128)(2,1)S(1)}, bf16[128,256]{1,0:T(8,128)(2,1)S(1)}, u32[]{:S(2)}, u32[]{:S(2)}) collective-permute-start(bf16[128,256]{1,0:T(8,128)(2,1)S(1)} %add_convert_fusion.3), channel_id=1, source_target_pairs={{0,8},{4,12},{8,0},{12,4},{16,24},{20,28},{24,16},{28,20},{1,9},{5... | collective-permute-start | bytes 196616 | tf_op jit(solution)/shard_map/ppermute | solution.py:307
  42.0 1.5 %shard_map.100 = bf16[1024,256]{1,0:T(8,128)(2,1)S(1)} custom-call(s32[96]{0:T(128)S(1)} %copy-done.5, s32[9]{0:T(128)S(1)} %copy-done.7, bf16[64,128,128]{2,1,0:T(8,128)(2,1)S(1)} %copy-done, bf16[1024,256]{1,0:T(8,128)(2,1)S(1)} %get-tuple-element.12.refs_3_), custom_call_target="tpu_custom_call" | custom-call | tf_op jit(solution)/shard_map/pallas_call | solution.py:245
  43.5 0.1 collective-permute-start.6
  43.6 0.7 collective-permute-done.10
  44.3 3.8 %collective-permute-start.11 = (bf16[128,256]{1,0:T(8,128)(2,1)S(1)}, bf16[128,256]{1,0:T(8,128)(2,1)S(1)}, u32[]{:S(2)}, u32[]{:S(2)}) collective-permute-start(bf16[128,256]{1,0:T(8,128)(2,1)S(1)} %add_convert_fusion.2), channel_id=1, source_target_pairs={{0,16},{4,20},{8,24},{12,28},{16,0},{20,4},{24,8},{28,12},{1,17},{... | collective-permute-start | bytes 196616 | tf_op jit(solution)/shard_map/ppermute | solution.py:307
  48.1 2.3 %shard_map.98 = bf16[1024,256]{1,0:T(8,128)(2,1)} custom-call(s32[96]{0:T(128)S(1)} %copy-done.5, s32[9]{0:T(128)S(1)} %copy-done.7, bf16[64,128,128]{2,1,0:T(8,128)(2,1)S(1)} %copy-done, bf16[1024,256]{1,0:T(8,128)(2,1)S(1)} %get-tuple-element.12.refs_3_), custom_call_target="tpu_custom_call" | custom-call | tf_op jit(solution)/shard_map/pallas_call | solution.py:245
  50.4 0.0 copy-start.1
  50.4 0.0 copy-start.6
  50.4 0.0 copy-start.8
  50.4 0.0 collective-permute-start.5
  50.4 0.0 collective-permute-done.11
  50.4 2.6 %collective-permute-start.12 = (bf16[128,256]{1,0:T(8,128)(2,1)S(1)}, bf16[128,256]{1,0:T(8,128)(2,1)S(1)}, u32[]{:S(2)}, u32[]{:S(2)}) collective-permute-start(bf16[128,256]{1,0:T(8,128)(2,1)S(1)} %add_convert_fusion.1), channel_id=1, source_target_pairs={{0,2},{1,3},{2,0},{3,1},{4,6},{5,7},{6,4},{7,5},{8,10},{9,11},{10,... | collective-permute-start | bytes 196616 | tf_op jit(solution)/shard_map/ppermute | solution.py:307
  53.0 0.0 collective-permute-done.6.refs_4_
  53.0 2.0 %shard_map.101 = bf16[1024,256]{1,0:T(8,128)(2,1)} custom-call(s32[96]{0:T(128)S(1)} %copy-done.5, s32[9]{0:T(128)S(1)} %copy-done.7, bf16[64,128,128]{2,1,0:T(8,128)(2,1)S(1)} %copy-done, bf16[1024,256]{1,0:T(8,128)(2,1)S(1)} %get-tuple-element.12.refs_3_, bf16[1024,256]{1,0:T(8,128)(2,1)S(1)} %collective-permute-done.6.refs_4_), custom_call_target="tpu_custom_call" | custom-call | tf_op jit(solution)/shard_map/pallas_call | solution.py:245
  55.0 1.4 %collective-permute-start.7 = (bf16[1024,256]{1,0:T(8,128)(2,1)}, bf16[1024,256]{1,0:T(8,128)(2,1)}, u32[]{:S(2)}, u32[]{:S(2)}) collective-permute-start(bf16[1024,256]{1,0:T(8,128)(2,1)} %shard_map.101), channel_id=1, source_target_pairs={{0,2},{1,3},{2,0},{3,1},{4,6},{5,7},{6,4},{7,5},{8,10},{9,11},{10,... | collective-permute-start | bytes 1572872 | tf_op jit(solution)/shard_map/ppermute | solution.py:280
  56.4 0.0 collective-permute-done.12
  56.4 0.1 collective-permute-start.13
  56.5 0.0 collective-permute-done.5.refs_4_
  56.5 0.0 copy-done.1
  56.5 0.0 copy-done.6
  56.5 0.0 copy-done.8
  56.6 1.2 %shard_map.99 = f32[1024,256]{1,0:T(8,128)S(1)} custom-call(s32[96]{0:T(128)S(1)} %copy-done.6, s32[9]{0:T(128)S(1)} %copy-done.8, bf16[64,128,128]{2,1,0:T(8,128)(2,1)S(1)} %copy-done.1, bf16[1024,256]{1,0:T(8,128)(2,1)S(1)} %get-tuple-element.12.refs_3_, bf16[1024,256]{1,0:T(8,128)(2,1)S(1)} %collective-permute-done.5.refs_4_), custom_call_target="tpu_custom_call" | custom-call | tf_op jit(solution)/shard_map/pallas_call | solution.py:245
  57.8 0.1 collective-permute-done.13
  57.8 0.7 %maximum_select_fusion = f32[256,256]{1,0:T(8,128)} fusion(f32[128,256]{1,0:T(8,128)S(1)} %collective-permute-done.13, f32[128,256]{1,0:T(8,128)S(1)} %convert_add_fusion, pred[]{:T(512)S(6)} %eq.3), kind=kLoop, calls=%fused_computation.1 | loop fusion | flops 196608 | bytes 524289 | tf_op jit(solution)/shard_map/jit(_where)/select_n | solution.py:316
  58.6 10.7 %collective-permute-done.7 = bf16[1024,256]{1,0:T(8,128)(2,1)} collective-permute-done((bf16[1024,256]{1,0:T(8,128)(2,1)}, bf16[1024,256]{1,0:T(8,128)(2,1)}, u32[]{:S(2)}, u32[]{:S(2)}) %collective-permute-start.7) | collective-permute-done | bytes 524320 | tf_op jit(solution)/shard_map/ppermute | solution.py:280
  69.3 2.0 %add_convert_fusion = bf16[1024,256]{1,0:T(8,128)(2,1)} fusion(f32[1024,256]{1,0:T(8,128)S(1)} %shard_map.99, bf16[1024,256]{1,0:T(8,128)(2,1)} %collective-permute-done.7), kind=kLoop, calls=%fused_computation | loop fusion | flops 786432 | bytes 2097152 | tf_op jit(solution)/shard_map/convert_element_type | solution.py:301
  (5 shorter events, 0.1 us)
Async XLA Ops:
  0.6 20.9 %collective-permute-start.4 = (bf16[1024,256]{1,0:T(8,128)(2,1)}, bf16[1024,256]{1,0:T(8,128)(2,1)S(1)}, u32[]{:S(2)}, u32[]{:S(2)}) collective-permute-start(bf16[1024,256]{1,0:T(8,128)(2,1)} %refs_3_.1), channel_id=1, source_target_pairs={{0,1},{1,0},{2,3},{3,2},{4,5},{5,4},{6,7},{7,6},{8,9},{9,8},{10,11... | collective-permute-start | bytes 1572872 | tf_op jit(solution)/shard_map/ppermute | solution.py:280
  2.2 9.8 %collective-permute-start.2 = (bf16[512,256]{1,0:T(8,128)(2,1)S(1)}, bf16[512,256]{1,0:T(8,128)(2,1)S(1)}, u32[]{:S(2)}, u32[]{:S(2)}) collective-permute-start(bf16[512,256]{1,0:T(8,128)(2,1)S(1)} %get-tuple-element.15), channel_id=1, source_target_pairs={{0,2},{1,3},{2,0},{3,1},{4,6},{5,7},{6,4},{7,5},{8,10},{9,11},{10,... | collective-permute-start | bytes 786440 | tf_op jit(solution)/shard_map/ppermute | solution.py:280
  4.8 12.6 %collective-permute-start = (bf16[512,256]{1,0:T(8,128)(2,1)S(1)}, bf16[512,256]{1,0:T(8,128)(2,1)S(1)}, u32[]{:S(2)}, u32[]{:S(2)}) collective-permute-start(bf16[512,256]{1,0:T(8,128)(2,1)S(1)} %get-tuple-element.16), channel_id=1, source_target_pairs={{0,2},{1,3},{2,0},{3,1},{4,6},{5,7},{6,4},{7,5},{8,10},{9,11},{10,... | collective-permute-start | bytes 786440 | tf_op jit(solution)/shard_map/ppermute | solution.py:280
  12.0 15.3 %collective-permute-start.3 = (bf16[512,256]{1,0:T(8,128)(2,1)S(1)}, bf16[512,256]{1,0:T(8,128)(2,1)S(1)}, u32[]{:S(2)}, u32[]{:S(2)}) collective-permute-start(bf16[512,256]{1,0:T(8,128)(2,1)S(1)} %collective-permute-done.2.refs_3_), channel_id=1, source_target_pairs={{0,1},{1,0},{2,3},{3,2},{4,5},{5,4},{6,7},{7,6},{8,9},{9,8},{10,11... | collective-permute-start | bytes 786440 | tf_op jit(solution)/shard_map/ppermute | solution.py:280
  17.4 11.1 %collective-permute-start.1 = (bf16[512,256]{1,0:T(8,128)(2,1)S(1)}, bf16[512,256]{1,0:T(8,128)(2,1)S(1)}, u32[]{:S(2)}, u32[]{:S(2)}) collective-permute-start(bf16[512,256]{1,0:T(8,128)(2,1)S(1)} %collective-permute-done.refs_3_), channel_id=1, source_target_pairs={{0,1},{1,0},{2,3},{3,2},{4,5},{5,4},{6,7},{7,6},{8,9},{9,8},{10,11... | collective-permute-start | bytes 786440 | tf_op jit(solution)/shard_map/ppermute | solution.py:280
  21.5 1.6 %copy-start = (bf16[64,128,128]{2,1,0:T(8,128)(2,1)S(1)}, bf16[64,128,128]{2,1,0:T(8,128)(2,1)}, u32[]{:S(2)}) copy-start(bf16[64,128,128]{2,1,0:T(8,128)(2,1)} %refs_2_.13) | copy-start | bytes 6291460
  23.1 1.0 %copy-start.2 = (bf16[1024,256]{1,0:T(8,128)(2,1)S(1)}, bf16[1024,256]{1,0:T(8,128)(2,1)}, u32[]{:S(2)}) copy-start(bf16[1024,256]{1,0:T(8,128)(2,1)} %refs_3_.1) | copy-start | bytes 1572868
  24.1 0.7 copy-start.5
  24.8 0.6 copy-start.7
  27.3 1.2 %copy-start.3 = (bf16[1024,256]{1,0:T(8,128)(2,1)S(1)}, bf16[1024,256]{1,0:T(8,128)(2,1)}, u32[]{:S(2)}) copy-start(bf16[1024,256]{1,0:T(8,128)(2,1)} %refs_7_.1) | copy-start | bytes 1572868
  27.3 1.2 %copy-start.4 = (bf16[256,256]{1,0:T(8,128)(2,1)S(1)}, bf16[256,256]{1,0:T(8,128)(2,1)}, u32[]{:S(2)}) copy-start(bf16[256,256]{1,0:T(8,128)(2,1)} %refs_6_.1) | copy-start | bytes 393220
  31.4 3.7 %collective-permute-start.8 = (f32[128,256]{1,0:T(8,128)S(1)}, f32[128,256]{1,0:T(8,128)S(1)}, u32[]{:S(2)}, u32[]{:S(2)}) collective-permute-start(f32[128,256]{1,0:T(8,128)S(1)} %get-tuple-element.14), channel_id=1, source_target_pairs={{0,1},{1,0},{2,3},{3,2},{4,5},{5,4},{6,7},{7,6},{8,9},{9,8},{10,11... | collective-permute-start | bytes 393224 | tf_op jit(solution)/shard_map/ppermute | solution.py:280
  35.1 4.4 %collective-permute-start.9 = (bf16[128,256]{1,0:T(8,128)(2,1)S(1)}, bf16[128,256]{1,0:T(8,128)(2,1)S(1)}, u32[]{:S(2)}, u32[]{:S(2)}) collective-permute-start(bf16[128,256]{1,0:T(8,128)(2,1)S(1)} %add_convert_fusion.4), channel_id=1, source_target_pairs={{0,4},{4,0},{8,12},{12,8},{16,20},{20,16},{24,28},{28,24},{1,5},{5... | collective-permute-start | bytes 196616 | tf_op jit(solution)/shard_map/ppermute | solution.py:307
  39.6 4.7 %collective-permute-start.10 = (bf16[128,256]{1,0:T(8,128)(2,1)S(1)}, bf16[128,256]{1,0:T(8,128)(2,1)S(1)}, u32[]{:S(2)}, u32[]{:S(2)}) collective-permute-start(bf16[128,256]{1,0:T(8,128)(2,1)S(1)} %add_convert_fusion.3), channel_id=1, source_target_pairs={{0,8},{4,12},{8,0},{12,4},{16,24},{20,28},{24,16},{28,20},{1,9},{5... | collective-permute-start | bytes 196616 | tf_op jit(solution)/shard_map/ppermute | solution.py:307
  43.5 9.5 %collective-permute-start.6 = (bf16[1024,256]{1,0:T(8,128)(2,1)S(1)}, bf16[1024,256]{1,0:T(8,128)(2,1)S(1)}, u32[]{:S(2)}, u32[]{:S(2)}) collective-permute-start(bf16[1024,256]{1,0:T(8,128)(2,1)S(1)} %shard_map.100), channel_id=1, source_target_pairs={{0,1},{1,0},{2,3},{3,2},{4,5},{5,4},{6,7},{7,6},{8,9},{9,8},{10,11... | collective-permute-start | bytes 1572872 | tf_op jit(solution)/shard_map/ppermute | solution.py:280
  44.3 6.1 %collective-permute-start.11 = (bf16[128,256]{1,0:T(8,128)(2,1)S(1)}, bf16[128,256]{1,0:T(8,128)(2,1)S(1)}, u32[]{:S(2)}, u32[]{:S(2)}) collective-permute-start(bf16[128,256]{1,0:T(8,128)(2,1)S(1)} %add_convert_fusion.2), channel_id=1, source_target_pairs={{0,16},{4,20},{8,24},{12,28},{16,0},{20,4},{24,8},{28,12},{1,17},{... | collective-permute-start | bytes 196616 | tf_op jit(solution)/shard_map/ppermute | solution.py:307
  50.4 6.1 %copy-start.1 = (bf16[64,128,128]{2,1,0:T(8,128)(2,1)S(1)}, bf16[64,128,128]{2,1,0:T(8,128)(2,1)}, u32[]{:S(2)}) copy-start(bf16[64,128,128]{2,1,0:T(8,128)(2,1)} %refs_2_.13) | copy-start | bytes 6291460
  50.4 6.2 %copy-start.6 = (s32[96]{0:T(128)S(1)}, s32[96]{0:T(128)}, u32[]{:S(2)}) copy-start(s32[96]{0:T(128)} %get-tuple-element.9.refs_0_) | copy-start | bytes 1156
  50.4 6.2 %copy-start.8 = (s32[9]{0:T(128)S(1)}, s32[9]{0:T(128)}, u32[]{:S(2)}) copy-start(s32[9]{0:T(128)} %get-tuple-element.10.refs_1_) | copy-start | bytes 112
  50.4 6.1 %collective-permute-start.5 = (bf16[1024,256]{1,0:T(8,128)(2,1)}, bf16[1024,256]{1,0:T(8,128)(2,1)S(1)}, u32[]{:S(2)}, u32[]{:S(2)}) collective-permute-start(bf16[1024,256]{1,0:T(8,128)(2,1)} %shard_map.98), channel_id=1, source_target_pairs={{0,1},{1,0},{2,3},{3,2},{4,5},{5,4},{6,7},{7,6},{8,9},{9,8},{10,11... | collective-permute-start | bytes 1572872 | tf_op jit(solution)/shard_map/ppermute | solution.py:280
  50.4 6.0 %collective-permute-start.12 = (bf16[128,256]{1,0:T(8,128)(2,1)S(1)}, bf16[128,256]{1,0:T(8,128)(2,1)S(1)}, u32[]{:S(2)}, u32[]{:S(2)}) collective-permute-start(bf16[128,256]{1,0:T(8,128)(2,1)S(1)} %add_convert_fusion.1), channel_id=1, source_target_pairs={{0,2},{1,3},{2,0},{3,1},{4,6},{5,7},{6,4},{7,5},{8,10},{9,11},{10,... | collective-permute-start | bytes 196616 | tf_op jit(solution)/shard_map/ppermute | solution.py:307
  55.0 14.3 %collective-permute-start.7 = (bf16[1024,256]{1,0:T(8,128)(2,1)}, bf16[1024,256]{1,0:T(8,128)(2,1)}, u32[]{:S(2)}, u32[]{:S(2)}) collective-permute-start(bf16[1024,256]{1,0:T(8,128)(2,1)} %shard_map.101), channel_id=1, source_target_pairs={{0,2},{1,3},{2,0},{3,1},{4,6},{5,7},{6,4},{7,5},{8,10},{9,11},{10,... | collective-permute-start | bytes 1572872 | tf_op jit(solution)/shard_map/ppermute | solution.py:280
  56.4 1.4 %collective-permute-start.13 = (f32[128,256]{1,0:T(8,128)S(1)}, f32[128,256]{1,0:T(8,128)S(1)}, u32[]{:S(2)}, u32[]{:S(2)}) collective-permute-start(f32[128,256]{1,0:T(8,128)S(1)} %convert_add_fusion), channel_id=1, source_target_pairs={{0,1},{1,0},{2,3},{3,2},{4,5},{5,4},{6,7},{7,6},{8,9},{9,8},{10,11... | collective-permute-start | bytes 393224 | tf_op jit(solution)/shard_map/ppermute | solution.py:280

commit v2 on v1

v2 whole, which is shorter than its diff:
```python
import functools

import jax
import jax.numpy as jnp
from jax import lax
from jax.experimental import pallas as pl
from jax.experimental.pallas import tpu as pltpu
from jax.sharding import PartitionSpec as P

TILE = 128
UNROLL = 4
F32 = jnp.float32
BF16 = jnp.bfloat16

SMEM = pl.BlockSpec(memory_space=pltpu.SMEM)
VMEM = pl.BlockSpec(memory_space=pltpu.VMEM)


def params(mib):
    return pltpu.CompilerParams(vmem_limit_bytes=mib << 20)


class Plan:
    def __init__(self, slots, cats, blocks_dev):
        self.slots, self.cats, self.blocks_dev = slots, cats, blocks_dev
        self.length = slots + cats * (UNROLL - 1)
        self.length = (self.length + UNROLL - 1) // UNROLL * UNROLL

    def bounds(self, list_ref, lo, hi):
        return list_ref[self.length + lo], list_ref[self.length + hi]


def prep_body(plan, pad_col, me_ref, cnt_ref, rows_ref, cols_ref, list_ref):
    me = me_ref[0]
    cats, blocks_dev = plan.cats, plan.blocks_dev
    pad = (blocks_dev << 8) | (pad_col << 16)
    live = cnt_ref[0]

    def category(col):
        if cats == 1:
            return 0, col
        return lax.bitwise_xor(col // blocks_dev, me) * 8, lax.rem(col, blocks_dev)

    def count(s, total):
        return total + (1 << category(cols_ref[s])[0])

    total = lax.fori_loop(0, live, count, jnp.int32(0))
    group = jnp.int32(0)
    places = jnp.int32(0)
    for k in range(cats):
        n = (total >> (8 * k)) & 255
        list_ref[plan.length + k] = group
        places = places + ((group * UNROLL) << (8 * k))
        group = group + (n + UNROLL - 1) // UNROLL
        for u in range(1, UNROLL):
            list_ref[lax.max(group * UNROLL - u, 0)] = pad
    list_ref[plan.length + cats] = group

    def place(s, places):
        shift, local = category(cols_ref[s])
        list_ref[(places >> shift) & 255] = s | (rows_ref[s] << 8) | (local << 16)
        return places + (1 << shift)

    lax.fori_loop(0, live, place, places)


def prepare(plan, pad_col, me, info):
    return pl.pallas_call(
        functools.partial(prep_body, plan, pad_col),
        out_shape=jax.ShapeDtypeStruct((plan.length + plan.cats + 1,), jnp.int32),
        in_specs=[SMEM] * 4,
        out_specs=SMEM,
    )(me.reshape(1), *info)


def tile_of(e):
    return e & 255


def row_of(e):
    return (e >> 8) & 255


def col_of(e):
    return e >> 16


def rows_at(block):
    return pl.ds(pl.multiple_of(block * TILE, TILE), TILE)


def tie(x, *others):
    return lax.optimization_barrier((x, *others))[0]


def forward_groups(list_ref, bounds, tiles_ref, x_ref, acc):
    last = x_ref.shape[0] // TILE - 1

    def step(g, carry):
        es = [list_ref[g * UNROLL + u] for u in range(UNROLL)]
        ds = [
            jnp.dot(
                tiles_ref[tile_of(e)],
                x_ref[rows_at(lax.min(col_of(e), last)), :],
                preferred_element_type=F32,
            )
            for e in es
        ]
        for e, d in zip(es, ds):
            acc[row_of(e)] += d
        return carry

    lax.fori_loop(*bounds, step, 0)


def backward_groups(list_ref, bounds, tiles_ref, s_ref, acc):
    last = s_ref.shape[0] // TILE - 1

    def step(g, carry):
        es = [list_ref[g * UNROLL + u] for u in range(UNROLL)]
        ds = [
            lax.dot_general(
                tiles_ref[tile_of(e)],
                s_ref[rows_at(lax.min(row_of(e), last)), :],
                (((0,), (0,)), ((), ())),
                preferred_element_type=F32,
            )
            for e in es
        ]
        for e, d in zip(es, ds):
            acc[col_of(e)] += d
        return carry

    lax.fori_loop(*bounds, step, 0)


def forward_body(plan, phases, final, first, refs):
    refs = list(refs)
    list_ref, tiles_ref = refs[:2]
    xs = refs[2:2 + len(phases)]
    refs = refs[2 + len(phases):]
    blocks_dev = plan.blocks_dev
    if not first:
        acc_in = refs.pop(0)
    if final:
        w_ref, cot_ref, core_ref, act_ref, sw_ref, keep_ref, send_ref, acc, wg = refs
    else:
        acc_out, acc = refs
    if first:
        acc[...] = jnp.zeros_like(acc)
    else:
        acc[0:blocks_dev] = acc_in[...]
    for k, x_ref in zip(phases, xs):
        forward_groups(list_ref, plan.bounds(list_ref, k, k + 1), tiles_ref, x_ref, acc)
    if not final:
        acc_out[...] = acc[0:blocks_dev]
        return
    hid = w_ref.shape[0]
    w = w_ref[...]
    step_blocks = 4 if blocks_dev % 4 == 0 else 1
    n = step_blocks * TILE
    for b in range(0, blocks_dev, step_blocks):
        at = slice(b * TILE, b * TILE + n)
        agg = acc[b:b + step_blocks].reshape(n, hid).astype(BF16)
        pre = jnp.dot(agg, w, preferred_element_type=F32)
        sig = jax.nn.sigmoid(pre)
        act_ref[at, :] = (pre * sig).astype(BF16)
        slope = (cot_ref[at, :].astype(F32) * sig * (1.0 + pre * (1.0 - sig))).astype(BF16)
        sw_ref[at, :] = lax.dot_general(
            slope, w, (((1,), (1,)), ((), ())), preferred_element_type=F32
        ).astype(BF16)
        part = lax.dot_general(agg, slope, (((0,), (0,)), ((), ())), preferred_element_type=F32)
        if b == 0:
            wg[...] = part
        else:
            wg[...] += part
    rows = keep_ref.shape[0]
    core = core_ref[0]
    keep_ref[...] = wg[pl.ds(pl.multiple_of(core * rows, rows), rows), :]
    send_ref[...] = wg[pl.ds(pl.multiple_of((1 - core) * rows, rows), rows), :]


def forward(plan, lst, tiles, xs, phases, acc=None, tail=None):
    hid = xs[0].shape[1]
    blocks_dev = plan.blocks_dev
    first, final = acc is None, tail is not None
    args = [lst, tiles, *xs] + ([] if first else [acc])
    specs = [SMEM] + [VMEM] * (len(args) - 1)
    scratch = [pltpu.VMEM((blocks_dev + 1, TILE, hid), F32)]
    if final:
        args += list(tail)
        specs += [VMEM, VMEM, SMEM]
        out = (
            jax.ShapeDtypeStruct((blocks_dev * TILE, hid), BF16),
            jax.ShapeDtypeStruct((blocks_dev * TILE, hid), BF16),
            jax.ShapeDtypeStruct((hid // 2, hid), F32),
            jax.ShapeDtypeStruct((hid // 2, hid), F32),
        )
        out_specs = (VMEM,) * 4
        scratch.append(pltpu.VMEM((hid, hid), F32))
    else:
        out = jax.ShapeDtypeStruct((blocks_dev, TILE, hid), F32)
        out_specs = VMEM

    def body(*refs):
        forward_body(plan, phases, final, first, refs)

    return pl.pallas_call(
        body,
        out_shape=out,
        in_specs=specs,
        out_specs=out_specs,
        scratch_shapes=scratch,
        compiler_params=params(12),
    )(*args)


def backward(plan, sources, blocks, extra=None, dtype=BF16):
    hid = sources[0][3].shape[1]
    args = [part for source in sources for part in source[1:]]
    specs = [SMEM, VMEM, VMEM] * len(sources)
    if extra is not None:
        args.append(extra)
        specs.append(VMEM)

    def body(*refs):
        out_ref, acc = refs[-2:]
        if extra is None:
            acc[...] = jnp.zeros_like(acc)
        else:
            acc[0:blocks] = refs[-3][...].astype(F32).reshape(blocks, TILE, hid)
        for i, source in enumerate(sources):
            list_ref, tiles_ref, s_ref = refs[3 * i:3 * i + 3]
            bounds = plan.bounds(list_ref, source[0], source[0] + 1)
            backward_groups(list_ref, bounds, tiles_ref, s_ref, acc)
        out_ref[...] = acc[0:blocks].reshape(blocks * TILE, hid).astype(dtype)

    return pl.pallas_call(
        body,
        out_shape=jax.ShapeDtypeStruct((blocks * TILE, hid), dtype),
        in_specs=specs,
        out_specs=VMEM,
        scratch_shapes=[pltpu.VMEM((blocks + 1, TILE, hid), F32)],
        compiler_params=params(40 if blocks > 8 else 12),
    )(*args)


def local_four(features, weight, cotangent, tiles, tile_rows, tile_cols, tile_counts):
    blocks_dev = features.shape[0] // TILE
    me = lax.axis_index("grp").astype(jnp.int32)
    core = lax.bitwise_and(me, 1)

    def swap(x, bit):
        return lax.ppermute(x, "grp", [(i, i ^ bit) for i in range(4)])

    def fold(w, axis, size, bit, *others):
        other = lax.ppermute(w, axis, [(i, i ^ bit) for i in range(size)])
        if others:
            other = tie(other, *others)
        return (w.astype(F32) + other.astype(F32)).astype(BF16)

    far = swap(features, 2)
    sib = swap(features, 1)
    plan = Plan(tile_rows.shape[0], 4, blocks_dev)
    lst = prepare(plan, blocks_dev, me, [tile_counts, tile_rows, tile_cols])
    acc = forward(plan, lst, tiles, [features, sib], [0, 1])
    far = tie(far, acc)
    diag = swap(far, 1)
    acc = forward(plan, lst, tiles, [far], [2], acc)
    activated, sw, keep, send = forward(
        plan, lst, tiles, [diag], [3], acc, (weight, cotangent, core.reshape(1))
    )

    def part(rel, sw, extra=None, dtype=BF16):
        return backward(plan, [(rel, lst, tiles, sw)], blocks_dev, extra, dtype)

    send = swap(send, 1)
    p3 = part(3, sw)
    r3 = swap(p3, 1)
    w = (keep + tie(send, p3)).astype(BF16)
    q = part(2, tie(sw, w), None, F32)
    q = (q + r3.astype(F32)).astype(BF16)
    q_far = swap(q, 2)
    w = fold(w, "grp", 4, 2, q)
    p1 = part(1, tie(sw, w))
    r1 = swap(p1, 1)
    w = fold(w, "row", 8, 1, p1)
    p0 = part(0, tie(sw, w), r1, F32)
    w = fold(w, "row", 8, 2, p0)
    w = fold(w, "row", 8, 4, q_far)
    other = swap(w, 1)
    weight_grad = jnp.where(
        core == 0, jnp.concatenate([w, other]), jnp.concatenate([other, w])
    ).astype(F32)
    feature_grad = (p0 + q_far.astype(F32)).astype(BF16)
    return activated, feature_grad, weight_grad


def local_any(features, weight, cotangent, tiles, tile_rows, tile_cols, tile_counts):
    blocks_dev = features.shape[0] // TILE
    group_blocks = blocks_dev * lax.axis_size("grp")
    me = lax.axis_index("grp").astype(jnp.int32)
    panel = lax.all_gather(features, "grp", axis=0, tiled=True)
    info = [tile_counts, tile_rows, tile_cols]
    plan = Plan(tile_rows.shape[0], 1, blocks_dev)
    lst = prepare(plan, group_blocks, me, info)
    activated, sw, keep, send = forward(
        plan, lst, tiles, [panel], [0], None, (weight, cotangent, jnp.zeros((1,), jnp.int32))
    )
    partial = backward(plan, [(0, lst, tiles, sw)], group_blocks)
    feature_grad = lax.psum_scatter(partial, "grp", scatter_dimension=0, tiled=True)
    weight_grad = lax.psum(jnp.concatenate([keep, send]), ("row", "grp"))
    return activated, feature_grad, weight_grad


def solution(mesh):
    split = P(("row", "grp"))
    four = mesh.shape["grp"] == 4 and mesh.shape["row"] == 8
    return jax.shard_map(
        local_four if four else local_any,
        mesh=mesh,
        in_specs=(split, P(), split, split, split, split, split),
        out_specs=(split, split, P()),
        check_vma=False,
    )
```

time: 71.8 us -> 51.9 us (0.72)
  the two profiles are of different devices: /device:TPU:0 before, /device:TPU:9 now
where the time goes in v2:
time: 51.9 us; the launch traced here: 50.9 us
  starting transfers between devices  15.1 us (29%)
  waiting for transfers between devices  14.1 us (27%)
  Pallas kernels  11.3 us (22%)
  local copies, waits for them, and re-layouts  5.13 us (10%)
  other arithmetic  3.74 us (7%)
  between operations  1.42 us (3%)
    ppermute x8, waiting for transfers between devices, swap(): return lax.ppermute(x, 'grp', [(i, i ^ bit) for i in range(4)])  10.4 us
    ppermute x8, starting transfers between devices, swap(): return lax.ppermute(x, 'grp', [(i, i ^ bit) for i in range(4)])  10.2 us
    pallas_call x3, Pallas kernels, forward(): pl.pallas_call(body, out_shape=out, in_specs=specs, out_specs=out_specs,...  5.79 us
    unnamed x18, local copies, waits for them, and re-layouts  5.13 us
    ppermute x4, starting transfers between devices, fold(): other = lax.ppermute(w, axis, [(i, i ^ bit) for i in range(size)])  4.94 us
    pallas_call x4, Pallas kernels, backward(): pl.pallas_call(body, out_shape=jax.ShapeDtypeStruct((blocks * TILE, hid),...  4.05 us
    ppermute x4, waiting for transfers between devices, fold(): other = lax.ppermute(w, axis, [(i, i ^ bit) for i in range(size)])  3.73 us
    convert_element_type x1, other arithmetic, local_four(): feature_grad = (p0 + q_far.astype(F32)).astype(BF16)  1.95 us
  transfers between devices with their start and end apart: 12, of which 7 were waited for; matrix products, arithmetic and copies ran while one was open for 6% of the time, Pallas kernels for 13%

profile of v2, /device:TPU:9, one launch (start us, length us, event | category | flops | bytes accessed | tf_op | source)
XLA Modules:
  0.0 50.9 jit_solution(933300060215164307)
XLA Ops:
  0.6 0.7 %collective-permute-start.1 = (bf16[1024,256]{1,0:T(8,128)(2,1)}, bf16[1024,256]{1,0:T(8,128)(2,1)S(1)}, u32[]{:S(2)}, u32[]{:S(2)}) collective-permute-start(bf16[1024,256]{1,0:T(8,128)(2,1)} %refs_2_.1), channel_id=1, source_target_pairs={{0,1},{1,0},{2,3},{3,2},{4,5},{5,4},{6,7},{7,6},{8,9},{9,8},{10,11... | collective-permute-start | bytes 1572872 | tf_op jit(solution)/shard_map/ppermute | solution.py:254
  1.4 1.3 %collective-permute-start = (bf16[1024,256]{1,0:T(8,128)(2,1)}, bf16[1024,256]{1,0:T(8,128)(2,1)}, u32[]{:S(2)}, u32[]{:S(2)}) collective-permute-start(bf16[1024,256]{1,0:T(8,128)(2,1)} %refs_2_.1), channel_id=1, source_target_pairs={{0,2},{1,3},{2,0},{3,1},{4,6},{5,7},{6,4},{7,5},{8,10},{9,11},{10,... | collective-permute-start | bytes 1572872 | tf_op jit(solution)/shard_map/ppermute | solution.py:254
  3.3 1.5 %shard_map.94.refs_0_ = s32[81]{0:T(128)} custom-call(s32[1]{0:T(128)} %bitcast.me_ref, s32[1]{0:T(128)S(6)} %copy.10.cnt_ref, s32[64]{0:T(128)} %rows_ref.1, s32[64]{0:T(128)} %cols_ref.1), custom_call_target="tpu_custom_call" | custom-call | tf_op jit(solution)/shard_map/pallas_call | solution.py:68
  4.8 0.0 collective-permute-done.1.refs_3_
  4.8 0.0 copy-start.4
  4.8 0.8 %copy-done.4 = bf16[1024,256]{1,0:T(8,128)(2,1)} copy-done((bf16[1024,256]{1,0:T(8,128)(2,1)}, bf16[1024,256]{1,0:T(8,128)(2,1)S(1)}, u32[]{:S(2)}) %copy-start.4) | copy-done | bytes 524312
  5.6 0.0 copy-start
  5.6 1.6 %copy-done = bf16[64,128,128]{2,1,0:T(8,128)(2,1)S(1)} copy-done((bf16[64,128,128]{2,1,0:T(8,128)(2,1)S(1)}, bf16[64,128,128]{2,1,0:T(8,128)(2,1)}, u32[]{:S(2)}) %copy-start) | copy-done | bytes 2097176
  7.2 0.0 copy-start.2
  7.2 1.0 %copy-done.2 = bf16[1024,256]{1,0:T(8,128)(2,1)S(1)} copy-done((bf16[1024,256]{1,0:T(8,128)(2,1)S(1)}, bf16[1024,256]{1,0:T(8,128)(2,1)}, u32[]{:S(2)}) %copy-start.2) | copy-done | bytes 524312
  8.2 0.0 copy-start.5
  8.2 1.0 %copy-done.5 = bf16[1024,256]{1,0:T(8,128)(2,1)S(1)} copy-done((bf16[1024,256]{1,0:T(8,128)(2,1)S(1)}, bf16[1024,256]{1,0:T(8,128)(2,1)}, u32[]{:S(2)}) %copy-start.5) | copy-done | bytes 524312
  9.3 0.0 copy-start.7
  9.3 0.7 %copy-done.7 = s32[81]{0:T(128)S(1)} copy-done((s32[81]{0:T(128)S(1)}, s32[81]{0:T(128)}, u32[]{:S(2)}) %copy-start.7) | copy-done | bytes 348
  9.9 0.0 copy-start.1
  9.9 0.0 copy-start.8
  9.9 1.1 %shard_map.95.refs_3_ = f32[8,128,256]{2,1,0:T(8,128)S(1)} custom-call(s32[81]{0:T(128)S(1)} %copy-done.7, bf16[64,128,128]{2,1,0:T(8,128)(2,1)S(1)} %copy-done, bf16[1024,256]{1,0:T(8,128)(2,1)S(1)} %copy-done.2, bf16[1024,256]{1,0:T(8,128)(2,1)S(1)} %copy-done.5), custom_call_target="tpu_custom_call" | custom-call | tf_op jit(solution)/shard_map/pallas_call | solution.py:208
  11.1 4.1 %collective-permute-done.refs_2_ = bf16[1024,256]{1,0:T(8,128)(2,1)} collective-permute-done((bf16[1024,256]{1,0:T(8,128)(2,1)}, bf16[1024,256]{1,0:T(8,128)(2,1)}, u32[]{:S(2)}, u32[]{:S(2)}) %collective-permute-start) | collective-permute-done | bytes 524320 | tf_op jit(solution)/shard_map/ppermute | solution.py:254
  15.2 0.8 %collective-permute-start.2 = (bf16[1024,256]{1,0:T(8,128)(2,1)}, bf16[1024,256]{1,0:T(8,128)(2,1)}, u32[]{:S(2)}, u32[]{:S(2)}) collective-permute-start(bf16[1024,256]{1,0:T(8,128)(2,1)} %collective-permute-done.refs_2_), channel_id=1, source_target_pairs={{0,1},{1,0},{2,3},{3,2},{4,5},{5,4},{6,7},{7,6},{8,9},{9,8},{10,11... | collective-permute-start | bytes 1572872 | tf_op jit(solution)/shard_map/ppermute | solution.py:254
  16.0 0.0 copy-done.1
  16.0 0.0 copy-done.8
  16.0 0.0 copy-start.3
  16.0 0.0 copy-start.6
  16.1 1.7 %shard_map.96.refs_3_ = f32[8,128,256]{2,1,0:T(8,128)S(1)} custom-call(s32[81]{0:T(128)S(1)} %copy-done.8, bf16[64,128,128]{2,1,0:T(8,128)(2,1)S(1)} %copy-done.1, bf16[1024,256]{1,0:T(8,128)(2,1)} %collective-permute-done.refs_2_, f32[8,128,256]{2,1,0:T(8,128)S(1)} %shard_map.95.refs_3_), custom_call_target="tpu_custom_call" | custom-call | tf_op jit(solution)/shard_map/pallas_call | solution.py:208
  17.8 0.1 collective-permute-done.2.refs_2_
  17.9 0.0 copy-done.3
  17.9 0.0 copy-done.6
  17.9 2.9 %shard_map.97 = (bf16[1024,256]{1,0:T(8,128)(2,1)}, bf16[1024,256]{1,0:T(8,128)(2,1)S(1)}, f32[128,256]{1,0:T(8,128)S(1)}, f32[128,256]{1,0:T(8,128)S(1)}) custom-call(s32[81]{0:T(128)S(1)} %copy-done.8, bf16[64,128,128]{2,1,0:T(8,128)(2,1)S(1)} %copy-done.1, bf16[1024,256]{1,0:T(8,128)(2,1)} %collective-permute-done.2.refs_2_, ...), custom_call_target="tpu_custom_call" | custom-call | tf_op jit(solution)/shard_map/pallas_call | solution.py:208
  20.9 0.9 %shard_map.98 = bf16[1024,256]{1,0:T(8,128)(2,1)S(1)} custom-call(s32[81]{0:T(128)S(1)} %copy-done.8, bf16[64,128,128]{2,1,0:T(8,128)(2,1)S(1)} %copy-done.1, bf16[1024,256]{1,0:T(8,128)(2,1)S(1)} %get-tuple-element.26.refs_2_), custom_call_target="tpu_custom_call" | custom-call | tf_op jit(solution)/shard_map/pallas_call | solution.py:238
  21.8 1.9 %collective-permute-start.5 = (bf16[1024,256]{1,0:T(8,128)(2,1)S(1)}, bf16[1024,256]{1,0:T(8,128)(2,1)S(1)}, u32[]{:S(2)}, u32[]{:S(2)}) collective-permute-start(bf16[1024,256]{1,0:T(8,128)(2,1)S(1)} %shard_map.98), channel_id=1, source_target_pairs={{0,1},{1,0},{2,3},{3,2},{4,5},{5,4},{6,7},{7,6},{8,9},{9,8},{10,11... | collective-permute-start | bytes 1572872 | tf_op jit(solution)/shard_map/ppermute | solution.py:254
  23.7 0.1 collective-permute-start.3
  23.8 1.6 %collective-permute-done.3 = f32[128,256]{1,0:T(8,128)S(1)} collective-permute-done((f32[128,256]{1,0:T(8,128)S(1)}, f32[128,256]{1,0:T(8,128)S(1)}, u32[]{:S(2)}, u32[]{:S(2)}) %collective-permute-start.3) | collective-permute-done | bytes 131104 | tf_op jit(solution)/shard_map/ppermute | solution.py:254
  25.5 0.8 %collective-permute-start.4 = (bf16[128,256]{1,0:T(8,128)(2,1)S(1)}, bf16[128,256]{1,0:T(8,128)(2,1)S(1)}, u32[]{:S(2)}, u32[]{:S(2)}) collective-permute-start(bf16[128,256]{1,0:T(8,128)(2,1)S(1)} %add_convert_fusion.6), channel_id=1, source_target_pairs={{0,2},{1,3},{2,0},{3,1},{4,6},{5,7},{6,4},{7,5},{8,10},{9,11},{10,... | collective-permute-start | bytes 196616 | tf_op jit(solution)/shard_map/ppermute | solution.py:257
  26.3 1.2 %shard_map.99 = f32[1024,256]{1,0:T(8,128)S(1)} custom-call(s32[81]{0:T(128)S(1)} %copy-done.8, bf16[64,128,128]{2,1,0:T(8,128)(2,1)S(1)} %copy-done.1, bf16[1024,256]{1,0:T(8,128)(2,1)S(1)} %get-tuple-element.26.refs_2_), custom_call_target="tpu_custom_call" | custom-call | tf_op jit(solution)/shard_map/pallas_call | solution.py:238
  27.5 0.0 collective-permute-done.5
  27.5 1.0 %add_convert_fusion.1 = bf16[1024,256]{1,0:T(8,128)(2,1)} fusion(f32[1024,256]{1,0:T(8,128)S(1)} %shard_map.99, bf16[1024,256]{1,0:T(8,128)(2,1)S(1)} %collective-permute-done.5), kind=kLoop, calls=%fused_computation.1 | loop fusion | flops 786432 | bytes 2097152 | tf_op jit(solution)/shard_map/convert_element_type | solution.py:282
  28.5 0.2 collective-permute-done.4
  28.7 0.9 %shard_map.100 = bf16[1024,256]{1,0:T(8,128)(2,1)S(1)} custom-call(s32[81]{0:T(128)S(1)} %copy-done.8, bf16[64,128,128]{2,1,0:T(8,128)(2,1)S(1)} %copy-done.1, bf16[1024,256]{1,0:T(8,128)(2,1)S(1)} %get-tuple-element.26.refs_2_), custom_call_target="tpu_custom_call" | custom-call | tf_op jit(solution)/shard_map/pallas_call | solution.py:238
  29.6 2.7 %collective-permute-start.7 = (bf16[1024,256]{1,0:T(8,128)(2,1)S(1)}, bf16[1024,256]{1,0:T(8,128)(2,1)S(1)}, u32[]{:S(2)}, u32[]{:S(2)}) collective-permute-start(bf16[1024,256]{1,0:T(8,128)(2,1)S(1)} %shard_map.100), channel_id=1, source_target_pairs={{0,1},{1,0},{2,3},{3,2},{4,5},{5,4},{6,7},{7,6},{8,9},{9,8},{10,11... | collective-permute-start | bytes 1572872 | tf_op jit(solution)/shard_map/ppermute | solution.py:254
  32.3 0.9 %collective-permute-start.6 = (bf16[128,256]{1,0:T(8,128)(2,1)S(1)}, bf16[128,256]{1,0:T(8,128)(2,1)S(1)}, u32[]{:S(2)}, u32[]{:S(2)}) collective-permute-start(bf16[128,256]{1,0:T(8,128)(2,1)S(1)} %add_convert_fusion.5), channel_id=1, source_target_pairs={{0,4},{4,0},{8,12},{12,8},{16,20},{20,16},{24,28},{28,24},{1,5},{5... | collective-permute-start | bytes 196616 | tf_op jit(solution)/shard_map/ppermute | solution.py:257
  33.2 1.7 %collective-permute-start.8 = (bf16[1024,256]{1,0:T(8,128)(2,1)}, bf16[1024,256]{1,0:T(8,128)(2,1)}, u32[]{:S(2)}, u32[]{:S(2)}) collective-permute-start(bf16[1024,256]{1,0:T(8,128)(2,1)} %add_convert_fusion.1), channel_id=1, source_target_pairs={{0,2},{1,3},{2,0},{3,1},{4,6},{5,7},{6,4},{7,5},{8,10},{9,11},{10,... | collective-permute-start | bytes 1572872 | tf_op jit(solution)/shard_map/ppermute | solution.py:254
  34.9 1.0 %collective-permute-done.6 = bf16[128,256]{1,0:T(8,128)(2,1)S(1)} collective-permute-done((bf16[128,256]{1,0:T(8,128)(2,1)S(1)}, bf16[128,256]{1,0:T(8,128)(2,1)S(1)}, u32[]{:S(2)}, u32[]{:S(2)}) %collective-permute-start.6) | collective-permute-done | bytes 65568 | tf_op jit(solution)/shard_map/ppermute | solution.py:257
  36.0 0.1 collective-permute-start.9
  36.1 0.0 collective-permute-done.7.refs_3_
  36.1 0.9 %shard_map.101 = f32[1024,256]{1,0:T(8,128)S(1)} custom-call(s32[81]{0:T(128)S(1)} %copy-done.8, bf16[64,128,128]{2,1,0:T(8,128)(2,1)S(1)} %copy-done.1, bf16[1024,256]{1,0:T(8,128)(2,1)S(1)} %get-tuple-element.26.refs_2_, bf16[1024,256]{1,0:T(8,128)(2,1)S(1)} %collective-permute-done.7.refs_3_), custom_call_target="tpu_custom_call" | custom-call | tf_op jit(solution)/shard_map/pallas_call | solution.py:238
  37.0 2.5 %collective-permute-done.9 = bf16[128,256]{1,0:T(8,128)(2,1)S(1)} collective-permute-done((bf16[128,256]{1,0:T(8,128)(2,1)S(1)}, bf16[128,256]{1,0:T(8,128)(2,1)S(1)}, u32[]{:S(2)}, u32[]{:S(2)}) %collective-permute-start.9) | collective-permute-done | bytes 65568 | tf_op jit(solution)/shard_map/ppermute | solution.py:257
  39.6 3.2 %collective-permute-start.10 = (bf16[128,256]{1,0:T(8,128)(2,1)S(1)}, bf16[128,256]{1,0:T(8,128)(2,1)S(1)}, u32[]{:S(2)}, u32[]{:S(2)}) collective-permute-start(bf16[128,256]{1,0:T(8,128)(2,1)S(1)} %add_convert_fusion.3), channel_id=1, source_target_pairs={{0,16},{4,20},{8,24},{12,28},{16,0},{20,4},{24,8},{28,12},{1,17},{... | collective-permute-start | bytes 196616 | tf_op jit(solution)/shard_map/ppermute | solution.py:257
  42.7 4.5 %collective-permute-done.8 = bf16[1024,256]{1,0:T(8,128)(2,1)} collective-permute-done((bf16[1024,256]{1,0:T(8,128)(2,1)}, bf16[1024,256]{1,0:T(8,128)(2,1)}, u32[]{:S(2)}, u32[]{:S(2)}) %collective-permute-start.8) | collective-permute-done | bytes 524320 | tf_op jit(solution)/shard_map/ppermute | solution.py:254
  47.2 0.0 collective-permute-done.10
  47.3 0.9 %collective-permute-start.11 = (bf16[128,256]{1,0:T(8,128)(2,1)S(1)}, bf16[128,256]{1,0:T(8,128)(2,1)S(1)}, u32[]{:S(2)}, u32[]{:S(2)}) collective-permute-start(bf16[128,256]{1,0:T(8,128)(2,1)S(1)} %add_convert_fusion.2), channel_id=1, source_target_pairs={{0,1},{1,0},{2,3},{3,2},{4,5},{5,4},{6,7},{7,6},{8,9},{9,8},{10,11... | collective-permute-start | bytes 196616 | tf_op jit(solution)/shard_map/ppermute | solution.py:254
  48.2 1.9 %add_convert_fusion = bf16[1024,256]{1,0:T(8,128)(2,1)} fusion(f32[1024,256]{1,0:T(8,128)S(1)} %shard_map.101, bf16[1024,256]{1,0:T(8,128)(2,1)} %collective-permute-done.8), kind=kLoop, calls=%fused_computation | loop fusion | flops 786432 | bytes 2097152 | tf_op jit(solution)/shard_map/convert_element_type | solution.py:295
  50.2 0.0 collective-permute-done.11
  50.2 0.7 %fusion = f32[256,256]{1,0:T(8,128)} fusion(bf16[128,256]{1,0:T(8,128)(2,1)S(1)} %collective-permute-done.11, bf16[128,256]{1,0:T(8,128)(2,1)S(1)} %add_convert_fusion.2, pred[]{:T(512)S(6)} %eq.3), kind=kLoop, calls=%fused_computation.3 | loop fusion | flops 655360 | bytes 393217 | tf_op jit(solution)/shard_map/convert_element_type | solution.py:294
  (5 shorter events, 0.1 us)
Async XLA Ops:
  0.6 4.1 %collective-permute-start.1 = (bf16[1024,256]{1,0:T(8,128)(2,1)}, bf16[1024,256]{1,0:T(8,128)(2,1)S(1)}, u32[]{:S(2)}, u32[]{:S(2)}) collective-permute-start(bf16[1024,256]{1,0:T(8,128)(2,1)} %refs_2_.1), channel_id=1, source_target_pairs={{0,1},{1,0},{2,3},{3,2},{4,5},{5,4},{6,7},{7,6},{8,9},{9,8},{10,11... | collective-permute-start | bytes 1572872 | tf_op jit(solution)/shard_map/ppermute | solution.py:254
  1.4 13.8 %collective-permute-start = (bf16[1024,256]{1,0:T(8,128)(2,1)}, bf16[1024,256]{1,0:T(8,128)(2,1)}, u32[]{:S(2)}, u32[]{:S(2)}) collective-permute-start(bf16[1024,256]{1,0:T(8,128)(2,1)} %refs_2_.1), channel_id=1, source_target_pairs={{0,2},{1,3},{2,0},{3,1},{4,6},{5,7},{6,4},{7,5},{8,10},{9,11},{10,... | collective-permute-start | bytes 1572872 | tf_op jit(solution)/shard_map/ppermute | solution.py:254
  4.8 0.8 %copy-start.4 = (bf16[1024,256]{1,0:T(8,128)(2,1)}, bf16[1024,256]{1,0:T(8,128)(2,1)S(1)}, u32[]{:S(2)}) copy-start(bf16[1024,256]{1,0:T(8,128)(2,1)S(1)} %collective-permute-done.1.refs_3_) | copy-start | bytes 1572868
  5.6 1.6 %copy-start = (bf16[64,128,128]{2,1,0:T(8,128)(2,1)S(1)}, bf16[64,128,128]{2,1,0:T(8,128)(2,1)}, u32[]{:S(2)}) copy-start(bf16[64,128,128]{2,1,0:T(8,128)(2,1)} %refs_1_.13) | copy-start | bytes 6291460
  7.2 1.0 %copy-start.2 = (bf16[1024,256]{1,0:T(8,128)(2,1)S(1)}, bf16[1024,256]{1,0:T(8,128)(2,1)}, u32[]{:S(2)}) copy-start(bf16[1024,256]{1,0:T(8,128)(2,1)} %refs_2_.1) | copy-start | bytes 1572868
  8.2 1.0 %copy-start.5 = (bf16[1024,256]{1,0:T(8,128)(2,1)S(1)}, bf16[1024,256]{1,0:T(8,128)(2,1)}, u32[]{:S(2)}) copy-start(bf16[1024,256]{1,0:T(8,128)(2,1)} %copy-done.4) | copy-start | bytes 1572868
  9.3 0.7 %copy-start.7 = (s32[81]{0:T(128)S(1)}, s32[81]{0:T(128)}, u32[]{:S(2)}) copy-start(s32[81]{0:T(128)} %shard_map.94.refs_0_) | copy-start | bytes 976
  9.9 6.1 %copy-start.1 = (bf16[64,128,128]{2,1,0:T(8,128)(2,1)S(1)}, bf16[64,128,128]{2,1,0:T(8,128)(2,1)}, u32[]{:S(2)}) copy-start(bf16[64,128,128]{2,1,0:T(8,128)(2,1)} %refs_1_.13) | copy-start | bytes 6291460
  9.9 6.1 %copy-start.8 = (s32[81]{0:T(128)S(1)}, s32[81]{0:T(128)}, u32[]{:S(2)}) copy-start(s32[81]{0:T(128)} %shard_map.94.refs_0_) | copy-start | bytes 976
  15.2 2.7 %collective-permute-start.2 = (bf16[1024,256]{1,0:T(8,128)(2,1)}, bf16[1024,256]{1,0:T(8,128)(2,1)}, u32[]{:S(2)}, u32[]{:S(2)}) collective-permute-start(bf16[1024,256]{1,0:T(8,128)(2,1)} %collective-permute-done.refs_2_), channel_id=1, source_target_pairs={{0,1},{1,0},{2,3},{3,2},{4,5},{5,4},{6,7},{7,6},{8,9},{9,8},{10,11... | collective-permute-start | bytes 1572872 | tf_op jit(solution)/shard_map/ppermute | solution.py:254
  16.0 1.9 %copy-start.3 = (bf16[1024,256]{1,0:T(8,128)(2,1)S(1)}, bf16[1024,256]{1,0:T(8,128)(2,1)}, u32[]{:S(2)}) copy-start(bf16[1024,256]{1,0:T(8,128)(2,1)} %refs_5_.1) | copy-start | bytes 1572868
  16.0 1.9 %copy-start.6 = (bf16[256,256]{1,0:T(8,128)(2,1)S(1)}, bf16[256,256]{1,0:T(8,128)(2,1)}, u32[]{:S(2)}) copy-start(bf16[256,256]{1,0:T(8,128)(2,1)} %refs_4_.1) | copy-start | bytes 393220
  21.8 5.7 %collective-permute-start.5 = (bf16[1024,256]{1,0:T(8,128)(2,1)S(1)}, bf16[1024,256]{1,0:T(8,128)(2,1)S(1)}, u32[]{:S(2)}, u32[]{:S(2)}) collective-permute-start(bf16[1024,256]{1,0:T(8,128)(2,1)S(1)} %shard_map.98), channel_id=1, source_target_pairs={{0,1},{1,0},{2,3},{3,2},{4,5},{5,4},{6,7},{7,6},{8,9},{9,8},{10,11... | collective-permute-start | bytes 1572872 | tf_op jit(solution)/shard_map/ppermute | solution.py:254
  23.7 1.7 %collective-permute-start.3 = (f32[128,256]{1,0:T(8,128)S(1)}, f32[128,256]{1,0:T(8,128)S(1)}, u32[]{:S(2)}, u32[]{:S(2)}) collective-permute-start(f32[128,256]{1,0:T(8,128)S(1)} %get-tuple-element.20), channel_id=1, source_target_pairs={{0,1},{1,0},{2,3},{3,2},{4,5},{5,4},{6,7},{7,6},{8,9},{9,8},{10,11... | collective-permute-start | bytes 393224 | tf_op jit(solution)/shard_map/ppermute | solution.py:254
  25.5 3.2 %collective-permute-start.4 = (bf16[128,256]{1,0:T(8,128)(2,1)S(1)}, bf16[128,256]{1,0:T(8,128)(2,1)S(1)}, u32[]{:S(2)}, u32[]{:S(2)}) collective-permute-start(bf16[128,256]{1,0:T(8,128)(2,1)S(1)} %add_convert_fusion.6), channel_id=1, source_target_pairs={{0,2},{1,3},{2,0},{3,1},{4,6},{5,7},{6,4},{7,5},{8,10},{9,11},{10,... | collective-permute-start | bytes 196616 | tf_op jit(solution)/shard_map/ppermute | solution.py:257
  29.6 6.4 %collective-permute-start.7 = (bf16[1024,256]{1,0:T(8,128)(2,1)S(1)}, bf16[1024,256]{1,0:T(8,128)(2,1)S(1)}, u32[]{:S(2)}, u32[]{:S(2)}) collective-permute-start(bf16[1024,256]{1,0:T(8,128)(2,1)S(1)} %shard_map.100), channel_id=1, source_target_pairs={{0,1},{1,0},{2,3},{3,2},{4,5},{5,4},{6,7},{7,6},{8,9},{9,8},{10,11... | collective-permute-start | bytes 1572872 | tf_op jit(solution)/shard_map/ppermute | solution.py:254
  32.3 3.7 %collective-permute-start.6 = (bf16[128,256]{1,0:T(8,128)(2,1)S(1)}, bf16[128,256]{1,0:T(8,128)(2,1)S(1)}, u32[]{:S(2)}, u32[]{:S(2)}) collective-permute-start(bf16[128,256]{1,0:T(8,128)(2,1)S(1)} %add_convert_fusion.5), channel_id=1, source_target_pairs={{0,4},{4,0},{8,12},{12,8},{16,20},{20,16},{24,28},{28,24},{1,5},{5... | collective-permute-start | bytes 196616 | tf_op jit(solution)/shard_map/ppermute | solution.py:257
  33.2 14.0 %collective-permute-start.8 = (bf16[1024,256]{1,0:T(8,128)(2,1)}, bf16[1024,256]{1,0:T(8,128)(2,1)}, u32[]{:S(2)}, u32[]{:S(2)}) collective-permute-start(bf16[1024,256]{1,0:T(8,128)(2,1)} %add_convert_fusion.1), channel_id=1, source_target_pairs={{0,2},{1,3},{2,0},{3,1},{4,6},{5,7},{6,4},{7,5},{8,10},{9,11},{10,... | collective-permute-start | bytes 1572872 | tf_op jit(solution)/shard_map/ppermute | solution.py:254
  36.0 3.6 %collective-permute-start.9 = (bf16[128,256]{1,0:T(8,128)(2,1)S(1)}, bf16[128,256]{1,0:T(8,128)(2,1)S(1)}, u32[]{:S(2)}, u32[]{:S(2)}) collective-permute-start(bf16[128,256]{1,0:T(8,128)(2,1)S(1)} %add_convert_fusion.4), channel_id=1, source_target_pairs={{0,8},{4,12},{8,0},{12,4},{16,24},{20,28},{24,16},{28,20},{1,9},{5... | collective-permute-start | bytes 196616 | tf_op jit(solution)/shard_map/ppermute | solution.py:257
  39.6 7.7 %collective-permute-start.10 = (bf16[128,256]{1,0:T(8,128)(2,1)S(1)}, bf16[128,256]{1,0:T(8,128)(2,1)S(1)}, u32[]{:S(2)}, u32[]{:S(2)}) collective-permute-start(bf16[128,256]{1,0:T(8,128)(2,1)S(1)} %add_convert_fusion.3), channel_id=1, source_target_pairs={{0,16},{4,20},{8,24},{12,28},{16,0},{20,4},{24,8},{28,12},{1,17},{... | collective-permute-start | bytes 196616 | tf_op jit(solution)/shard_map/ppermute | solution.py:257
  47.3 2.9 %collective-permute-start.11 = (bf16[128,256]{1,0:T(8,128)(2,1)S(1)}, bf16[128,256]{1,0:T(8,128)(2,1)S(1)}, u32[]{:S(2)}, u32[]{:S(2)}) collective-permute-start(bf16[128,256]{1,0:T(8,128)(2,1)S(1)} %add_convert_fusion.2), channel_id=1, source_target_pairs={{0,1},{1,0},{2,3},{3,2},{4,5},{5,4},{6,7},{7,6},{8,9},{9,8},{10,11... | collective-permute-start | bytes 196616 | tf_op jit(solution)/shard_map/ppermute | solution.py:254

commit v3 on v2

--- a/solution.py
+++ b/solution.py
@@ -215,7 +215,7 @@
     )(*args)
 
 
-def backward(plan, sources, blocks, extra=None, dtype=BF16):
+def backward(plan, sources, blocks, extra=None, dtype=BF16, us=0):
     hid = sources[0][3].shape[1]
     args = [part for source in sources for part in source[1:]]
     specs = [SMEM, VMEM, VMEM] * len(sources)
@@ -242,6 +242,9 @@
         out_specs=VMEM,
         scratch_shapes=[pltpu.VMEM((blocks + 1, TILE, hid), F32)],
         compiler_params=params(40 if blocks > 8 else 12),
+        cost_estimate=pl.CostEstimate(
+            flops=int(us * 1.1e9), bytes_accessed=1024, transcendentals=0
+        ),
     )(*args)
 
 
@@ -271,28 +274,28 @@
         plan, lst, tiles, [diag], [3], acc, (weight, cotangent, core.reshape(1))
     )
 
-    def part(rel, sw, extra=None, dtype=BF16):
-        return backward(plan, [(rel, lst, tiles, sw)], blocks_dev, extra, dtype)
+    def part(rel, sw, extra=None, dtype=BF16, us=0):
+        return backward(plan, [(rel, lst, tiles, sw)], blocks_dev, extra, dtype, us)
 
     send = swap(send, 1)
     p3 = part(3, sw)
     r3 = swap(p3, 1)
-    w = (keep + tie(send, p3)).astype(BF16)
-    q = part(2, tie(sw, w), None, F32)
+    w = (keep + send).astype(BF16)
+    q = part(2, tie(sw, w), None, F32, 10)
     q = (q + r3.astype(F32)).astype(BF16)
     q_far = swap(q, 2)
     w = fold(w, "grp", 4, 2, q)
+    p0 = part(0, tie(sw, w), None, F32)
+    w = fold(w, "row", 8, 1, p0)
     p1 = part(1, tie(sw, w))
     r1 = swap(p1, 1)
-    w = fold(w, "row", 8, 1, p1)
-    p0 = part(0, tie(sw, w), r1, F32)
-    w = fold(w, "row", 8, 2, p0)
+    w = fold(w, "row", 8, 2, p1)
     w = fold(w, "row", 8, 4, q_far)
-    other = swap(w, 1)
+    feature_grad = (p0 + r1.astype(F32) + q_far.astype(F32)).astype(BF16)
+    other = tie(swap(w, 1), feature_grad)
     weight_grad = jnp.where(
         core == 0, jnp.concatenate([w, other]), jnp.concatenate([other, w])
     ).astype(F32)
-    feature_grad = (p0 + q_far.astype(F32)).astype(BF16)
     return activated, feature_grad, weight_grad
 
 

time: 51.9 us -> 48.1 us (0.927)
  the two profiles are of different devices: /device:TPU:9 before, /device:TPU:0 now
where the time goes in v3:
time: 48.1 us; the launch traced here: 47.6 us
  starting transfers between devices  12.8 us (27%)
  Pallas kernels  12.7 us (26%)
  waiting for transfers between devices  11.7 us (24%)
  local copies, waits for them, and re-layouts  5.14 us (11%)
  other arithmetic  3.79 us (8%)
  between operations  1.43 us (3%)
    ppermute x4, starting transfers between devices, fold(): other = lax.ppermute(w, axis, [(i, i ^ bit) for i in range(size)])  7.57 us
    ppermute x4, waiting for transfers between devices, fold(): other = lax.ppermute(w, axis, [(i, i ^ bit) for i in range(size)])  6.08 us
    pallas_call x3, Pallas kernels, forward(): pl.pallas_call(body, out_shape=out, in_specs=specs, out_specs=out_specs,...  6.01 us
    ppermute x8, waiting for transfers between devices, swap(): return lax.ppermute(x, 'grp', [(i, i ^ bit) for i in range(4)])  5.62 us
    ppermute x8, starting transfers between devices, swap(): return lax.ppermute(x, 'grp', [(i, i ^ bit) for i in range(4)])  5.23 us
    unnamed x18, local copies, waits for them, and re-layouts  5.14 us
    pallas_call x4, Pallas kernels, backward(): pl.pallas_call(body, out_shape=jax.ShapeDtypeStruct((blocks * TILE, hid),...  5.11 us
    convert_element_type x1, other arithmetic, local_four(): feature_grad = (p0 + r1.astype(F32) + q_far.astype(F32)).astype(BF16)  1.99 us
  transfers between devices with their start and end apart: 12, of which 7 were waited for; matrix products, arithmetic and copies ran while one was open for 6% of the time, Pallas kernels for 20%

profile of v3, /device:TPU:0, one launch (start us, length us, event | category | flops | bytes accessed | tf_op | source)
XLA Modules:
  0.0 47.6 jit_solution(1617325012489825172)
XLA Ops:
  0.6 0.5 %collective-permute-start.1 = (bf16[1024,256]{1,0:T(8,128)(2,1)}, bf16[1024,256]{1,0:T(8,128)(2,1)S(1)}, u32[]{:S(2)}, u32[]{:S(2)}) collective-permute-start(bf16[1024,256]{1,0:T(8,128)(2,1)} %refs_2_.1), channel_id=1, source_target_pairs={{0,1},{1,0},{2,3},{3,2},{4,5},{5,4},{6,7},{7,6},{8,9},{9,8},{10,11... | collective-permute-start | bytes 1572872 | tf_op jit(solution)/shard_map/ppermute | solution.py:257
  1.1 2.6 %collective-permute-start = (bf16[1024,256]{1,0:T(8,128)(2,1)}, bf16[1024,256]{1,0:T(8,128)(2,1)}, u32[]{:S(2)}, u32[]{:S(2)}) collective-permute-start(bf16[1024,256]{1,0:T(8,128)(2,1)} %refs_2_.1), channel_id=1, source_target_pairs={{0,2},{1,3},{2,0},{3,1},{4,6},{5,7},{6,4},{7,5},{8,10},{9,11},{10,... | collective-permute-start | bytes 1572872 | tf_op jit(solution)/shard_map/ppermute | solution.py:257
  4.4 1.6 %shard_map.94.refs_0_ = s32[81]{0:T(128)} custom-call(s32[1]{0:T(128)} %bitcast.me_ref, s32[1]{0:T(128)S(6)} %copy.10.cnt_ref, s32[64]{0:T(128)} %rows_ref.1, s32[64]{0:T(128)} %cols_ref.1), custom_call_target="tpu_custom_call" | custom-call | tf_op jit(solution)/shard_map/pallas_call | solution.py:68
  6.0 0.0 collective-permute-done.1.refs_3_
  6.0 0.0 copy-start.4
  6.0 0.8 %copy-done.4 = bf16[1024,256]{1,0:T(8,128)(2,1)} copy-done((bf16[1024,256]{1,0:T(8,128)(2,1)}, bf16[1024,256]{1,0:T(8,128)(2,1)S(1)}, u32[]{:S(2)}) %copy-start.4) | copy-done | bytes 524312
  6.8 0.0 copy-start
  6.8 1.6 %copy-done = bf16[64,128,128]{2,1,0:T(8,128)(2,1)S(1)} copy-done((bf16[64,128,128]{2,1,0:T(8,128)(2,1)S(1)}, bf16[64,128,128]{2,1,0:T(8,128)(2,1)}, u32[]{:S(2)}) %copy-start) | copy-done | bytes 2097176
  8.4 0.0 copy-start.2
  8.4 1.0 %copy-done.2 = bf16[1024,256]{1,0:T(8,128)(2,1)S(1)} copy-done((bf16[1024,256]{1,0:T(8,128)(2,1)S(1)}, bf16[1024,256]{1,0:T(8,128)(2,1)}, u32[]{:S(2)}) %copy-start.2) | copy-done | bytes 524312
  9.4 0.0 copy-start.5
  9.4 1.0 %copy-done.5 = bf16[1024,256]{1,0:T(8,128)(2,1)S(1)} copy-done((bf16[1024,256]{1,0:T(8,128)(2,1)S(1)}, bf16[1024,256]{1,0:T(8,128)(2,1)}, u32[]{:S(2)}) %copy-start.5) | copy-done | bytes 524312
  10.5 0.0 copy-start.7
  10.5 0.7 %copy-done.7 = s32[81]{0:T(128)S(1)} copy-done((s32[81]{0:T(128)S(1)}, s32[81]{0:T(128)}, u32[]{:S(2)}) %copy-start.7) | copy-done | bytes 348
  11.1 0.0 copy-start.1
  11.1 0.0 copy-start.8
  11.1 1.1 %shard_map.95.refs_3_ = f32[8,128,256]{2,1,0:T(8,128)S(1)} custom-call(s32[81]{0:T(128)S(1)} %copy-done.7, bf16[64,128,128]{2,1,0:T(8,128)(2,1)S(1)} %copy-done, bf16[1024,256]{1,0:T(8,128)(2,1)S(1)} %copy-done.2, bf16[1024,256]{1,0:T(8,128)(2,1)S(1)} %copy-done.5), custom_call_target="tpu_custom_call" | custom-call | tf_op jit(solution)/shard_map/pallas_call | solution.py:208
  12.3 4.3 %collective-permute-done.refs_2_ = bf16[1024,256]{1,0:T(8,128)(2,1)} collective-permute-done((bf16[1024,256]{1,0:T(8,128)(2,1)}, bf16[1024,256]{1,0:T(8,128)(2,1)}, u32[]{:S(2)}, u32[]{:S(2)}) %collective-permute-start) | collective-permute-done | bytes 524320 | tf_op jit(solution)/shard_map/ppermute | solution.py:257
  16.6 0.0 collective-permute-start.2
  16.6 0.0 copy-done.1
  16.6 0.0 copy-done.8
  16.6 0.0 copy-start.3
  16.6 0.0 copy-start.6
  16.6 1.7 %shard_map.96.refs_3_ = f32[8,128,256]{2,1,0:T(8,128)S(1)} custom-call(s32[81]{0:T(128)S(1)} %copy-done.8, bf16[64,128,128]{2,1,0:T(8,128)(2,1)S(1)} %copy-done.1, bf16[1024,256]{1,0:T(8,128)(2,1)} %collective-permute-done.refs_2_, f32[8,128,256]{2,1,0:T(8,128)S(1)} %shard_map.95.refs_3_), custom_call_target="tpu_custom_call" | custom-call | tf_op jit(solution)/shard_map/pallas_call | solution.py:208
  18.3 0.5 %collective-permute-done.2.refs_2_ = bf16[1024,256]{1,0:T(8,128)(2,1)} collective-permute-done((bf16[1024,256]{1,0:T(8,128)(2,1)}, bf16[1024,256]{1,0:T(8,128)(2,1)}, u32[]{:S(2)}, u32[]{:S(2)}) %collective-permute-start.2) | collective-permute-done | bytes 524320 | tf_op jit(solution)/shard_map/ppermute | solution.py:257
  18.8 0.0 copy-done.3
  18.8 0.0 copy-done.6
  18.8 3.2 %shard_map.97 = (bf16[1024,256]{1,0:T(8,128)(2,1)}, bf16[1024,256]{1,0:T(8,128)(2,1)S(1)}, f32[128,256]{1,0:T(8,128)S(1)}, f32[128,256]{1,0:T(8,128)S(1)}) custom-call(s32[81]{0:T(128)S(1)} %copy-done.8, bf16[64,128,128]{2,1,0:T(8,128)(2,1)S(1)} %copy-done.1, bf16[1024,256]{1,0:T(8,128)(2,1)} %collective-permute-done.2.refs_2_, ...), custom_call_target="tpu_custom_call" | custom-call | tf_op jit(solution)/shard_map/pallas_call | solution.py:208
  22.0 0.0 collective-permute-start.3
  22.0 1.2 %shard_map.99 = bf16[1024,256]{1,0:T(8,128)(2,1)S(1)} custom-call(s32[81]{0:T(128)S(1)} %copy-done.8, bf16[64,128,128]{2,1,0:T(8,128)(2,1)S(1)} %copy-done.1, bf16[1024,256]{1,0:T(8,128)(2,1)S(1)} %get-tuple-element.25.refs_2_), custom_call_target="tpu_custom_call" | custom-call | bytes 1024 | tf_op jit(solution)/shard_map/pallas_call | solution.py:238
  23.2 0.3 collective-permute-start.5
  23.5 0.0 collective-permute-done.3
  23.5 3.9 %collective-permute-start.4 = (bf16[128,256]{1,0:T(8,128)(2,1)S(1)}, bf16[128,256]{1,0:T(8,128)(2,1)S(1)}, u32[]{:S(2)}, u32[]{:S(2)}) collective-permute-start(bf16[128,256]{1,0:T(8,128)(2,1)S(1)} %add_convert_fusion.6), channel_id=1, source_target_pairs={{0,2},{1,3},{2,0},{3,1},{4,6},{5,7},{6,4},{7,5},{8,10},{9,11},{10,... | collective-permute-start | bytes 196616 | tf_op jit(solution)/shard_map/ppermute | solution.py:260
  27.4 1.2 %shard_map.98 = f32[1024,256]{1,0:T(8,128)S(1)} custom-call(s32[81]{0:T(128)S(1)} %copy-done.8, bf16[64,128,128]{2,1,0:T(8,128)(2,1)S(1)} %copy-done.1, bf16[1024,256]{1,0:T(8,128)(2,1)S(1)} %get-tuple-element.25.refs_2_), custom_call_target="tpu_custom_call" | custom-call | flops 11000000512 | bytes 1024 | tf_op jit(solution)/shard_map/pallas_call | solution.py:238
  28.6 0.0 collective-permute-done.5
  28.6 1.0 %add_convert_fusion.1 = bf16[1024,256]{1,0:T(8,128)(2,1)} fusion(f32[1024,256]{1,0:T(8,128)S(1)} %shard_map.98, bf16[1024,256]{1,0:T(8,128)(2,1)S(1)} %collective-permute-done.5), kind=kLoop, calls=%fused_computation.1 | loop fusion | flops 786432 | bytes 2097152 | tf_op jit(solution)/shard_map/convert_element_type | solution.py:285
  29.6 0.3 collective-permute-done.4
  29.9 1.1 %collective-permute-start.6 = (bf16[128,256]{1,0:T(8,128)(2,1)S(1)}, bf16[128,256]{1,0:T(8,128)(2,1)S(1)}, u32[]{:S(2)}, u32[]{:S(2)}) collective-permute-start(bf16[128,256]{1,0:T(8,128)(2,1)S(1)} %add_convert_fusion.5), channel_id=1, source_target_pairs={{0,4},{4,0},{8,12},{12,8},{16,20},{20,16},{24,28},{28,24},{1,5},{5... | collective-permute-start | bytes 196616 | tf_op jit(solution)/shard_map/ppermute | solution.py:260
  31.0 1.7 %collective-permute-start.8 = (bf16[1024,256]{1,0:T(8,128)(2,1)}, bf16[1024,256]{1,0:T(8,128)(2,1)}, u32[]{:S(2)}, u32[]{:S(2)}) collective-permute-start(bf16[1024,256]{1,0:T(8,128)(2,1)} %add_convert_fusion.1), channel_id=1, source_target_pairs={{0,2},{1,3},{2,0},{3,1},{4,6},{5,7},{6,4},{7,5},{8,10},{9,11},{10,... | collective-permute-start | bytes 1572872 | tf_op jit(solution)/shard_map/ppermute | solution.py:257
  32.7 1.0 %shard_map.100 = f32[1024,256]{1,0:T(8,128)S(1)} custom-call(s32[81]{0:T(128)S(1)} %copy-done.8, bf16[64,128,128]{2,1,0:T(8,128)(2,1)S(1)} %copy-done.1, bf16[1024,256]{1,0:T(8,128)(2,1)S(1)} %get-tuple-element.25.refs_2_), custom_call_target="tpu_custom_call" | custom-call | bytes 1024 | tf_op jit(solution)/shard_map/pallas_call | solution.py:238
  33.7 0.6 %collective-permute-done.6 = bf16[128,256]{1,0:T(8,128)(2,1)S(1)} collective-permute-done((bf16[128,256]{1,0:T(8,128)(2,1)S(1)}, bf16[128,256]{1,0:T(8,128)(2,1)S(1)}, u32[]{:S(2)}, u32[]{:S(2)}) %collective-permute-start.6) | collective-permute-done | bytes 65568 | tf_op jit(solution)/shard_map/ppermute | solution.py:260
  34.2 0.1 collective-permute-start.9
  34.3 1.7 %shard_map.101 = bf16[1024,256]{1,0:T(8,128)(2,1)} custom-call(s32[81]{0:T(128)S(1)} %copy-done.8, bf16[64,128,128]{2,1,0:T(8,128)(2,1)S(1)} %copy-done.1, bf16[1024,256]{1,0:T(8,128)(2,1)S(1)} %get-tuple-element.25.refs_2_), custom_call_target="tpu_custom_call" | custom-call | bytes 1024 | tf_op jit(solution)/shard_map/pallas_call | solution.py:238
  36.1 0.0 collective-permute-start.7
  36.1 2.5 %collective-permute-done.9 = bf16[128,256]{1,0:T(8,128)(2,1)S(1)} collective-permute-done((bf16[128,256]{1,0:T(8,128)(2,1)S(1)}, bf16[128,256]{1,0:T(8,128)(2,1)S(1)}, u32[]{:S(2)}, u32[]{:S(2)}) %collective-permute-start.9) | collective-permute-done | bytes 65568 | tf_op jit(solution)/shard_map/ppermute | solution.py:260
  38.6 2.5 %collective-permute-start.10 = (bf16[128,256]{1,0:T(8,128)(2,1)S(1)}, bf16[128,256]{1,0:T(8,128)(2,1)S(1)}, u32[]{:S(2)}, u32[]{:S(2)}) collective-permute-start(bf16[128,256]{1,0:T(8,128)(2,1)S(1)} %add_convert_fusion.3), channel_id=1, source_target_pairs={{0,16},{4,20},{8,24},{12,28},{16,0},{20,4},{24,8},{28,12},{1,17},{... | collective-permute-start | bytes 196616 | tf_op jit(solution)/shard_map/ppermute | solution.py:260
  41.1 2.8 %collective-permute-done.10 = bf16[128,256]{1,0:T(8,128)(2,1)S(1)} collective-permute-done((bf16[128,256]{1,0:T(8,128)(2,1)S(1)}, bf16[128,256]{1,0:T(8,128)(2,1)S(1)}, u32[]{:S(2)}, u32[]{:S(2)}) %collective-permute-start.10) | collective-permute-done | bytes 65568 | tf_op jit(solution)/shard_map/ppermute | solution.py:260
  43.9 0.8 %collective-permute-done.8 = bf16[1024,256]{1,0:T(8,128)(2,1)} collective-permute-done((bf16[1024,256]{1,0:T(8,128)(2,1)}, bf16[1024,256]{1,0:T(8,128)(2,1)}, u32[]{:S(2)}, u32[]{:S(2)}) %collective-permute-start.8) | collective-permute-done | bytes 524320 | tf_op jit(solution)/shard_map/ppermute | solution.py:257
  44.8 0.1 collective-permute-start.11
  44.8 0.0 collective-permute-done.7
  44.8 2.0 %add_convert_fusion = bf16[1024,256]{1,0:T(8,128)(2,1)} fusion(bf16[1024,256]{1,0:T(8,128)(2,1)} %collective-permute-done.8, f32[1024,256]{1,0:T(8,128)S(1)} %shard_map.100, bf16[1024,256]{1,0:T(8,128)(2,1)S(1)} %collective-permute-done.7), kind=kLoop, calls=%fused_computation | loop fusion | flops 1310720 | bytes 2621440 | tf_op jit(solution)/shard_map/convert_element_type | solution.py:294
  46.8 0.0 collective-permute-done.11
  46.8 0.7 %fusion = f32[256,256]{1,0:T(8,128)} fusion(bf16[128,256]{1,0:T(8,128)(2,1)S(1)} %collective-permute-done.11, bf16[128,256]{1,0:T(8,128)(2,1)S(1)} %add_convert_fusion.2, pred[]{:T(512)S(6)} %eq.3), kind=kLoop, calls=%fused_computation.3 | loop fusion | flops 655360 | bytes 393217 | tf_op jit(solution)/shard_map/convert_element_type | solution.py:298
  (5 shorter events, 0.1 us)
Async XLA Ops:
  0.6 5.4 %collective-permute-start.1 = (bf16[1024,256]{1,0:T(8,128)(2,1)}, bf16[1024,256]{1,0:T(8,128)(2,1)S(1)}, u32[]{:S(2)}, u32[]{:S(2)}) collective-permute-start(bf16[1024,256]{1,0:T(8,128)(2,1)} %refs_2_.1), channel_id=1, source_target_pairs={{0,1},{1,0},{2,3},{3,2},{4,5},{5,4},{6,7},{7,6},{8,9},{9,8},{10,11... | collective-permute-start | bytes 1572872 | tf_op jit(solution)/shard_map/ppermute | solution.py:257
  1.1 15.4 %collective-permute-start = (bf16[1024,256]{1,0:T(8,128)(2,1)}, bf16[1024,256]{1,0:T(8,128)(2,1)}, u32[]{:S(2)}, u32[]{:S(2)}) collective-permute-start(bf16[1024,256]{1,0:T(8,128)(2,1)} %refs_2_.1), channel_id=1, source_target_pairs={{0,2},{1,3},{2,0},{3,1},{4,6},{5,7},{6,4},{7,5},{8,10},{9,11},{10,... | collective-permute-start | bytes 1572872 | tf_op jit(solution)/shard_map/ppermute | solution.py:257
  6.0 0.8 %copy-start.4 = (bf16[1024,256]{1,0:T(8,128)(2,1)}, bf16[1024,256]{1,0:T(8,128)(2,1)S(1)}, u32[]{:S(2)}) copy-start(bf16[1024,256]{1,0:T(8,128)(2,1)S(1)} %collective-permute-done.1.refs_3_) | copy-start | bytes 1572868
  6.8 1.6 %copy-start = (bf16[64,128,128]{2,1,0:T(8,128)(2,1)S(1)}, bf16[64,128,128]{2,1,0:T(8,128)(2,1)}, u32[]{:S(2)}) copy-start(bf16[64,128,128]{2,1,0:T(8,128)(2,1)} %refs_1_.13) | copy-start | bytes 6291460
  8.4 1.0 %copy-start.2 = (bf16[1024,256]{1,0:T(8,128)(2,1)S(1)}, bf16[1024,256]{1,0:T(8,128)(2,1)}, u32[]{:S(2)}) copy-start(bf16[1024,256]{1,0:T(8,128)(2,1)} %refs_2_.1) | copy-start | bytes 1572868
  9.4 1.0 %copy-start.5 = (bf16[1024,256]{1,0:T(8,128)(2,1)S(1)}, bf16[1024,256]{1,0:T(8,128)(2,1)}, u32[]{:S(2)}) copy-start(bf16[1024,256]{1,0:T(8,128)(2,1)} %copy-done.4) | copy-start | bytes 1572868
  10.5 0.7 %copy-start.7 = (s32[81]{0:T(128)S(1)}, s32[81]{0:T(128)}, u32[]{:S(2)}) copy-start(s32[81]{0:T(128)} %shard_map.94.refs_0_) | copy-start | bytes 976
  11.1 5.4 %copy-start.1 = (bf16[64,128,128]{2,1,0:T(8,128)(2,1)S(1)}, bf16[64,128,128]{2,1,0:T(8,128)(2,1)}, u32[]{:S(2)}) copy-start(bf16[64,128,128]{2,1,0:T(8,128)(2,1)} %refs_1_.13) | copy-start | bytes 6291460
  11.1 5.4 %copy-start.8 = (s32[81]{0:T(128)S(1)}, s32[81]{0:T(128)}, u32[]{:S(2)}) copy-start(s32[81]{0:T(128)} %shard_map.94.refs_0_) | copy-start | bytes 976
  16.6 2.3 %collective-permute-start.2 = (bf16[1024,256]{1,0:T(8,128)(2,1)}, bf16[1024,256]{1,0:T(8,128)(2,1)}, u32[]{:S(2)}, u32[]{:S(2)}) collective-permute-start(bf16[1024,256]{1,0:T(8,128)(2,1)} %collective-permute-done.refs_2_), channel_id=1, source_target_pairs={{0,1},{1,0},{2,3},{3,2},{4,5},{5,4},{6,7},{7,6},{8,9},{9,8},{10,11... | collective-permute-start | bytes 1572872 | tf_op jit(solution)/shard_map/ppermute | solution.py:257
  16.6 2.2 %copy-start.3 = (bf16[1024,256]{1,0:T(8,128)(2,1)S(1)}, bf16[1024,256]{1,0:T(8,128)(2,1)}, u32[]{:S(2)}) copy-start(bf16[1024,256]{1,0:T(8,128)(2,1)} %refs_5_.1) | copy-start | bytes 1572868
  16.6 2.2 %copy-start.6 = (bf16[256,256]{1,0:T(8,128)(2,1)S(1)}, bf16[256,256]{1,0:T(8,128)(2,1)}, u32[]{:S(2)}) copy-start(bf16[256,256]{1,0:T(8,128)(2,1)} %refs_4_.1) | copy-start | bytes 393220
  22.0 1.5 %collective-permute-start.3 = (f32[128,256]{1,0:T(8,128)S(1)}, f32[128,256]{1,0:T(8,128)S(1)}, u32[]{:S(2)}, u32[]{:S(2)}) collective-permute-start(f32[128,256]{1,0:T(8,128)S(1)} %get-tuple-element.20), channel_id=1, source_target_pairs={{0,1},{1,0},{2,3},{3,2},{4,5},{5,4},{6,7},{7,6},{8,9},{9,8},{10,11... | collective-permute-start | bytes 393224 | tf_op jit(solution)/shard_map/ppermute | solution.py:257
  23.2 5.4 %collective-permute-start.5 = (bf16[1024,256]{1,0:T(8,128)(2,1)S(1)}, bf16[1024,256]{1,0:T(8,128)(2,1)S(1)}, u32[]{:S(2)}, u32[]{:S(2)}) collective-permute-start(bf16[1024,256]{1,0:T(8,128)(2,1)S(1)} %shard_map.99), channel_id=1, source_target_pairs={{0,1},{1,0},{2,3},{3,2},{4,5},{5,4},{6,7},{7,6},{8,9},{9,8},{10,11... | collective-permute-start | bytes 1572872 | tf_op jit(solution)/shard_map/ppermute | solution.py:257
  23.5 6.3 %collective-permute-start.4 = (bf16[128,256]{1,0:T(8,128)(2,1)S(1)}, bf16[128,256]{1,0:T(8,128)(2,1)S(1)}, u32[]{:S(2)}, u32[]{:S(2)}) collective-permute-start(bf16[128,256]{1,0:T(8,128)(2,1)S(1)} %add_convert_fusion.6), channel_id=1, source_target_pairs={{0,2},{1,3},{2,0},{3,1},{4,6},{5,7},{6,4},{7,5},{8,10},{9,11},{10,... | collective-permute-start | bytes 196616 | tf_op jit(solution)/shard_map/ppermute | solution.py:260
  29.9 4.3 %collective-permute-start.6 = (bf16[128,256]{1,0:T(8,128)(2,1)S(1)}, bf16[128,256]{1,0:T(8,128)(2,1)S(1)}, u32[]{:S(2)}, u32[]{:S(2)}) collective-permute-start(bf16[128,256]{1,0:T(8,128)(2,1)S(1)} %add_convert_fusion.5), channel_id=1, source_target_pairs={{0,4},{4,0},{8,12},{12,8},{16,20},{20,16},{24,28},{28,24},{1,5},{5... | collective-permute-start | bytes 196616 | tf_op jit(solution)/shard_map/ppermute | solution.py:260
  31.0 13.8 %collective-permute-start.8 = (bf16[1024,256]{1,0:T(8,128)(2,1)}, bf16[1024,256]{1,0:T(8,128)(2,1)}, u32[]{:S(2)}, u32[]{:S(2)}) collective-permute-start(bf16[1024,256]{1,0:T(8,128)(2,1)} %add_convert_fusion.1), channel_id=1, source_target_pairs={{0,2},{1,3},{2,0},{3,1},{4,6},{5,7},{6,4},{7,5},{8,10},{9,11},{10,... | collective-permute-start | bytes 1572872 | tf_op jit(solution)/shard_map/ppermute | solution.py:257
  34.2 4.3 %collective-permute-start.9 = (bf16[128,256]{1,0:T(8,128)(2,1)S(1)}, bf16[128,256]{1,0:T(8,128)(2,1)S(1)}, u32[]{:S(2)}, u32[]{:S(2)}) collective-permute-start(bf16[128,256]{1,0:T(8,128)(2,1)S(1)} %add_convert_fusion.4), channel_id=1, source_target_pairs={{0,8},{4,12},{8,0},{12,4},{16,24},{20,28},{24,16},{28,20},{1,9},{5... | collective-permute-start | bytes 196616 | tf_op jit(solution)/shard_map/ppermute | solution.py:260
  36.1 8.8 %collective-permute-start.7 = (bf16[1024,256]{1,0:T(8,128)(2,1)}, bf16[1024,256]{1,0:T(8,128)(2,1)S(1)}, u32[]{:S(2)}, u32[]{:S(2)}) collective-permute-start(bf16[1024,256]{1,0:T(8,128)(2,1)} %shard_map.101), channel_id=1, source_target_pairs={{0,1},{1,0},{2,3},{3,2},{4,5},{5,4},{6,7},{7,6},{8,9},{9,8},{10,11... | collective-permute-start | bytes 1572872 | tf_op jit(solution)/shard_map/ppermute | solution.py:257
  38.6 5.3 %collective-permute-start.10 = (bf16[128,256]{1,0:T(8,128)(2,1)S(1)}, bf16[128,256]{1,0:T(8,128)(2,1)S(1)}, u32[]{:S(2)}, u32[]{:S(2)}) collective-permute-start(bf16[128,256]{1,0:T(8,128)(2,1)S(1)} %add_convert_fusion.3), channel_id=1, source_target_pairs={{0,16},{4,20},{8,24},{12,28},{16,0},{20,4},{24,8},{28,12},{1,17},{... | collective-permute-start | bytes 196616 | tf_op jit(solution)/shard_map/ppermute | solution.py:260
  44.8 2.1 %collective-permute-start.11 = (bf16[128,256]{1,0:T(8,128)(2,1)S(1)}, bf16[128,256]{1,0:T(8,128)(2,1)S(1)}, u32[]{:S(2)}, u32[]{:S(2)}) collective-permute-start(bf16[128,256]{1,0:T(8,128)(2,1)S(1)} %add_convert_fusion.2), channel_id=1, source_target_pairs={{0,1},{1,0},{2,3},{3,2},{4,5},{5,4},{6,7},{7,6},{8,9},{9,8},{10,11... | collective-permute-start | bytes 196616 | tf_op jit(solution)/shard_map/ppermute | solution.py:257

commit v4 on v3

--- a/solution.py
+++ b/solution.py
@@ -8,7 +8,7 @@
 from jax.sharding import PartitionSpec as P
 
 TILE = 128
-UNROLL = 4
+UNROLL = 8
 F32 = jnp.float32
 BF16 = jnp.bfloat16
 
@@ -91,6 +91,47 @@
 
 def tie(x, *others):
     return lax.optimization_barrier((x, *others))[0]
+
+
+def join(*xs):
+    return lax.optimization_barrier(xs)
+
+
+def move(x):
+    def body(x_ref, out_ref, sem):
+        copy = pltpu.make_async_copy(x_ref, out_ref, sem)
+        copy.start()
+        copy.wait()
+
+    return pl.pallas_call(
+        body,
+        out_shape=jax.ShapeDtypeStruct(x.shape, x.dtype),
+        in_specs=[VMEM],
+        out_specs=pl.BlockSpec(memory_space=pl.ANY),
+        scratch_shapes=[pltpu.SemaphoreType.DMA],
+        cost_estimate=pl.CostEstimate(flops=0, bytes_accessed=1024, transcendentals=0),
+        compiler_params=params(4),
+    )(x)
+
+
+def add_rows(total, *parts):
+    shape = parts[0].shape
+
+    def body(*refs):
+        out_ref = refs[-1]
+        acc = refs[0][0:shape[0], :]
+        for ref in refs[1:-1]:
+            acc = acc + ref[...].astype(F32)
+        out_ref[...] = acc.astype(BF16)
+
+    return pl.pallas_call(
+        body,
+        out_shape=jax.ShapeDtypeStruct(shape, BF16),
+        in_specs=[VMEM] * (1 + len(parts)),
+        out_specs=VMEM,
+        cost_estimate=pl.CostEstimate(flops=0, bytes_accessed=1024, transcendentals=0),
+        compiler_params=params(8),
+    )(total, *parts)
 
 
 def forward_groups(list_ref, bounds, tiles_ref, x_ref, acc):
@@ -145,15 +186,14 @@
     if final:
         w_ref, cot_ref, core_ref, act_ref, sw_ref, keep_ref, send_ref, acc, wg = refs
     else:
-        acc_out, acc = refs
+        (acc,) = refs
     if first:
         acc[...] = jnp.zeros_like(acc)
     else:
-        acc[0:blocks_dev] = acc_in[...]
+        acc[0:blocks_dev] = acc_in[0:blocks_dev]
     for k, x_ref in zip(phases, xs):
         forward_groups(list_ref, plan.bounds(list_ref, k, k + 1), tiles_ref, x_ref, acc)
     if not final:
-        acc_out[...] = acc[0:blocks_dev]
         return
     hid = w_ref.shape[0]
     w = w_ref[...]
@@ -163,7 +203,7 @@
         at = slice(b * TILE, b * TILE + n)
         agg = acc[b:b + step_blocks].reshape(n, hid).astype(BF16)
         pre = jnp.dot(agg, w, preferred_element_type=F32)
-        sig = jax.nn.sigmoid(pre)
+        sig = 0.5 + 0.5 * jnp.tanh(0.5 * pre)
         act_ref[at, :] = (pre * sig).astype(BF16)
         slope = (cot_ref[at, :].astype(F32) * sig * (1.0 + pre * (1.0 - sig))).astype(BF16)
         sw_ref[at, :] = lax.dot_general(
@@ -186,12 +226,13 @@
     first, final = acc is None, tail is not None
     args = [lst, tiles, *xs] + ([] if first else [acc])
     specs = [SMEM] + [VMEM] * (len(args) - 1)
-    scratch = [pltpu.VMEM((blocks_dev + 1, TILE, hid), F32)]
+    scratch = []
     if final:
+        scratch.append(pltpu.VMEM((blocks_dev + 1, TILE, hid), F32))
         args += list(tail)
         specs += [VMEM, VMEM, SMEM]
         out = (
-            jax.ShapeDtypeStruct((blocks_dev * TILE, hid), BF16),
+            pltpu.VMEM((blocks_dev * TILE, hid), BF16),
             jax.ShapeDtypeStruct((blocks_dev * TILE, hid), BF16),
             jax.ShapeDtypeStruct((hid // 2, hid), F32),
             jax.ShapeDtypeStruct((hid // 2, hid), F32),
@@ -199,7 +240,7 @@
         out_specs = (VMEM,) * 4
         scratch.append(pltpu.VMEM((hid, hid), F32))
     else:
-        out = jax.ShapeDtypeStruct((blocks_dev, TILE, hid), F32)
+        out = jax.ShapeDtypeStruct((blocks_dev + 1, TILE, hid), F32)
         out_specs = VMEM
 
     def body(*refs):
@@ -215,37 +256,32 @@
     )(*args)
 
 
-def backward(plan, sources, blocks, extra=None, dtype=BF16, us=0):
-    hid = sources[0][3].shape[1]
-    args = [part for source in sources for part in source[1:]]
-    specs = [SMEM, VMEM, VMEM] * len(sources)
-    if extra is not None:
-        args.append(extra)
-        specs.append(VMEM)
-
-    def body(*refs):
-        out_ref, acc = refs[-2:]
-        if extra is None:
-            acc[...] = jnp.zeros_like(acc)
-        else:
-            acc[0:blocks] = refs[-3][...].astype(F32).reshape(blocks, TILE, hid)
-        for i, source in enumerate(sources):
-            list_ref, tiles_ref, s_ref = refs[3 * i:3 * i + 3]
-            bounds = plan.bounds(list_ref, source[0], source[0] + 1)
-            backward_groups(list_ref, bounds, tiles_ref, s_ref, acc)
-        out_ref[...] = acc[0:blocks].reshape(blocks * TILE, hid).astype(dtype)
-
-    return pl.pallas_call(
+def backward(plan, lst, rel, tiles, s, blocks, rounded=True, us=0):
+    hid = s.shape[1]
+
+    def body(list_ref, tiles_ref, s_ref, out_ref, acc=None):
+        acc = acc if rounded else out_ref
+        acc[...] = jnp.zeros_like(acc)
+        bounds = plan.bounds(list_ref, rel, rel + 1)
+        backward_groups(list_ref, bounds, tiles_ref, s_ref, acc)
+        if rounded:
+            out_ref[...] = acc[0:blocks].reshape(blocks * TILE, hid).astype(BF16)
+
+    shape = (blocks + 1, TILE, hid)
+    out = pl.pallas_call(
         body,
-        out_shape=jax.ShapeDtypeStruct((blocks * TILE, hid), dtype),
-        in_specs=specs,
+        out_shape=jax.ShapeDtypeStruct(
+            (blocks * TILE, hid) if rounded else shape, BF16 if rounded else F32
+        ),
+        in_specs=[SMEM, VMEM, VMEM],
         out_specs=VMEM,
-        scratch_shapes=[pltpu.VMEM((blocks + 1, TILE, hid), F32)],
+        scratch_shapes=[pltpu.VMEM(shape, F32)] if rounded else [],
         compiler_params=params(40 if blocks > 8 else 12),
         cost_estimate=pl.CostEstimate(
             flops=int(us * 1.1e9), bytes_accessed=1024, transcendentals=0
         ),
-    )(*args)
+    )(lst, tiles, s)
+    return out if rounded else out.reshape(-1, hid)
 
 
 def local_four(features, weight, cotangent, tiles, tile_rows, tile_cols, tile_counts):
@@ -267,32 +303,34 @@
     plan = Plan(tile_rows.shape[0], 4, blocks_dev)
     lst = prepare(plan, blocks_dev, me, [tile_counts, tile_rows, tile_cols])
     acc = forward(plan, lst, tiles, [features, sib], [0, 1])
-    far = tie(far, acc)
+    far, acc = join(far, acc)
     diag = swap(far, 1)
     acc = forward(plan, lst, tiles, [far], [2], acc)
     activated, sw, keep, send = forward(
         plan, lst, tiles, [diag], [3], acc, (weight, cotangent, core.reshape(1))
     )
 
-    def part(rel, sw, extra=None, dtype=BF16, us=0):
-        return backward(plan, [(rel, lst, tiles, sw)], blocks_dev, extra, dtype, us)
+    def part(rel, sw, rounded=True, us=0):
+        return backward(plan, lst, rel, tiles, sw, blocks_dev, rounded, us)
 
     send = swap(send, 1)
     p3 = part(3, sw)
     r3 = swap(p3, 1)
     w = (keep + send).astype(BF16)
-    q = part(2, tie(sw, w), None, F32, 10)
-    q = (q + r3.astype(F32)).astype(BF16)
+    q = part(2, tie(sw, w), False, 10)
+    q = add_rows(q, r3)
     q_far = swap(q, 2)
     w = fold(w, "grp", 4, 2, q)
-    p0 = part(0, tie(sw, w), None, F32)
+    p0 = part(0, tie(sw, w), False)
     w = fold(w, "row", 8, 1, p0)
     p1 = part(1, tie(sw, w))
     r1 = swap(p1, 1)
     w = fold(w, "row", 8, 2, p1)
-    w = fold(w, "row", 8, 4, q_far)
-    feature_grad = (p0 + r1.astype(F32) + q_far.astype(F32)).astype(BF16)
-    other = tie(swap(w, 1), feature_grad)
+    activated = move(tie(activated, w))
+    w = fold(w, "row", 8, 4, activated, q_far)
+    feature_grad = add_rows(p0, r1, q_far)
+    w = tie(w, feature_grad)
+    other = swap(w, 1)
     weight_grad = jnp.where(
         core == 0, jnp.concatenate([w, other]), jnp.concatenate([other, w])
     ).astype(F32)
@@ -310,7 +348,7 @@
     activated, sw, keep, send = forward(
         plan, lst, tiles, [panel], [0], None, (weight, cotangent, jnp.zeros((1,), jnp.int32))
     )
-    partial = backward(plan, [(0, lst, tiles, sw)], group_blocks)
+    partial = backward(plan, lst, 0, tiles, sw, group_blocks)
     feature_grad = lax.psum_scatter(partial, "grp", scatter_dimension=0, tiled=True)
     weight_grad = lax.psum(jnp.concatenate([keep, send]), ("row", "grp"))
     return activated, feature_grad, weight_grad

time: 48.1 us -> 45.5 us (0.946)
  Pallas kernels: 12.7 us -> 17.6 us
  waiting for transfers between devices: 11.7 us -> 8.3 us
  other arithmetic: 3.79 us -> 0.81 us
  starting transfers between devices: 12.8 us -> 11.9 us
    convert_element_type x2 -> x0, other arithmetic: 2.97 us -> none  [the longest x1 1.99 us: local_four(): feature_grad = (p0 + r1.astype(F32) + q_far.astype(F32)).astype(BF16)]
    pallas_call x4 -> x7, Pallas kernels: 5.11 us -> 7.83 us  [the longest x4 5.99 us: backward(): pl.pallas_call(body, out_shape=jax.ShapeDtypeStruct((blocks * TILE, hid)...]
    ppermute x8, waiting for transfers between devices: 5.62 us -> 3.78 us  [swap(): return lax.ppermute(x, 'grp', [(i, i ^ bit) for i in range(4)])]
    ppermute x4, waiting for transfers between devices: 6.08 us -> 4.53 us  [fold(): other = lax.ppermute(w, axis, [(i, i ^ bit) for i in range(size)])]
    pallas_call x1, Pallas kernels: 1.59 us -> 2.82 us  [prepare(): pl.pallas_call(functools.partial(prep_body, plan, pad_col), out_shape=jax...]
    pallas_call x3, Pallas kernels: 6.01 us -> 6.9 us  [forward(): pl.pallas_call(body, out_shape=out, in_specs=specs, out_specs=out_specs,...]
    ppermute x4, starting transfers between devices: 7.57 us -> 6.94 us  [fold(): other = lax.ppermute(w, axis, [(i, i ^ bit) for i in range(size)])]
  transfers between devices with their start and end apart: 12 -> 12, of which waited for: 7 -> 6; matrix products, arithmetic and copies ran while one was open for 6% -> 0% of each run, Pallas kernels for 20% -> 30%
where the time goes in v4:
time: 45.5 us; the launch traced here: 45.2 us
  Pallas kernels  17.6 us (39%)
  starting transfers between devices  11.9 us (26%)
  waiting for transfers between devices  8.3 us (18%)
  local copies, waits for them, and re-layouts  5.14 us (11%)
  between operations  1.46 us (3%)
  other arithmetic  0.81 us (2%)
    ppermute x4, starting transfers between devices, fold(): other = lax.ppermute(w, axis, [(i, i ^ bit) for i in range(size)])  6.94 us
    pallas_call x3, Pallas kernels, forward(): pl.pallas_call(body, out_shape=out, in_specs=specs, out_specs=out_specs,...  6.9 us
    pallas_call x4, Pallas kernels, backward(): pl.pallas_call(body, out_shape=jax.ShapeDtypeStruct((blocks * TILE, hid)...  5.99 us
    unnamed x18, local copies, waits for them, and re-layouts  5.14 us
    ppermute x8, starting transfers between devices, swap(): return lax.ppermute(x, 'grp', [(i, i ^ bit) for i in range(4)])  5 us
    ppermute x4, waiting for transfers between devices, fold(): other = lax.ppermute(w, axis, [(i, i ^ bit) for i in range(size)])  4.53 us
    ppermute x8, waiting for transfers between devices, swap(): return lax.ppermute(x, 'grp', [(i, i ^ bit) for i in range(4)])  3.78 us
    pallas_call x1, Pallas kernels, prepare(): pl.pallas_call(functools.partial(prep_body, plan, pad_col), out_shape=jax...  2.82 us
  transfers between devices with their start and end apart: 12, of which 6 were waited for; matrix products, arithmetic and copies ran while one was open for 0% of the time, Pallas kernels for 30%

profile of v4, /device:TPU:0, one launch (start us, length us, event | category | flops | bytes accessed | tf_op | source)
XLA Modules:
  0.0 45.2 jit_solution(4435075490019134432)
XLA Ops:
  0.6 0.5 %collective-permute-start.1 = (bf16[1024,256]{1,0:T(8,128)(2,1)}, bf16[1024,256]{1,0:T(8,128)(2,1)S(1)}, u32[]{:S(2)}, u32[]{:S(2)}) collective-permute-start(bf16[1024,256]{1,0:T(8,128)(2,1)} %refs_2_.1), channel_id=1, source_target_pairs={{0,1},{1,0},{2,3},{3,2},{4,5},{5,4},{6,7},{7,6},{8,9},{9,8},{10,11... | collective-permute-start | bytes 1572872 | tf_op jit(solution)/shard_map/ppermute | solution.py:293
  1.1 2.6 %collective-permute-start = (bf16[1024,256]{1,0:T(8,128)(2,1)}, bf16[1024,256]{1,0:T(8,128)(2,1)}, u32[]{:S(2)}, u32[]{:S(2)}) collective-permute-start(bf16[1024,256]{1,0:T(8,128)(2,1)} %refs_2_.1), channel_id=1, source_target_pairs={{0,2},{1,3},{2,0},{3,1},{4,6},{5,7},{6,4},{7,5},{8,10},{9,11},{10,... | collective-permute-start | bytes 1572872 | tf_op jit(solution)/shard_map/ppermute | solution.py:293
  4.4 2.8 %shard_map.94.refs_0_.list_ref = s32[101]{0:T(128)} custom-call(s32[1]{0:T(128)} %bitcast.me_ref, s32[1]{0:T(128)S(6)} %copy.10.cnt_ref, s32[64]{0:T(128)} %rows_ref.1, s32[64]{0:T(128)} %cols_ref.1), custom_call_target="tpu_custom_call" | custom-call | tf_op jit(solution)/shard_map/pallas_call | solution.py:68
  7.2 0.0 collective-permute-done.1.refs_3_
  7.2 0.0 copy-start.4
  7.2 0.8 %copy-done.4 = bf16[1024,256]{1,0:T(8,128)(2,1)} copy-done((bf16[1024,256]{1,0:T(8,128)(2,1)}, bf16[1024,256]{1,0:T(8,128)(2,1)S(1)}, u32[]{:S(2)}) %copy-start.4) | copy-done | bytes 524312
  8.0 0.0 copy-start
  8.0 1.6 %copy-done = bf16[64,128,128]{2,1,0:T(8,128)(2,1)S(1)} copy-done((bf16[64,128,128]{2,1,0:T(8,128)(2,1)S(1)}, bf16[64,128,128]{2,1,0:T(8,128)(2,1)}, u32[]{:S(2)}) %copy-start) | copy-done | bytes 2097176
  9.6 0.0 copy-start.2
  9.6 1.0 %copy-done.2 = bf16[1024,256]{1,0:T(8,128)(2,1)S(1)} copy-done((bf16[1024,256]{1,0:T(8,128)(2,1)S(1)}, bf16[1024,256]{1,0:T(8,128)(2,1)}, u32[]{:S(2)}) %copy-start.2) | copy-done | bytes 524312
  10.7 0.0 copy-start.5
  10.7 1.0 %copy-done.5 = bf16[1024,256]{1,0:T(8,128)(2,1)S(1)} copy-done((bf16[1024,256]{1,0:T(8,128)(2,1)S(1)}, bf16[1024,256]{1,0:T(8,128)(2,1)}, u32[]{:S(2)}) %copy-start.5) | copy-done | bytes 524312
  11.7 0.0 copy-start.7
  11.7 0.7 %copy-done.7 = s32[101]{0:T(128)S(1)} copy-done((s32[101]{0:T(128)S(1)}, s32[101]{0:T(128)}, u32[]{:S(2)}) %copy-start.7) | copy-done | bytes 428
  12.4 0.0 copy-start.1
  12.4 0.0 copy-start.8
  12.4 2.1 %shard_map.95.refs_3_ = f32[9,128,256]{2,1,0:T(8,128)S(1)} custom-call(s32[101]{0:T(128)S(1)} %copy-done.7, bf16[64,128,128]{2,1,0:T(8,128)(2,1)S(1)} %copy-done, bf16[1024,256]{1,0:T(8,128)(2,1)S(1)} %copy-done.2, bf16[1024,256]{1,0:T(8,128)(2,1)S(1)} %copy-done.5), custom_call_target="tpu_custom_call" | custom-call | tf_op jit(solution)/shard_map/pallas_call | solution.py:249
  14.5 2.1 %collective-permute-done.refs_2_ = bf16[1024,256]{1,0:T(8,128)(2,1)} collective-permute-done((bf16[1024,256]{1,0:T(8,128)(2,1)}, bf16[1024,256]{1,0:T(8,128)(2,1)}, u32[]{:S(2)}, u32[]{:S(2)}) %collective-permute-start) | collective-permute-done | bytes 524320 | tf_op jit(solution)/shard_map/ppermute | solution.py:293
  16.6 0.0 collective-permute-start.2
  16.6 0.0 copy-done.1
  16.6 0.0 copy-done.8
  16.6 0.0 copy-start.3
  16.6 0.0 copy-start.6
  16.6 1.8 %shard_map.96.refs_3_ = f32[9,128,256]{2,1,0:T(8,128)S(1)} custom-call(s32[101]{0:T(128)S(1)} %copy-done.8, bf16[64,128,128]{2,1,0:T(8,128)(2,1)S(1)} %copy-done.1, bf16[1024,256]{1,0:T(8,128)(2,1)} %collective-permute-done.refs_2_, f32[9,128,256]{2,1,0:T(8,128)S(1)} %shard_map.95.refs_3_), custom_call_target="tpu_custom_call" | custom-call | tf_op jit(solution)/shard_map/pallas_call | solution.py:249
  18.4 0.4 collective-permute-done.2.refs_2_
  18.8 0.0 copy-done.3
  18.8 0.0 copy-done.6
  18.8 3.0 %shard_map.97 = (bf16[1024,256]{1,0:T(8,128)(2,1)S(1)}, bf16[1024,256]{1,0:T(8,128)(2,1)S(1)}, f32[128,256]{1,0:T(8,128)S(1)}, f32[128,256]{1,0:T(8,128)S(1)}) custom-call(s32[101]{0:T(128)S(1)} %copy-done.8, bf16[64,128,128]{2,1,0:T(8,128)(2,1)S(1)} %copy-done.1, bf16[1024,256]{1,0:T(8,128)(2,1)} %collective-permute-done.2.refs_2_, ...), custom_call_target="tpu_custom_call" | custom-call | tf_op jit(solution)/shard_map/pallas_call | solution.py:249
  21.8 0.1 collective-permute-start.3
  21.9 1.7 %shard_map.99 = bf16[1024,256]{1,0:T(8,128)(2,1)S(1)} custom-call(s32[101]{0:T(128)S(1)} %copy-done.8, bf16[64,128,128]{2,1,0:T(8,128)(2,1)S(1)} %copy-done.1, bf16[1024,256]{1,0:T(8,128)(2,1)S(1)} %get-tuple-element.28.s_ref), custom_call_target="tpu_custom_call" | custom-call | bytes 1024 | tf_op jit(solution)/shard_map/pallas_call | solution.py:271
  23.6 0.2 collective-permute-start.5
  23.8 0.0 collective-permute-done.3
  23.9 0.9 %collective-permute-start.4 = (bf16[128,256]{1,0:T(8,128)(2,1)S(1)}, bf16[128,256]{1,0:T(8,128)(2,1)S(1)}, u32[]{:S(2)}, u32[]{:S(2)}) collective-permute-start(bf16[128,256]{1,0:T(8,128)(2,1)S(1)} %add_convert_fusion.4), channel_id=1, source_target_pairs={{0,2},{1,3},{2,0},{3,1},{4,6},{5,7},{6,4},{7,5},{8,10},{9,11},{10,... | collective-permute-start | bytes 196616 | tf_op jit(solution)/shard_map/ppermute | solution.py:296
  24.8 1.3 %shard_map.98 = f32[9,128,256]{2,1,0:T(8,128)S(1)} custom-call(s32[101]{0:T(128)S(1)} %copy-done.8, bf16[64,128,128]{2,1,0:T(8,128)(2,1)S(1)} %copy-done.1, bf16[1024,256]{1,0:T(8,128)(2,1)S(1)} %get-tuple-element.28.s_ref), custom_call_target="tpu_custom_call" | custom-call | flops 11000000512 | bytes 1024 | tf_op jit(solution)/shard_map/pallas_call | solution.py:271
  26.1 0.0 collective-permute-done.5.refs_1_
  26.1 0.1 shard_map.100
  26.2 2.1 %collective-permute-done.4 = bf16[128,256]{1,0:T(8,128)(2,1)S(1)} collective-permute-done((bf16[128,256]{1,0:T(8,128)(2,1)S(1)}, bf16[128,256]{1,0:T(8,128)(2,1)S(1)}, u32[]{:S(2)}, u32[]{:S(2)}) %collective-permute-start.4) | collective-permute-done | bytes 65568 | tf_op jit(solution)/shard_map/ppermute | solution.py:296
  28.3 1.1 %collective-permute-start.6 = (bf16[128,256]{1,0:T(8,128)(2,1)S(1)}, bf16[128,256]{1,0:T(8,128)(2,1)S(1)}, u32[]{:S(2)}, u32[]{:S(2)}) collective-permute-start(bf16[128,256]{1,0:T(8,128)(2,1)S(1)} %add_convert_fusion.3), channel_id=1, source_target_pairs={{0,4},{4,0},{8,12},{12,8},{16,20},{20,16},{24,28},{28,24},{1,5},{5... | collective-permute-start | bytes 196616 | tf_op jit(solution)/shard_map/ppermute | solution.py:296
  29.4 1.5 %collective-permute-start.9 = (bf16[1024,256]{1,0:T(8,128)(2,1)S(1)}, bf16[1024,256]{1,0:T(8,128)(2,1)S(1)}, u32[]{:S(2)}, u32[]{:S(2)}) collective-permute-start(bf16[1024,256]{1,0:T(8,128)(2,1)S(1)} %shard_map.100), channel_id=1, source_target_pairs={{0,2},{1,3},{2,0},{3,1},{4,6},{5,7},{6,4},{7,5},{8,10},{9,11},{10,... | collective-permute-start | bytes 1572872 | tf_op jit(solution)/shard_map/ppermute | solution.py:293
  30.9 1.7 %shard_map.101 = f32[9,128,256]{2,1,0:T(8,128)S(1)} custom-call(s32[101]{0:T(128)S(1)} %copy-done.8, bf16[64,128,128]{2,1,0:T(8,128)(2,1)S(1)} %copy-done.1, bf16[1024,256]{1,0:T(8,128)(2,1)S(1)} %get-tuple-element.28.s_ref), custom_call_target="tpu_custom_call" | custom-call | bytes 1024 | tf_op jit(solution)/shard_map/pallas_call | solution.py:271
  32.6 0.0 collective-permute-done.6
  32.7 2.0 %collective-permute-start.7 = (bf16[128,256]{1,0:T(8,128)(2,1)S(1)}, bf16[128,256]{1,0:T(8,128)(2,1)S(1)}, u32[]{:S(2)}, u32[]{:S(2)}) collective-permute-start(bf16[128,256]{1,0:T(8,128)(2,1)S(1)} %add_convert_fusion.2), channel_id=1, source_target_pairs={{0,8},{4,12},{8,0},{12,4},{16,24},{20,28},{24,16},{28,20},{1,9},{5... | collective-permute-start | bytes 196616 | tf_op jit(solution)/shard_map/ppermute | solution.py:296
  34.6 1.4 %shard_map.102 = bf16[1024,256]{1,0:T(8,128)(2,1)S(1)} custom-call(s32[101]{0:T(128)S(1)} %copy-done.8, bf16[64,128,128]{2,1,0:T(8,128)(2,1)S(1)} %copy-done.1, bf16[1024,256]{1,0:T(8,128)(2,1)S(1)} %get-tuple-element.28.s_ref), custom_call_target="tpu_custom_call" | custom-call | bytes 1024 | tf_op jit(solution)/shard_map/pallas_call | solution.py:271
  36.0 0.1 collective-permute-start.8
  36.0 0.9 %collective-permute-done.7 = bf16[128,256]{1,0:T(8,128)(2,1)S(1)} collective-permute-done((bf16[128,256]{1,0:T(8,128)(2,1)S(1)}, bf16[128,256]{1,0:T(8,128)(2,1)S(1)}, u32[]{:S(2)}, u32[]{:S(2)}) %collective-permute-start.7) | collective-permute-done | bytes 65568 | tf_op jit(solution)/shard_map/ppermute | solution.py:296
  37.0 3.0 %collective-permute-start.10 = (bf16[128,256]{1,0:T(8,128)(2,1)S(1)}, bf16[128,256]{1,0:T(8,128)(2,1)S(1)}, u32[]{:S(2)}, u32[]{:S(2)}) collective-permute-start(bf16[128,256]{1,0:T(8,128)(2,1)S(1)} %add_convert_fusion.1), channel_id=1, source_target_pairs={{0,16},{4,20},{8,24},{12,28},{16,0},{20,4},{24,8},{28,12},{1,17},{... | collective-permute-start | bytes 196616 | tf_op jit(solution)/shard_map/ppermute | solution.py:296
  40.0 0.8 %shard_map.103 = bf16[1024,256]{1,0:T(8,128)(2,1)} custom-call(bf16[1024,256]{1,0:T(8,128)(2,1)S(1)} %get-tuple-element.30.x_ref), custom_call_target="tpu_custom_call" | custom-call | bytes 1024 | tf_op jit(solution)/shard_map/pallas_call | solution.py:106
  40.8 1.5 %collective-permute-done.10 = bf16[128,256]{1,0:T(8,128)(2,1)S(1)} collective-permute-done((bf16[128,256]{1,0:T(8,128)(2,1)S(1)}, bf16[128,256]{1,0:T(8,128)(2,1)S(1)}, u32[]{:S(2)}, u32[]{:S(2)}) %collective-permute-start.10) | collective-permute-done | bytes 65568 | tf_op jit(solution)/shard_map/ppermute | solution.py:296
  42.2 0.0 collective-permute-done.9.refs_2_
  42.3 0.0 collective-permute-done.8.refs_1_
  42.3 0.9 %shard_map.104 = bf16[1024,256]{1,0:T(8,128)(2,1)} custom-call(f32[1152,256]{1,0:T(8,128)S(1)} %bitcast.4, bf16[1024,256]{1,0:T(8,128)(2,1)S(1)} %collective-permute-done.8.refs_1_, bf16[1024,256]{1,0:T(8,128)(2,1)S(1)} %collective-permute-done.9.refs_2_), custom_call_target="tpu_custom_call" | custom-call | bytes 1024 | tf_op jit(solution)/shard_map/pallas_call | solution.py:127
  43.2 0.0 collective-permute-start.11
  43.2 1.3 %collective-permute-done.11 = bf16[128,256]{1,0:T(8,128)(2,1)S(1)} collective-permute-done((bf16[128,256]{1,0:T(8,128)(2,1)S(1)}, bf16[128,256]{1,0:T(8,128)(2,1)S(1)}, u32[]{:S(2)}, u32[]{:S(2)}) %collective-permute-start.11) | collective-permute-done | bytes 65568 | tf_op jit(solution)/shard_map/ppermute | solution.py:293
  44.5 0.7 %fusion = f32[256,256]{1,0:T(8,128)} fusion(bf16[128,256]{1,0:T(8,128)(2,1)S(1)} %collective-permute-done.11, bf16[128,256]{1,0:T(8,128)(2,1)S(1)} %add_convert_fusion, pred[]{:T(512)S(6)} %eq.3), kind=kLoop, calls=%fused_computation.1 | loop fusion | flops 655360 | bytes 393217 | tf_op jit(solution)/shard_map/convert_element_type | solution.py:336
  (5 shorter events, 0.1 us)
Async XLA Ops:
  0.6 6.6 %collective-permute-start.1 = (bf16[1024,256]{1,0:T(8,128)(2,1)}, bf16[1024,256]{1,0:T(8,128)(2,1)S(1)}, u32[]{:S(2)}, u32[]{:S(2)}) collective-permute-start(bf16[1024,256]{1,0:T(8,128)(2,1)} %refs_2_.1), channel_id=1, source_target_pairs={{0,1},{1,0},{2,3},{3,2},{4,5},{5,4},{6,7},{7,6},{8,9},{9,8},{10,11... | collective-permute-start | bytes 1572872 | tf_op jit(solution)/shard_map/ppermute | solution.py:293
  1.1 15.4 %collective-permute-start = (bf16[1024,256]{1,0:T(8,128)(2,1)}, bf16[1024,256]{1,0:T(8,128)(2,1)}, u32[]{:S(2)}, u32[]{:S(2)}) collective-permute-start(bf16[1024,256]{1,0:T(8,128)(2,1)} %refs_2_.1), channel_id=1, source_target_pairs={{0,2},{1,3},{2,0},{3,1},{4,6},{5,7},{6,4},{7,5},{8,10},{9,11},{10,... | collective-permute-start | bytes 1572872 | tf_op jit(solution)/shard_map/ppermute | solution.py:293
  7.2 0.8 %copy-start.4 = (bf16[1024,256]{1,0:T(8,128)(2,1)}, bf16[1024,256]{1,0:T(8,128)(2,1)S(1)}, u32[]{:S(2)}) copy-start(bf16[1024,256]{1,0:T(8,128)(2,1)S(1)} %collective-permute-done.1.refs_3_) | copy-start | bytes 1572868
  8.0 1.6 %copy-start = (bf16[64,128,128]{2,1,0:T(8,128)(2,1)S(1)}, bf16[64,128,128]{2,1,0:T(8,128)(2,1)}, u32[]{:S(2)}) copy-start(bf16[64,128,128]{2,1,0:T(8,128)(2,1)} %tiles_ref.7) | copy-start | bytes 6291460
  9.6 1.0 %copy-start.2 = (bf16[1024,256]{1,0:T(8,128)(2,1)S(1)}, bf16[1024,256]{1,0:T(8,128)(2,1)}, u32[]{:S(2)}) copy-start(bf16[1024,256]{1,0:T(8,128)(2,1)} %refs_2_.1) | copy-start | bytes 1572868
  10.7 1.0 %copy-start.5 = (bf16[1024,256]{1,0:T(8,128)(2,1)S(1)}, bf16[1024,256]{1,0:T(8,128)(2,1)}, u32[]{:S(2)}) copy-start(bf16[1024,256]{1,0:T(8,128)(2,1)} %copy-done.4) | copy-start | bytes 1572868
  11.7 0.7 %copy-start.7 = (s32[101]{0:T(128)S(1)}, s32[101]{0:T(128)}, u32[]{:S(2)}) copy-start(s32[101]{0:T(128)} %shard_map.94.refs_0_.list_ref) | copy-start | bytes 1216
  12.4 4.2 %copy-start.1 = (bf16[64,128,128]{2,1,0:T(8,128)(2,1)S(1)}, bf16[64,128,128]{2,1,0:T(8,128)(2,1)}, u32[]{:S(2)}) copy-start(bf16[64,128,128]{2,1,0:T(8,128)(2,1)} %tiles_ref.7) | copy-start | bytes 6291460
  12.4 4.2 %copy-start.8 = (s32[101]{0:T(128)S(1)}, s32[101]{0:T(128)}, u32[]{:S(2)}) copy-start(s32[101]{0:T(128)} %shard_map.94.refs_0_.list_ref) | copy-start | bytes 1216
  16.6 2.3 %collective-permute-start.2 = (bf16[1024,256]{1,0:T(8,128)(2,1)}, bf16[1024,256]{1,0:T(8,128)(2,1)}, u32[]{:S(2)}, u32[]{:S(2)}) collective-permute-start(bf16[1024,256]{1,0:T(8,128)(2,1)} %collective-permute-done.refs_2_), channel_id=1, source_target_pairs={{0,1},{1,0},{2,3},{3,2},{4,5},{5,4},{6,7},{7,6},{8,9},{9,8},{10,11... | collective-permute-start | bytes 1572872 | tf_op jit(solution)/shard_map/ppermute | solution.py:293
  16.6 2.2 %copy-start.3 = (bf16[1024,256]{1,0:T(8,128)(2,1)S(1)}, bf16[1024,256]{1,0:T(8,128)(2,1)}, u32[]{:S(2)}) copy-start(bf16[1024,256]{1,0:T(8,128)(2,1)} %refs_5_.1) | copy-start | bytes 1572868
  16.6 2.2 %copy-start.6 = (bf16[256,256]{1,0:T(8,128)(2,1)S(1)}, bf16[256,256]{1,0:T(8,128)(2,1)}, u32[]{:S(2)}) copy-start(bf16[256,256]{1,0:T(8,128)(2,1)} %refs_4_.1) | copy-start | bytes 393220
  21.8 2.0 %collective-permute-start.3 = (f32[128,256]{1,0:T(8,128)S(1)}, f32[128,256]{1,0:T(8,128)S(1)}, u32[]{:S(2)}, u32[]{:S(2)}) collective-permute-start(f32[128,256]{1,0:T(8,128)S(1)} %get-tuple-element.22), channel_id=1, source_target_pairs={{0,1},{1,0},{2,3},{3,2},{4,5},{5,4},{6,7},{7,6},{8,9},{9,8},{10,11... | collective-permute-start | bytes 393224 | tf_op jit(solution)/shard_map/ppermute | solution.py:293
  23.6 2.5 %collective-permute-start.5 = (bf16[1024,256]{1,0:T(8,128)(2,1)S(1)}, bf16[1024,256]{1,0:T(8,128)(2,1)S(1)}, u32[]{:S(2)}, u32[]{:S(2)}) collective-permute-start(bf16[1024,256]{1,0:T(8,128)(2,1)S(1)} %shard_map.99), channel_id=1, source_target_pairs={{0,1},{1,0},{2,3},{3,2},{4,5},{5,4},{6,7},{7,6},{8,9},{9,8},{10,11... | collective-permute-start | bytes 1572872 | tf_op jit(solution)/shard_map/ppermute | solution.py:293
  23.9 4.4 %collective-permute-start.4 = (bf16[128,256]{1,0:T(8,128)(2,1)S(1)}, bf16[128,256]{1,0:T(8,128)(2,1)S(1)}, u32[]{:S(2)}, u32[]{:S(2)}) collective-permute-start(bf16[128,256]{1,0:T(8,128)(2,1)S(1)} %add_convert_fusion.4), channel_id=1, source_target_pairs={{0,2},{1,3},{2,0},{3,1},{4,6},{5,7},{6,4},{7,5},{8,10},{9,11},{10,... | collective-permute-start | bytes 196616 | tf_op jit(solution)/shard_map/ppermute | solution.py:296
  28.3 4.3 %collective-permute-start.6 = (bf16[128,256]{1,0:T(8,128)(2,1)S(1)}, bf16[128,256]{1,0:T(8,128)(2,1)S(1)}, u32[]{:S(2)}, u32[]{:S(2)}) collective-permute-start(bf16[128,256]{1,0:T(8,128)(2,1)S(1)} %add_convert_fusion.3), channel_id=1, source_target_pairs={{0,4},{4,0},{8,12},{12,8},{16,20},{20,16},{24,28},{28,24},{1,5},{5... | collective-permute-start | bytes 196616 | tf_op jit(solution)/shard_map/ppermute | solution.py:296
  29.4 12.8 %collective-permute-start.9 = (bf16[1024,256]{1,0:T(8,128)(2,1)S(1)}, bf16[1024,256]{1,0:T(8,128)(2,1)S(1)}, u32[]{:S(2)}, u32[]{:S(2)}) collective-permute-start(bf16[1024,256]{1,0:T(8,128)(2,1)S(1)} %shard_map.100), channel_id=1, source_target_pairs={{0,2},{1,3},{2,0},{3,1},{4,6},{5,7},{6,4},{7,5},{8,10},{9,11},{10,... | collective-permute-start | bytes 1572872 | tf_op jit(solution)/shard_map/ppermute | solution.py:293
  32.7 4.3 %collective-permute-start.7 = (bf16[128,256]{1,0:T(8,128)(2,1)S(1)}, bf16[128,256]{1,0:T(8,128)(2,1)S(1)}, u32[]{:S(2)}, u32[]{:S(2)}) collective-permute-start(bf16[128,256]{1,0:T(8,128)(2,1)S(1)} %add_convert_fusion.2), channel_id=1, source_target_pairs={{0,8},{4,12},{8,0},{12,4},{16,24},{20,28},{24,16},{28,20},{1,9},{5... | collective-permute-start | bytes 196616 | tf_op jit(solution)/shard_map/ppermute | solution.py:296
  36.0 6.3 %collective-permute-start.8 = (bf16[1024,256]{1,0:T(8,128)(2,1)S(1)}, bf16[1024,256]{1,0:T(8,128)(2,1)S(1)}, u32[]{:S(2)}, u32[]{:S(2)}) collective-permute-start(bf16[1024,256]{1,0:T(8,128)(2,1)S(1)} %shard_map.102), channel_id=1, source_target_pairs={{0,1},{1,0},{2,3},{3,2},{4,5},{5,4},{6,7},{7,6},{8,9},{9,8},{10,11... | collective-permute-start | bytes 1572872 | tf_op jit(solution)/shard_map/ppermute | solution.py:293
  37.0 5.2 %collective-permute-start.10 = (bf16[128,256]{1,0:T(8,128)(2,1)S(1)}, bf16[128,256]{1,0:T(8,128)(2,1)S(1)}, u32[]{:S(2)}, u32[]{:S(2)}) collective-permute-start(bf16[128,256]{1,0:T(8,128)(2,1)S(1)} %add_convert_fusion.1), channel_id=1, source_target_pairs={{0,16},{4,20},{8,24},{12,28},{16,0},{20,4},{24,8},{28,12},{1,17},{... | collective-permute-start | bytes 196616 | tf_op jit(solution)/shard_map/ppermute | solution.py:296
  43.2 1.3 %collective-permute-start.11 = (bf16[128,256]{1,0:T(8,128)(2,1)S(1)}, bf16[128,256]{1,0:T(8,128)(2,1)S(1)}, u32[]{:S(2)}, u32[]{:S(2)}) collective-permute-start(bf16[128,256]{1,0:T(8,128)(2,1)S(1)} %add_convert_fusion), channel_id=1, source_target_pairs={{0,1},{1,0},{2,3},{3,2},{4,5},{5,4},{6,7},{7,6},{8,9},{9,8},{10,11... | collective-permute-start | bytes 196616 | tf_op jit(solution)/shard_map/ppermute | solution.py:293

commit v5 on v4

--- a/solution.py
+++ b/solution.py
@@ -55,6 +55,7 @@
         for u in range(1, UNROLL):
             list_ref[lax.max(group * UNROLL - u, 0)] = pad
     list_ref[plan.length + cats] = group
+    list_ref[plan.length + cats + 1] = me if cats > 1 else 0
 
     def place(s, places):
         shift, local = category(cols_ref[s])
@@ -67,7 +68,7 @@
 def prepare(plan, pad_col, me, info):
     return pl.pallas_call(
         functools.partial(prep_body, plan, pad_col),
-        out_shape=jax.ShapeDtypeStruct((plan.length + plan.cats + 1,), jnp.int32),
+        out_shape=pltpu.SMEM((plan.length + plan.cats + 2,), jnp.int32),
         in_specs=[SMEM] * 4,
         out_specs=SMEM,
     )(me.reshape(1), *info)
@@ -184,7 +185,7 @@
     if not first:
         acc_in = refs.pop(0)
     if final:
-        w_ref, cot_ref, core_ref, act_ref, sw_ref, keep_ref, send_ref, acc, wg = refs
+        w_ref, cot_ref, act_ref, sw_ref, keep_ref, send_ref, acc, wg = refs
     else:
         (acc,) = refs
     if first:
@@ -197,7 +198,7 @@
         return
     hid = w_ref.shape[0]
     w = w_ref[...]
-    step_blocks = 4 if blocks_dev % 4 == 0 else 1
+    step_blocks = blocks_dev
     n = step_blocks * TILE
     for b in range(0, blocks_dev, step_blocks):
         at = slice(b * TILE, b * TILE + n)
@@ -215,7 +216,7 @@
         else:
             wg[...] += part
     rows = keep_ref.shape[0]
-    core = core_ref[0]
+    core = list_ref[plan.length + plan.cats + 1] & 1
     keep_ref[...] = wg[pl.ds(pl.multiple_of(core * rows, rows), rows), :]
     send_ref[...] = wg[pl.ds(pl.multiple_of((1 - core) * rows, rows), rows), :]
 
@@ -230,7 +231,7 @@
     if final:
         scratch.append(pltpu.VMEM((blocks_dev + 1, TILE, hid), F32))
         args += list(tail)
-        specs += [VMEM, VMEM, SMEM]
+        specs += [VMEM, VMEM]
         out = (
             pltpu.VMEM((blocks_dev * TILE, hid), BF16),
             jax.ShapeDtypeStruct((blocks_dev * TILE, hid), BF16),
@@ -307,7 +308,7 @@
     diag = swap(far, 1)
     acc = forward(plan, lst, tiles, [far], [2], acc)
     activated, sw, keep, send = forward(
-        plan, lst, tiles, [diag], [3], acc, (weight, cotangent, core.reshape(1))
+        plan, lst, tiles, [diag], [3], acc, (weight, cotangent)
     )
 
     def part(rel, sw, rounded=True, us=0):
@@ -321,15 +322,14 @@
     q = add_rows(q, r3)
     q_far = swap(q, 2)
     w = fold(w, "grp", 4, 2, q)
+    p1 = part(1, tie(sw, w))
+    w = fold(w, "row", 8, 1, p1)
+    r1 = swap(tie(p1, w), 1)
     p0 = part(0, tie(sw, w), False)
-    w = fold(w, "row", 8, 1, p0)
-    p1 = part(1, tie(sw, w))
-    r1 = swap(p1, 1)
-    w = fold(w, "row", 8, 2, p1)
+    w = fold(w, "row", 8, 2, p0)
     activated = move(tie(activated, w))
-    w = fold(w, "row", 8, 4, activated, q_far)
     feature_grad = add_rows(p0, r1, q_far)
-    w = tie(w, feature_grad)
+    w = fold(w, "row", 8, 4, activated, feature_grad)
     other = swap(w, 1)
     weight_grad = jnp.where(
         core == 0, jnp.concatenate([w, other]), jnp.concatenate([other, w])
@@ -346,7 +346,7 @@
     plan = Plan(tile_rows.shape[0], 1, blocks_dev)
     lst = prepare(plan, group_blocks, me, info)
     activated, sw, keep, send = forward(
-        plan, lst, tiles, [panel], [0], None, (weight, cotangent, jnp.zeros((1,), jnp.int32))
+        plan, lst, tiles, [panel], [0], None, (weight, cotangent)
     )
     partial = backward(plan, lst, 0, tiles, sw, group_blocks)
     feature_grad = lax.psum_scatter(partial, "grp", scatter_dimension=0, tiled=True)

time: 45.5 us -> 43.5 us (0.956)
  Pallas kernels: 17.6 us -> 7.73 us
  waiting for transfers between devices: 8.3 us -> 16.4 us
  starting transfers between devices: 11.9 us -> 14.6 us
  local copies, waits for them, and re-layouts: 5.14 us -> 2.64 us
    ppermute x8, waiting for transfers between devices: 3.78 us -> 11.7 us  [swap(): return lax.ppermute(x, 'grp', [(i, i ^ bit) for i in range(4)])]
    pallas_call x3, Pallas kernels: 6.9 us -> 2.62 us  [forward(): pl.pallas_call(body, out_shape=out, in_specs=specs, out_specs=out_specs,...]
    pallas_call x4, Pallas kernels: 5.99 us -> 2.08 us  [backward(): pl.pallas_call(body, out_shape=jax.ShapeDtypeStruct((blocks * TILE, hid)...]
    unnamed x18 -> x8, local copies, waits for them, and re-layouts: 5.14 us -> 2.64 us
    ppermute x4, starting transfers between devices: 6.94 us -> 9.09 us  [fold(): other = lax.ppermute(w, axis, [(i, i ^ bit) for i in range(size)])]
    pallas_call x1, Pallas kernels: 2.82 us -> 1.2 us  [prepare(): pl.pallas_call(functools.partial(prep_body, plan, pad_col), out_shape=plt...]
    ppermute x8, starting transfers between devices: 5 us -> 5.46 us  [swap(): return lax.ppermute(x, 'grp', [(i, i ^ bit) for i in range(4)])]
  transfers between devices with their start and end apart: 12 -> 12, of which waited for: 6 -> 8; matrix products, arithmetic and copies ran while one was open for 0% -> 0% of each run, Pallas kernels for 30% -> 15%
where the time goes in v5:
time: 43.5 us; the launch traced here: 43.6 us
  waiting for transfers between devices  16.4 us (38%)
  starting transfers between devices  14.6 us (34%)
  Pallas kernels  7.73 us (18%)
  local copies, waits for them, and re-layouts  2.64 us (6%)
  between operations  1.45 us (3%)
  other arithmetic  0.81 us (2%)
    ppermute x8, waiting for transfers between devices, swap(): return lax.ppermute(x, 'grp', [(i, i ^ bit) for i in range(4)])  11.7 us
    ppermute x4, starting transfers between devices, fold(): other = lax.ppermute(w, axis, [(i, i ^ bit) for i in range(size)])  9.09 us
    ppermute x8, starting transfers between devices, swap(): return lax.ppermute(x, 'grp', [(i, i ^ bit) for i in range(4)])  5.46 us
    ppermute x4, waiting for transfers between devices, fold(): other = lax.ppermute(w, axis, [(i, i ^ bit) for i in range(size)])  4.64 us
    unnamed x8, local copies, waits for them, and re-layouts  2.64 us
    pallas_call x3, Pallas kernels, forward(): pl.pallas_call(body, out_shape=out, in_specs=specs, out_specs=out_specs,...  2.62 us
    pallas_call x4, Pallas kernels, backward(): pl.pallas_call(body, out_shape=jax.ShapeDtypeStruct((blocks * TILE, hid)...  2.08 us
    pallas_call x1, Pallas kernels, prepare(): pl.pallas_call(functools.partial(prep_body, plan, pad_col), out_shape=plt...  1.2 us
  transfers between devices with their start and end apart: 12, of which 8 were waited for; matrix products, arithmetic and copies ran while one was open for 0% of the time, Pallas kernels for 15%

profile of v5, /device:TPU:0, one launch (start us, length us, event | category | flops | bytes accessed | tf_op | source)
XLA Modules:
  0.0 43.6 jit_solution(2996889397145562126)
XLA Ops:
  0.6 0.5 %collective-permute-start.1 = (bf16[1024,256]{1,0:T(8,128)(2,1)}, bf16[1024,256]{1,0:T(8,128)(2,1)S(1)}, u32[]{:S(2)}, u32[]{:S(2)}) collective-permute-start(bf16[1024,256]{1,0:T(8,128)(2,1)} %refs_2_.1), channel_id=1, source_target_pairs={{0,1},{1,0},{2,3},{3,2},{4,5},{5,4},{6,7},{7,6},{8,9},{9,8},{10,11... | collective-permute-start | bytes 1572872 | tf_op jit(solution)/shard_map/ppermute | solution.py:294
  1.1 2.6 %collective-permute-start = (bf16[1024,256]{1,0:T(8,128)(2,1)}, bf16[1024,256]{1,0:T(8,128)(2,1)S(1)}, u32[]{:S(2)}, u32[]{:S(2)}) collective-permute-start(bf16[1024,256]{1,0:T(8,128)(2,1)} %refs_2_.1), channel_id=1, source_target_pairs={{0,2},{1,3},{2,0},{3,1},{4,6},{5,7},{6,4},{7,5},{8,10},{9,11},{10,... | collective-permute-start | bytes 1572872 | tf_op jit(solution)/shard_map/ppermute | solution.py:294
  4.4 1.2 %shard_map.94.refs_0_.list_ref = s32[102]{0:T(128)S(4)} custom-call(s32[1]{0:T(128)} %bitcast.me_ref, s32[1]{0:T(128)S(6)} %copy.10.cnt_ref, s32[64]{0:T(128)} %rows_ref.1, s32[64]{0:T(128)} %cols_ref.1), custom_call_target="tpu_custom_call" | custom-call | tf_op jit(solution)/shard_map/pallas_call | solution.py:69
  5.6 0.0 collective-permute-done.1.refs_3_
  5.6 0.0 copy-start
  5.6 1.6 %copy-done = bf16[64,128,128]{2,1,0:T(8,128)(2,1)S(1)} copy-done((bf16[64,128,128]{2,1,0:T(8,128)(2,1)S(1)}, bf16[64,128,128]{2,1,0:T(8,128)(2,1)}, u32[]{:S(2)}) %copy-start) | copy-done | bytes 2097176
  7.2 0.0 copy-start.1
  7.2 1.0 %copy-done.1 = bf16[1024,256]{1,0:T(8,128)(2,1)S(1)} copy-done((bf16[1024,256]{1,0:T(8,128)(2,1)S(1)}, bf16[1024,256]{1,0:T(8,128)(2,1)}, u32[]{:S(2)}) %copy-start.1) | copy-done | bytes 524312
  8.2 1.0 %shard_map.95.refs_3_ = f32[9,128,256]{2,1,0:T(8,128)S(1)} custom-call(s32[102]{0:T(128)S(4)} %shard_map.94.refs_0_.list_ref, bf16[64,128,128]{2,1,0:T(8,128)(2,1)S(1)} %copy-done, bf16[1024,256]{1,0:T(8,128)(2,1)S(1)} %copy-done.1, bf16[1024,256]{1,0:T(8,128)(2,1)S(1)} %collective-permute-done.1.refs_3_), custom_call_target="tpu_custom_call" | custom-call | tf_op jit(solution)/shard_map/pallas_call | solution.py:250
  9.2 0.0 copy-start.2
  9.2 0.0 copy-start.3
  9.3 7.2 %collective-permute-done.refs_2_ = bf16[1024,256]{1,0:T(8,128)(2,1)S(1)} collective-permute-done((bf16[1024,256]{1,0:T(8,128)(2,1)}, bf16[1024,256]{1,0:T(8,128)(2,1)S(1)}, u32[]{:S(2)}, u32[]{:S(2)}) %collective-permute-start) | collective-permute-done | bytes 524320 | tf_op jit(solution)/shard_map/ppermute | solution.py:294
  16.5 0.0 collective-permute-start.2
  16.5 0.4 shard_map.96.refs_3_
  16.8 1.5 %collective-permute-done.2.refs_2_ = bf16[1024,256]{1,0:T(8,128)(2,1)S(1)} collective-permute-done((bf16[1024,256]{1,0:T(8,128)(2,1)S(1)}, bf16[1024,256]{1,0:T(8,128)(2,1)S(1)}, u32[]{:S(2)}, u32[]{:S(2)}) %collective-permute-start.2) | collective-permute-done | bytes 524320 | tf_op jit(solution)/shard_map/ppermute | solution.py:294
  18.4 0.0 copy-done.2
  18.4 0.0 copy-done.3
  18.4 1.3 %shard_map.97 = (bf16[1024,256]{1,0:T(8,128)(2,1)S(1)}, bf16[1024,256]{1,0:T(8,128)(2,1)S(1)}, f32[128,256]{1,0:T(8,128)S(1)}, f32[128,256]{1,0:T(8,128)S(1)}) custom-call(s32[102]{0:T(128)S(4)} %shard_map.94.refs_0_.list_ref, bf16[64,128,128]{2,1,0:T(8,128)(2,1)S(1)} %copy-done, bf16[1024,256]{1,0:T(8,128)(2,1)S(1)} %collective-permute-done.2.refs_2_, ...), custom_call_target="tpu_custom_call" | custom-call | tf_op jit(solution)/shard_map/pallas_call | solution.py:250
  19.7 0.5 %collective-permute-start.3 = (f32[128,256]{1,0:T(8,128)S(1)}, f32[128,256]{1,0:T(8,128)S(1)}, u32[]{:S(2)}, u32[]{:S(2)}) collective-permute-start(f32[128,256]{1,0:T(8,128)S(1)} %get-tuple-element.22), channel_id=1, source_target_pairs={{0,1},{1,0},{2,3},{3,2},{4,5},{5,4},{6,7},{7,6},{8,9},{9,8},{10,11... | collective-permute-start | bytes 393224 | tf_op jit(solution)/shard_map/ppermute | solution.py:294
  20.2 0.5 %shard_map.99 = bf16[1024,256]{1,0:T(8,128)(2,1)S(1)} custom-call(s32[102]{0:T(128)S(4)} %shard_map.94.refs_0_.list_ref, bf16[64,128,128]{2,1,0:T(8,128)(2,1)S(1)} %copy-done, bf16[1024,256]{1,0:T(8,128)(2,1)S(1)} %get-tuple-element.28.s_ref), custom_call_target="tpu_custom_call" | custom-call | bytes 1024 | tf_op jit(solution)/shard_map/pallas_call | solution.py:272
  20.6 0.5 %collective-permute-start.5 = (bf16[1024,256]{1,0:T(8,128)(2,1)S(1)}, bf16[1024,256]{1,0:T(8,128)(2,1)S(1)}, u32[]{:S(2)}, u32[]{:S(2)}) collective-permute-start(bf16[1024,256]{1,0:T(8,128)(2,1)S(1)} %shard_map.99), channel_id=1, source_target_pairs={{0,1},{1,0},{2,3},{3,2},{4,5},{5,4},{6,7},{7,6},{8,9},{9,8},{10,11... | collective-permute-start | bytes 1572872 | tf_op jit(solution)/shard_map/ppermute | solution.py:294
  21.1 0.0 collective-permute-done.3
  21.2 2.1 %collective-permute-start.4 = (bf16[128,256]{1,0:T(8,128)(2,1)S(1)}, bf16[128,256]{1,0:T(8,128)(2,1)S(1)}, u32[]{:S(2)}, u32[]{:S(2)}) collective-permute-start(bf16[128,256]{1,0:T(8,128)(2,1)S(1)} %add_convert_fusion.4), channel_id=1, source_target_pairs={{0,2},{1,3},{2,0},{3,1},{4,6},{5,7},{6,4},{7,5},{8,10},{9,11},{10,... | collective-permute-start | bytes 196616 | tf_op jit(solution)/shard_map/ppermute | solution.py:297
  23.2 0.4 shard_map.98
  23.6 0.0 collective-permute-done.5.refs_1_
  23.7 0.1 shard_map.100
  23.8 1.9 %collective-permute-done.4 = bf16[128,256]{1,0:T(8,128)(2,1)S(1)} collective-permute-done((bf16[128,256]{1,0:T(8,128)(2,1)S(1)}, bf16[128,256]{1,0:T(8,128)(2,1)S(1)}, u32[]{:S(2)}, u32[]{:S(2)}) %collective-permute-start.4) | collective-permute-done | bytes 65568 | tf_op jit(solution)/shard_map/ppermute | solution.py:297
  25.7 2.2 %collective-permute-start.6 = (bf16[128,256]{1,0:T(8,128)(2,1)S(1)}, bf16[128,256]{1,0:T(8,128)(2,1)S(1)}, u32[]{:S(2)}, u32[]{:S(2)}) collective-permute-start(bf16[128,256]{1,0:T(8,128)(2,1)S(1)} %add_convert_fusion.3), channel_id=1, source_target_pairs={{0,4},{4,0},{8,12},{12,8},{16,20},{20,16},{24,28},{28,24},{1,5},{5... | collective-permute-start | bytes 196616 | tf_op jit(solution)/shard_map/ppermute | solution.py:297
  27.9 1.2 %collective-permute-start.9 = (bf16[1024,256]{1,0:T(8,128)(2,1)S(1)}, bf16[1024,256]{1,0:T(8,128)(2,1)S(1)}, u32[]{:S(2)}, u32[]{:S(2)}) collective-permute-start(bf16[1024,256]{1,0:T(8,128)(2,1)S(1)} %shard_map.100), channel_id=1, source_target_pairs={{0,2},{1,3},{2,0},{3,1},{4,6},{5,7},{6,4},{7,5},{8,10},{9,11},{10,... | collective-permute-start | bytes 1572872 | tf_op jit(solution)/shard_map/ppermute | solution.py:294
  29.1 0.5 %shard_map.101 = bf16[1024,256]{1,0:T(8,128)(2,1)S(1)} custom-call(s32[102]{0:T(128)S(4)} %shard_map.94.refs_0_.list_ref, bf16[64,128,128]{2,1,0:T(8,128)(2,1)S(1)} %copy-done, bf16[1024,256]{1,0:T(8,128)(2,1)S(1)} %get-tuple-element.28.s_ref), custom_call_target="tpu_custom_call" | custom-call | bytes 1024 | tf_op jit(solution)/shard_map/pallas_call | solution.py:272
  29.6 0.5 %collective-permute-done.6 = bf16[128,256]{1,0:T(8,128)(2,1)S(1)} collective-permute-done((bf16[128,256]{1,0:T(8,128)(2,1)S(1)}, bf16[128,256]{1,0:T(8,128)(2,1)S(1)}, u32[]{:S(2)}, u32[]{:S(2)}) %collective-permute-start.6) | collective-permute-done | bytes 65568 | tf_op jit(solution)/shard_map/ppermute | solution.py:297
  30.1 0.1 collective-permute-start.8
  30.2 1.7 %collective-permute-start.7 = (bf16[128,256]{1,0:T(8,128)(2,1)S(1)}, bf16[128,256]{1,0:T(8,128)(2,1)S(1)}, u32[]{:S(2)}, u32[]{:S(2)}) collective-permute-start(bf16[128,256]{1,0:T(8,128)(2,1)S(1)} %add_convert_fusion.2), channel_id=1, source_target_pairs={{0,8},{4,12},{8,0},{12,4},{16,24},{20,28},{24,16},{28,20},{1,9},{5... | collective-permute-start | bytes 196616 | tf_op jit(solution)/shard_map/ppermute | solution.py:297
  31.9 0.7 %shard_map.102 = f32[9,128,256]{2,1,0:T(8,128)S(1)} custom-call(s32[102]{0:T(128)S(4)} %shard_map.94.refs_0_.list_ref, bf16[64,128,128]{2,1,0:T(8,128)(2,1)S(1)} %copy-done, bf16[1024,256]{1,0:T(8,128)(2,1)S(1)} %get-tuple-element.28.s_ref), custom_call_target="tpu_custom_call" | custom-call | bytes 1024 | tf_op jit(solution)/shard_map/pallas_call | solution.py:272
  32.7 2.0 %collective-permute-done.7 = bf16[128,256]{1,0:T(8,128)(2,1)S(1)} collective-permute-done((bf16[128,256]{1,0:T(8,128)(2,1)S(1)}, bf16[128,256]{1,0:T(8,128)(2,1)S(1)}, u32[]{:S(2)}, u32[]{:S(2)}) %collective-permute-start.7) | collective-permute-done | bytes 65568 | tf_op jit(solution)/shard_map/ppermute | solution.py:297
  34.7 3.1 %collective-permute-start.10 = (bf16[128,256]{1,0:T(8,128)(2,1)S(1)}, bf16[128,256]{1,0:T(8,128)(2,1)S(1)}, u32[]{:S(2)}, u32[]{:S(2)}) collective-permute-start(bf16[128,256]{1,0:T(8,128)(2,1)S(1)} %add_convert_fusion.1), channel_id=1, source_target_pairs={{0,16},{4,20},{8,24},{12,28},{16,0},{20,4},{24,8},{28,12},{1,17},{... | collective-permute-start | bytes 196616 | tf_op jit(solution)/shard_map/ppermute | solution.py:297
  37.8 0.8 %shard_map.103 = bf16[1024,256]{1,0:T(8,128)(2,1)} custom-call(bf16[1024,256]{1,0:T(8,128)(2,1)S(1)} %get-tuple-element.30.x_ref), custom_call_target="tpu_custom_call" | custom-call | bytes 1024 | tf_op jit(solution)/shard_map/pallas_call | solution.py:107
  38.7 1.7 %collective-permute-done.9.refs_2_ = bf16[1024,256]{1,0:T(8,128)(2,1)S(1)} collective-permute-done((bf16[1024,256]{1,0:T(8,128)(2,1)S(1)}, bf16[1024,256]{1,0:T(8,128)(2,1)S(1)}, u32[]{:S(2)}, u32[]{:S(2)}) %collective-permute-start.9) | collective-permute-done | bytes 524320 | tf_op jit(solution)/shard_map/ppermute | solution.py:294
  40.4 0.0 collective-permute-done.8.refs_1_
  40.4 0.9 %shard_map.104 = bf16[1024,256]{1,0:T(8,128)(2,1)} custom-call(f32[1152,256]{1,0:T(8,128)S(1)} %bitcast.3, bf16[1024,256]{1,0:T(8,128)(2,1)S(1)} %collective-permute-done.8.refs_1_, bf16[1024,256]{1,0:T(8,128)(2,1)S(1)} %collective-permute-done.9.refs_2_), custom_call_target="tpu_custom_call" | custom-call | bytes 1024 | tf_op jit(solution)/shard_map/pallas_call | solution.py:128
  41.3 0.2 collective-permute-done.10
  41.5 0.1 collective-permute-start.11
  41.6 1.2 %collective-permute-done.11 = bf16[128,256]{1,0:T(8,128)(2,1)S(1)} collective-permute-done((bf16[128,256]{1,0:T(8,128)(2,1)S(1)}, bf16[128,256]{1,0:T(8,128)(2,1)S(1)}, u32[]{:S(2)}, u32[]{:S(2)}) %collective-permute-start.11) | collective-permute-done | bytes 65568 | tf_op jit(solution)/shard_map/ppermute | solution.py:294
  42.8 0.7 %fusion = f32[256,256]{1,0:T(8,128)} fusion(bf16[128,256]{1,0:T(8,128)(2,1)S(1)} %collective-permute-done.11, bf16[128,256]{1,0:T(8,128)(2,1)S(1)} %add_convert_fusion, pred[]{:T(512)S(6)} %eq.3), kind=kLoop, calls=%fused_computation.1 | loop fusion | flops 655360 | bytes 393217 | tf_op jit(solution)/shard_map/convert_element_type | solution.py:336
  (5 shorter events, 0.1 us)
Async XLA Ops:
  0.6 5.0 %collective-permute-start.1 = (bf16[1024,256]{1,0:T(8,128)(2,1)}, bf16[1024,256]{1,0:T(8,128)(2,1)S(1)}, u32[]{:S(2)}, u32[]{:S(2)}) collective-permute-start(bf16[1024,256]{1,0:T(8,128)(2,1)} %refs_2_.1), channel_id=1, source_target_pairs={{0,1},{1,0},{2,3},{3,2},{4,5},{5,4},{6,7},{7,6},{8,9},{9,8},{10,11... | collective-permute-start | bytes 1572872 | tf_op jit(solution)/shard_map/ppermute | solution.py:294
  1.1 15.3 %collective-permute-start = (bf16[1024,256]{1,0:T(8,128)(2,1)}, bf16[1024,256]{1,0:T(8,128)(2,1)S(1)}, u32[]{:S(2)}, u32[]{:S(2)}) collective-permute-start(bf16[1024,256]{1,0:T(8,128)(2,1)} %refs_2_.1), channel_id=1, source_target_pairs={{0,2},{1,3},{2,0},{3,1},{4,6},{5,7},{6,4},{7,5},{8,10},{9,11},{10,... | collective-permute-start | bytes 1572872 | tf_op jit(solution)/shard_map/ppermute | solution.py:294
  5.6 1.6 %copy-start = (bf16[64,128,128]{2,1,0:T(8,128)(2,1)S(1)}, bf16[64,128,128]{2,1,0:T(8,128)(2,1)}, u32[]{:S(2)}) copy-start(bf16[64,128,128]{2,1,0:T(8,128)(2,1)} %tiles_ref.7) | copy-start | bytes 6291460
  7.2 1.0 %copy-start.1 = (bf16[1024,256]{1,0:T(8,128)(2,1)S(1)}, bf16[1024,256]{1,0:T(8,128)(2,1)}, u32[]{:S(2)}) copy-start(bf16[1024,256]{1,0:T(8,128)(2,1)} %refs_2_.1) | copy-start | bytes 1572868
  9.2 9.2 %copy-start.2 = (bf16[1024,256]{1,0:T(8,128)(2,1)S(1)}, bf16[1024,256]{1,0:T(8,128)(2,1)}, u32[]{:S(2)}) copy-start(bf16[1024,256]{1,0:T(8,128)(2,1)} %refs_5_.1) | copy-start | bytes 1572868
  9.2 9.1 %copy-start.3 = (bf16[256,256]{1,0:T(8,128)(2,1)S(1)}, bf16[256,256]{1,0:T(8,128)(2,1)}, u32[]{:S(2)}) copy-start(bf16[256,256]{1,0:T(8,128)(2,1)} %refs_4_.1) | copy-start | bytes 393220
  16.5 1.9 %collective-permute-start.2 = (bf16[1024,256]{1,0:T(8,128)(2,1)S(1)}, bf16[1024,256]{1,0:T(8,128)(2,1)S(1)}, u32[]{:S(2)}, u32[]{:S(2)}) collective-permute-start(bf16[1024,256]{1,0:T(8,128)(2,1)S(1)} %collective-permute-done.refs_2_), channel_id=1, source_target_pairs={{0,1},{1,0},{2,3},{3,2},{4,5},{5,4},{6,7},{7,6},{8,9},{9,8},{10,11... | collective-permute-start | bytes 1572872 | tf_op jit(solution)/shard_map/ppermute | solution.py:294
  19.7 1.5 %collective-permute-start.3 = (f32[128,256]{1,0:T(8,128)S(1)}, f32[128,256]{1,0:T(8,128)S(1)}, u32[]{:S(2)}, u32[]{:S(2)}) collective-permute-start(f32[128,256]{1,0:T(8,128)S(1)} %get-tuple-element.22), channel_id=1, source_target_pairs={{0,1},{1,0},{2,3},{3,2},{4,5},{5,4},{6,7},{7,6},{8,9},{9,8},{10,11... | collective-permute-start | bytes 393224 | tf_op jit(solution)/shard_map/ppermute | solution.py:294
  20.6 3.0 %collective-permute-start.5 = (bf16[1024,256]{1,0:T(8,128)(2,1)S(1)}, bf16[1024,256]{1,0:T(8,128)(2,1)S(1)}, u32[]{:S(2)}, u32[]{:S(2)}) collective-permute-start(bf16[1024,256]{1,0:T(8,128)(2,1)S(1)} %shard_map.99), channel_id=1, source_target_pairs={{0,1},{1,0},{2,3},{3,2},{4,5},{5,4},{6,7},{7,6},{8,9},{9,8},{10,11... | collective-permute-start | bytes 1572872 | tf_op jit(solution)/shard_map/ppermute | solution.py:294
  21.2 4.5 %collective-permute-start.4 = (bf16[128,256]{1,0:T(8,128)(2,1)S(1)}, bf16[128,256]{1,0:T(8,128)(2,1)S(1)}, u32[]{:S(2)}, u32[]{:S(2)}) collective-permute-start(bf16[128,256]{1,0:T(8,128)(2,1)S(1)} %add_convert_fusion.4), channel_id=1, source_target_pairs={{0,2},{1,3},{2,0},{3,1},{4,6},{5,7},{6,4},{7,5},{8,10},{9,11},{10,... | collective-permute-start | bytes 196616 | tf_op jit(solution)/shard_map/ppermute | solution.py:297
  25.7 4.5 %collective-permute-start.6 = (bf16[128,256]{1,0:T(8,128)(2,1)S(1)}, bf16[128,256]{1,0:T(8,128)(2,1)S(1)}, u32[]{:S(2)}, u32[]{:S(2)}) collective-permute-start(bf16[128,256]{1,0:T(8,128)(2,1)S(1)} %add_convert_fusion.3), channel_id=1, source_target_pairs={{0,4},{4,0},{8,12},{12,8},{16,20},{20,16},{24,28},{28,24},{1,5},{5... | collective-permute-start | bytes 196616 | tf_op jit(solution)/shard_map/ppermute | solution.py:297
  27.9 12.5 %collective-permute-start.9 = (bf16[1024,256]{1,0:T(8,128)(2,1)S(1)}, bf16[1024,256]{1,0:T(8,128)(2,1)S(1)}, u32[]{:S(2)}, u32[]{:S(2)}) collective-permute-start(bf16[1024,256]{1,0:T(8,128)(2,1)S(1)} %shard_map.100), channel_id=1, source_target_pairs={{0,2},{1,3},{2,0},{3,1},{4,6},{5,7},{6,4},{7,5},{8,10},{9,11},{10,... | collective-permute-start | bytes 1572872 | tf_op jit(solution)/shard_map/ppermute | solution.py:294
  30.1 10.2 %collective-permute-start.8 = (bf16[1024,256]{1,0:T(8,128)(2,1)S(1)}, bf16[1024,256]{1,0:T(8,128)(2,1)S(1)}, u32[]{:S(2)}, u32[]{:S(2)}) collective-permute-start(bf16[1024,256]{1,0:T(8,128)(2,1)S(1)} %shard_map.101), channel_id=1, source_target_pairs={{0,1},{1,0},{2,3},{3,2},{4,5},{5,4},{6,7},{7,6},{8,9},{9,8},{10,11... | collective-permute-start | bytes 1572872 | tf_op jit(solution)/shard_map/ppermute | solution.py:294
  30.2 4.5 %collective-permute-start.7 = (bf16[128,256]{1,0:T(8,128)(2,1)S(1)}, bf16[128,256]{1,0:T(8,128)(2,1)S(1)}, u32[]{:S(2)}, u32[]{:S(2)}) collective-permute-start(bf16[128,256]{1,0:T(8,128)(2,1)S(1)} %add_convert_fusion.2), channel_id=1, source_target_pairs={{0,8},{4,12},{8,0},{12,4},{16,24},{20,28},{24,16},{28,20},{1,9},{5... | collective-permute-start | bytes 196616 | tf_op jit(solution)/shard_map/ppermute | solution.py:297
  34.7 6.8 %collective-permute-start.10 = (bf16[128,256]{1,0:T(8,128)(2,1)S(1)}, bf16[128,256]{1,0:T(8,128)(2,1)S(1)}, u32[]{:S(2)}, u32[]{:S(2)}) collective-permute-start(bf16[128,256]{1,0:T(8,128)(2,1)S(1)} %add_convert_fusion.1), channel_id=1, source_target_pairs={{0,16},{4,20},{8,24},{12,28},{16,0},{20,4},{24,8},{28,12},{1,17},{... | collective-permute-start | bytes 196616 | tf_op jit(solution)/shard_map/ppermute | solution.py:297
  41.5 1.3 %collective-permute-start.11 = (bf16[128,256]{1,0:T(8,128)(2,1)S(1)}, bf16[128,256]{1,0:T(8,128)(2,1)S(1)}, u32[]{:S(2)}, u32[]{:S(2)}) collective-permute-start(bf16[128,256]{1,0:T(8,128)(2,1)S(1)} %add_convert_fusion), channel_id=1, source_target_pairs={{0,1},{1,0},{2,3},{3,2},{4,5},{5,4},{6,7},{7,6},{8,9},{9,8},{10,11... | collective-permute-start | bytes 196616 | tf_op jit(solution)/shard_map/ppermute | solution.py:294

commit v6 on v5

--- a/solution.py
+++ b/solution.py
@@ -8,7 +8,7 @@
 from jax.sharding import PartitionSpec as P
 
 TILE = 128
-UNROLL = 8
+UNROLL = 16
 F32 = jnp.float32
 BF16 = jnp.bfloat16
 

time: 43.5 us -> 44 us (1.011)
    ppermute x8, waiting for transfers between devices: 11.7 us -> 12.7 us  [swap(): return lax.ppermute(x, 'grp', [(i, i ^ bit) for i in range(4)])]
    ppermute x4, waiting for transfers between devices: 4.64 us -> 4.04 us  [fold(): other = lax.ppermute(w, axis, [(i, i ^ bit) for i in range(size)])]
  transfers between devices with their start and end apart: 12 -> 12, of which waited for: 8 -> 7; matrix products, arithmetic and copies ran while one was open for 0% -> 0% of each run, Pallas kernels for 15% -> 15%
where the time goes in v6:
time: 44 us
  waiting for transfers between devices  16.7 us (38%)
  starting transfers between devices  14.5 us (33%)
  Pallas kernels  7.86 us (18%)
  local copies, waits for them, and re-layouts  2.64 us (6%)
  between operations  1.46 us (3%)
  other arithmetic  0.82 us (2%)
    ppermute x8, waiting for transfers between devices, swap(): return lax.ppermute(x, 'grp', [(i, i ^ bit) for i in range(4)])  12.7 us
    ppermute x4, starting transfers between devices, fold(): other = lax.ppermute(w, axis, [(i, i ^ bit) for i in range(size)])  8.83 us
    ppermute x8, starting transfers between devices, swap(): return lax.ppermute(x, 'grp', [(i, i ^ bit) for i in range(4)])  5.64 us
    ppermute x4, waiting for transfers between devices, fold(): other = lax.ppermute(w, axis, [(i, i ^ bit) for i in range(size)])  4.04 us
    pallas_call x3, Pallas kernels, forward(): pl.pallas_call(body, out_shape=out, in_specs=specs, out_specs=out_specs,...  2.86 us
    unnamed x8, local copies, waits for them, and re-layouts  2.64 us
    pallas_call x4, Pallas kernels, backward(): pl.pallas_call(body, out_shape=jax.ShapeDtypeStruct((blocks * TILE, hid)...  2.28 us
    pallas_call x2, Pallas kernels, add_rows(): pl.pallas_call(body, out_shape=jax.ShapeDtypeStruct(shape, BF16), in_spec...  1.04 us
  transfers between devices with their start and end apart: 12, of which 7 were waited for; matrix products, arithmetic and copies ran while one was open for 0% of the time, Pallas kernels for 15%

profile of v6, /device:TPU:0, one launch (start us, length us, event | category | flops | bytes accessed | tf_op | source)
XLA Modules:
  0.0 44.0 jit_solution(6128749705428007046)
XLA Ops:
  0.6 0.5 %collective-permute-start.1 = (bf16[1024,256]{1,0:T(8,128)(2,1)}, bf16[1024,256]{1,0:T(8,128)(2,1)S(1)}, u32[]{:S(2)}, u32[]{:S(2)}) collective-permute-start(bf16[1024,256]{1,0:T(8,128)(2,1)} %refs_2_.1), channel_id=1, source_target_pairs={{0,1},{1,0},{2,3},{3,2},{4,5},{5,4},{6,7},{7,6},{8,9},{9,8},{10,11... | collective-permute-start | bytes 1572872 | tf_op jit(solution)/shard_map/ppermute | solution.py:294
  1.1 2.6 %collective-permute-start = (bf16[1024,256]{1,0:T(8,128)(2,1)}, bf16[1024,256]{1,0:T(8,128)(2,1)S(1)}, u32[]{:S(2)}, u32[]{:S(2)}) collective-permute-start(bf16[1024,256]{1,0:T(8,128)(2,1)} %refs_2_.1), channel_id=1, source_target_pairs={{0,2},{1,3},{2,0},{3,1},{4,6},{5,7},{6,4},{7,5},{8,10},{9,11},{10,... | collective-permute-start | bytes 1572872 | tf_op jit(solution)/shard_map/ppermute | solution.py:294
  4.4 0.9 %shard_map.94.refs_0_.list_ref = s32[134]{0:T(256)S(4)} custom-call(s32[1]{0:T(128)} %bitcast.me_ref, s32[1]{0:T(128)S(6)} %copy.10.cnt_ref, s32[64]{0:T(128)} %rows_ref.1, s32[64]{0:T(128)} %cols_ref.1), custom_call_target="tpu_custom_call" | custom-call | tf_op jit(solution)/shard_map/pallas_call | solution.py:69
  5.3 0.0 collective-permute-done.1.refs_3_
  5.3 0.0 copy-start
  5.3 1.6 %copy-done = bf16[64,128,128]{2,1,0:T(8,128)(2,1)S(1)} copy-done((bf16[64,128,128]{2,1,0:T(8,128)(2,1)S(1)}, bf16[64,128,128]{2,1,0:T(8,128)(2,1)}, u32[]{:S(2)}) %copy-start) | copy-done | bytes 2097176
  6.9 0.0 copy-start.1
  6.9 1.0 %copy-done.1 = bf16[1024,256]{1,0:T(8,128)(2,1)S(1)} copy-done((bf16[1024,256]{1,0:T(8,128)(2,1)S(1)}, bf16[1024,256]{1,0:T(8,128)(2,1)}, u32[]{:S(2)}) %copy-start.1) | copy-done | bytes 524312
  7.9 0.9 %shard_map.95.refs_3_ = f32[9,128,256]{2,1,0:T(8,128)S(1)} custom-call(s32[134]{0:T(256)S(4)} %shard_map.94.refs_0_.list_ref, bf16[64,128,128]{2,1,0:T(8,128)(2,1)S(1)} %copy-done, bf16[1024,256]{1,0:T(8,128)(2,1)S(1)} %copy-done.1, bf16[1024,256]{1,0:T(8,128)(2,1)S(1)} %collective-permute-done.1.refs_3_), custom_call_target="tpu_custom_call" | custom-call | tf_op jit(solution)/shard_map/pallas_call | solution.py:250
  8.9 0.0 copy-start.2
  8.9 0.0 copy-start.3
  8.9 7.6 %collective-permute-done.refs_2_ = bf16[1024,256]{1,0:T(8,128)(2,1)S(1)} collective-permute-done((bf16[1024,256]{1,0:T(8,128)(2,1)}, bf16[1024,256]{1,0:T(8,128)(2,1)S(1)}, u32[]{:S(2)}, u32[]{:S(2)}) %collective-permute-start) | collective-permute-done | bytes 524320 | tf_op jit(solution)/shard_map/ppermute | solution.py:294
  16.5 0.0 collective-permute-start.2
  16.5 0.5 %shard_map.96.refs_3_ = f32[9,128,256]{2,1,0:T(8,128)S(1)} custom-call(s32[134]{0:T(256)S(4)} %shard_map.94.refs_0_.list_ref, bf16[64,128,128]{2,1,0:T(8,128)(2,1)S(1)} %copy-done, bf16[1024,256]{1,0:T(8,128)(2,1)S(1)} %collective-permute-done.refs_2_, f32[9,128,256]{2,1,0:T(8,128)S(1)} %shard_map.95.refs_3_), custom_call_target="tpu_custom_call" | custom-call | tf_op jit(solution)/shard_map/pallas_call | solution.py:250
  17.0 1.4 %collective-permute-done.2.refs_2_ = bf16[1024,256]{1,0:T(8,128)(2,1)S(1)} collective-permute-done((bf16[1024,256]{1,0:T(8,128)(2,1)S(1)}, bf16[1024,256]{1,0:T(8,128)(2,1)S(1)}, u32[]{:S(2)}, u32[]{:S(2)}) %collective-permute-start.2) | collective-permute-done | bytes 524320 | tf_op jit(solution)/shard_map/ppermute | solution.py:294
  18.4 0.0 copy-done.2
  18.4 0.0 copy-done.3
  18.4 1.4 %shard_map.97 = (bf16[1024,256]{1,0:T(8,128)(2,1)S(1)}, bf16[1024,256]{1,0:T(8,128)(2,1)S(1)}, f32[128,256]{1,0:T(8,128)S(1)}, f32[128,256]{1,0:T(8,128)S(1)}) custom-call(s32[134]{0:T(256)S(4)} %shard_map.94.refs_0_.list_ref, bf16[64,128,128]{2,1,0:T(8,128)(2,1)S(1)} %copy-done, bf16[1024,256]{1,0:T(8,128)(2,1)S(1)} %collective-permute-done.2.refs_2_, ...), custom_call_target="tpu_custom_call" | custom-call | tf_op jit(solution)/shard_map/pallas_call | solution.py:250
  19.8 0.2 collective-permute-start.3
  20.0 0.6 %shard_map.99 = bf16[1024,256]{1,0:T(8,128)(2,1)S(1)} custom-call(s32[134]{0:T(256)S(4)} %shard_map.94.refs_0_.list_ref, bf16[64,128,128]{2,1,0:T(8,128)(2,1)S(1)} %copy-done, bf16[1024,256]{1,0:T(8,128)(2,1)S(1)} %get-tuple-element.28.s_ref), custom_call_target="tpu_custom_call" | custom-call | bytes 1024 | tf_op jit(solution)/shard_map/pallas_call | solution.py:272
  20.6 0.5 %collective-permute-start.5 = (bf16[1024,256]{1,0:T(8,128)(2,1)S(1)}, bf16[1024,256]{1,0:T(8,128)(2,1)S(1)}, u32[]{:S(2)}, u32[]{:S(2)}) collective-permute-start(bf16[1024,256]{1,0:T(8,128)(2,1)S(1)} %shard_map.99), channel_id=1, source_target_pairs={{0,1},{1,0},{2,3},{3,2},{4,5},{5,4},{6,7},{7,6},{8,9},{9,8},{10,11... | collective-permute-start | bytes 1572872 | tf_op jit(solution)/shard_map/ppermute | solution.py:294
  21.1 0.2 collective-permute-done.3
  21.2 1.8 %collective-permute-start.4 = (bf16[128,256]{1,0:T(8,128)(2,1)S(1)}, bf16[128,256]{1,0:T(8,128)(2,1)S(1)}, u32[]{:S(2)}, u32[]{:S(2)}) collective-permute-start(bf16[128,256]{1,0:T(8,128)(2,1)S(1)} %add_convert_fusion.4), channel_id=1, source_target_pairs={{0,2},{1,3},{2,0},{3,1},{4,6},{5,7},{6,4},{7,5},{8,10},{9,11},{10,... | collective-permute-start | bytes 196616 | tf_op jit(solution)/shard_map/ppermute | solution.py:297
  23.0 0.5 %shard_map.98 = f32[9,128,256]{2,1,0:T(8,128)S(1)} custom-call(s32[134]{0:T(256)S(4)} %shard_map.94.refs_0_.list_ref, bf16[64,128,128]{2,1,0:T(8,128)(2,1)S(1)} %copy-done, bf16[1024,256]{1,0:T(8,128)(2,1)S(1)} %get-tuple-element.28.s_ref), custom_call_target="tpu_custom_call" | custom-call | flops 11000000512 | bytes 1024 | tf_op jit(solution)/shard_map/pallas_call | solution.py:272
  23.6 0.0 collective-permute-done.5.refs_1_
  23.6 0.1 shard_map.100
  23.7 1.9 %collective-permute-done.4 = bf16[128,256]{1,0:T(8,128)(2,1)S(1)} collective-permute-done((bf16[128,256]{1,0:T(8,128)(2,1)S(1)}, bf16[128,256]{1,0:T(8,128)(2,1)S(1)}, u32[]{:S(2)}, u32[]{:S(2)}) %collective-permute-start.4) | collective-permute-done | bytes 65568 | tf_op jit(solution)/shard_map/ppermute | solution.py:297
  25.6 2.1 %collective-permute-start.6 = (bf16[128,256]{1,0:T(8,128)(2,1)S(1)}, bf16[128,256]{1,0:T(8,128)(2,1)S(1)}, u32[]{:S(2)}, u32[]{:S(2)}) collective-permute-start(bf16[128,256]{1,0:T(8,128)(2,1)S(1)} %add_convert_fusion.3), channel_id=1, source_target_pairs={{0,4},{4,0},{8,12},{12,8},{16,20},{20,16},{24,28},{28,24},{1,5},{5... | collective-permute-start | bytes 196616 | tf_op jit(solution)/shard_map/ppermute | solution.py:297
  27.6 1.7 %collective-permute-start.9 = (bf16[1024,256]{1,0:T(8,128)(2,1)S(1)}, bf16[1024,256]{1,0:T(8,128)(2,1)S(1)}, u32[]{:S(2)}, u32[]{:S(2)}) collective-permute-start(bf16[1024,256]{1,0:T(8,128)(2,1)S(1)} %shard_map.100), channel_id=1, source_target_pairs={{0,2},{1,3},{2,0},{3,1},{4,6},{5,7},{6,4},{7,5},{8,10},{9,11},{10,... | collective-permute-start | bytes 1572872 | tf_op jit(solution)/shard_map/ppermute | solution.py:294
  29.4 0.6 %shard_map.101 = bf16[1024,256]{1,0:T(8,128)(2,1)S(1)} custom-call(s32[134]{0:T(256)S(4)} %shard_map.94.refs_0_.list_ref, bf16[64,128,128]{2,1,0:T(8,128)(2,1)S(1)} %copy-done, bf16[1024,256]{1,0:T(8,128)(2,1)S(1)} %get-tuple-element.28.s_ref), custom_call_target="tpu_custom_call" | custom-call | bytes 1024 | tf_op jit(solution)/shard_map/pallas_call | solution.py:272
  30.0 0.0 collective-permute-done.6
  30.0 0.1 collective-permute-start.8
  30.1 1.8 %collective-permute-start.7 = (bf16[128,256]{1,0:T(8,128)(2,1)S(1)}, bf16[128,256]{1,0:T(8,128)(2,1)S(1)}, u32[]{:S(2)}, u32[]{:S(2)}) collective-permute-start(bf16[128,256]{1,0:T(8,128)(2,1)S(1)} %add_convert_fusion.2), channel_id=1, source_target_pairs={{0,8},{4,12},{8,0},{12,4},{16,24},{20,28},{24,16},{28,20},{1,9},{5... | collective-permute-start | bytes 196616 | tf_op jit(solution)/shard_map/ppermute | solution.py:297
  31.9 0.5 %shard_map.102 = f32[9,128,256]{2,1,0:T(8,128)S(1)} custom-call(s32[134]{0:T(256)S(4)} %shard_map.94.refs_0_.list_ref, bf16[64,128,128]{2,1,0:T(8,128)(2,1)S(1)} %copy-done, bf16[1024,256]{1,0:T(8,128)(2,1)S(1)} %get-tuple-element.28.s_ref), custom_call_target="tpu_custom_call" | custom-call | bytes 1024 | tf_op jit(solution)/shard_map/pallas_call | solution.py:272
  32.4 2.2 %collective-permute-done.7 = bf16[128,256]{1,0:T(8,128)(2,1)S(1)} collective-permute-done((bf16[128,256]{1,0:T(8,128)(2,1)S(1)}, bf16[128,256]{1,0:T(8,128)(2,1)S(1)}, u32[]{:S(2)}, u32[]{:S(2)}) %collective-permute-start.7) | collective-permute-done | bytes 65568 | tf_op jit(solution)/shard_map/ppermute | solution.py:297
  34.6 3.2 %collective-permute-start.10 = (bf16[128,256]{1,0:T(8,128)(2,1)S(1)}, bf16[128,256]{1,0:T(8,128)(2,1)S(1)}, u32[]{:S(2)}, u32[]{:S(2)}) collective-permute-start(bf16[128,256]{1,0:T(8,128)(2,1)S(1)} %add_convert_fusion.1), channel_id=1, source_target_pairs={{0,16},{4,20},{8,24},{12,28},{16,0},{20,4},{24,8},{28,12},{1,17},{... | collective-permute-start | bytes 196616 | tf_op jit(solution)/shard_map/ppermute | solution.py:297
  37.8 0.8 %shard_map.103 = bf16[1024,256]{1,0:T(8,128)(2,1)} custom-call(bf16[1024,256]{1,0:T(8,128)(2,1)S(1)} %get-tuple-element.30.x_ref), custom_call_target="tpu_custom_call" | custom-call | bytes 1024 | tf_op jit(solution)/shard_map/pallas_call | solution.py:107
  38.6 2.3 %collective-permute-done.9.refs_2_ = bf16[1024,256]{1,0:T(8,128)(2,1)S(1)} collective-permute-done((bf16[1024,256]{1,0:T(8,128)(2,1)S(1)}, bf16[1024,256]{1,0:T(8,128)(2,1)S(1)}, u32[]{:S(2)}, u32[]{:S(2)}) %collective-permute-start.9) | collective-permute-done | bytes 524320 | tf_op jit(solution)/shard_map/ppermute | solution.py:294
  41.0 0.0 collective-permute-done.8.refs_1_
  41.0 0.9 %shard_map.104 = bf16[1024,256]{1,0:T(8,128)(2,1)} custom-call(f32[1152,256]{1,0:T(8,128)S(1)} %bitcast.3, bf16[1024,256]{1,0:T(8,128)(2,1)S(1)} %collective-permute-done.8.refs_1_, bf16[1024,256]{1,0:T(8,128)(2,1)S(1)} %collective-permute-done.9.refs_2_), custom_call_target="tpu_custom_call" | custom-call | bytes 1024 | tf_op jit(solution)/shard_map/pallas_call | solution.py:128
  41.9 0.0 collective-permute-done.10
  41.9 0.1 collective-permute-start.11
  42.0 1.2 %collective-permute-done.11 = bf16[128,256]{1,0:T(8,128)(2,1)S(1)} collective-permute-done((bf16[128,256]{1,0:T(8,128)(2,1)S(1)}, bf16[128,256]{1,0:T(8,128)(2,1)S(1)}, u32[]{:S(2)}, u32[]{:S(2)}) %collective-permute-start.11) | collective-permute-done | bytes 65568 | tf_op jit(solution)/shard_map/ppermute | solution.py:294
  43.3 0.7 %fusion = f32[256,256]{1,0:T(8,128)} fusion(bf16[128,256]{1,0:T(8,128)(2,1)S(1)} %collective-permute-done.11, bf16[128,256]{1,0:T(8,128)(2,1)S(1)} %add_convert_fusion, pred[]{:T(512)S(6)} %eq.3), kind=kLoop, calls=%fused_computation.1 | loop fusion | flops 655360 | bytes 393217 | tf_op jit(solution)/shard_map/convert_element_type | solution.py:336
  (5 shorter events, 0.1 us)
Async XLA Ops:
  0.6 4.6 %collective-permute-start.1 = (bf16[1024,256]{1,0:T(8,128)(2,1)}, bf16[1024,256]{1,0:T(8,128)(2,1)S(1)}, u32[]{:S(2)}, u32[]{:S(2)}) collective-permute-start(bf16[1024,256]{1,0:T(8,128)(2,1)} %refs_2_.1), channel_id=1, source_target_pairs={{0,1},{1,0},{2,3},{3,2},{4,5},{5,4},{6,7},{7,6},{8,9},{9,8},{10,11... | collective-permute-start | bytes 1572872 | tf_op jit(solution)/shard_map/ppermute | solution.py:294
  1.1 15.3 %collective-permute-start = (bf16[1024,256]{1,0:T(8,128)(2,1)}, bf16[1024,256]{1,0:T(8,128)(2,1)S(1)}, u32[]{:S(2)}, u32[]{:S(2)}) collective-permute-start(bf16[1024,256]{1,0:T(8,128)(2,1)} %refs_2_.1), channel_id=1, source_target_pairs={{0,2},{1,3},{2,0},{3,1},{4,6},{5,7},{6,4},{7,5},{8,10},{9,11},{10,... | collective-permute-start | bytes 1572872 | tf_op jit(solution)/shard_map/ppermute | solution.py:294
  5.3 1.6 %copy-start = (bf16[64,128,128]{2,1,0:T(8,128)(2,1)S(1)}, bf16[64,128,128]{2,1,0:T(8,128)(2,1)}, u32[]{:S(2)}) copy-start(bf16[64,128,128]{2,1,0:T(8,128)(2,1)} %tiles_ref.7) | copy-start | bytes 6291460
  6.9 1.0 %copy-start.1 = (bf16[1024,256]{1,0:T(8,128)(2,1)S(1)}, bf16[1024,256]{1,0:T(8,128)(2,1)}, u32[]{:S(2)}) copy-start(bf16[1024,256]{1,0:T(8,128)(2,1)} %refs_2_.1) | copy-start | bytes 1572868
  8.9 9.5 %copy-start.2 = (bf16[1024,256]{1,0:T(8,128)(2,1)S(1)}, bf16[1024,256]{1,0:T(8,128)(2,1)}, u32[]{:S(2)}) copy-start(bf16[1024,256]{1,0:T(8,128)(2,1)} %refs_5_.1) | copy-start | bytes 1572868
  8.9 9.5 %copy-start.3 = (bf16[256,256]{1,0:T(8,128)(2,1)S(1)}, bf16[256,256]{1,0:T(8,128)(2,1)}, u32[]{:S(2)}) copy-start(bf16[256,256]{1,0:T(8,128)(2,1)} %refs_4_.1) | copy-start | bytes 393220
  16.5 1.9 %collective-permute-start.2 = (bf16[1024,256]{1,0:T(8,128)(2,1)S(1)}, bf16[1024,256]{1,0:T(8,128)(2,1)S(1)}, u32[]{:S(2)}, u32[]{:S(2)}) collective-permute-start(bf16[1024,256]{1,0:T(8,128)(2,1)S(1)} %collective-permute-done.refs_2_), channel_id=1, source_target_pairs={{0,1},{1,0},{2,3},{3,2},{4,5},{5,4},{6,7},{7,6},{8,9},{9,8},{10,11... | collective-permute-start | bytes 1572872 | tf_op jit(solution)/shard_map/ppermute | solution.py:294
  19.8 1.4 %collective-permute-start.3 = (f32[128,256]{1,0:T(8,128)S(1)}, f32[128,256]{1,0:T(8,128)S(1)}, u32[]{:S(2)}, u32[]{:S(2)}) collective-permute-start(f32[128,256]{1,0:T(8,128)S(1)} %get-tuple-element.22), channel_id=1, source_target_pairs={{0,1},{1,0},{2,3},{3,2},{4,5},{5,4},{6,7},{7,6},{8,9},{9,8},{10,11... | collective-permute-start | bytes 393224 | tf_op jit(solution)/shard_map/ppermute | solution.py:294
  20.6 3.0 %collective-permute-start.5 = (bf16[1024,256]{1,0:T(8,128)(2,1)S(1)}, bf16[1024,256]{1,0:T(8,128)(2,1)S(1)}, u32[]{:S(2)}, u32[]{:S(2)}) collective-permute-start(bf16[1024,256]{1,0:T(8,128)(2,1)S(1)} %shard_map.99), channel_id=1, source_target_pairs={{0,1},{1,0},{2,3},{3,2},{4,5},{5,4},{6,7},{7,6},{8,9},{9,8},{10,11... | collective-permute-start | bytes 1572872 | tf_op jit(solution)/shard_map/ppermute | solution.py:294
  21.2 4.3 %collective-permute-start.4 = (bf16[128,256]{1,0:T(8,128)(2,1)S(1)}, bf16[128,256]{1,0:T(8,128)(2,1)S(1)}, u32[]{:S(2)}, u32[]{:S(2)}) collective-permute-start(bf16[128,256]{1,0:T(8,128)(2,1)S(1)} %add_convert_fusion.4), channel_id=1, source_target_pairs={{0,2},{1,3},{2,0},{3,1},{4,6},{5,7},{6,4},{7,5},{8,10},{9,11},{10,... | collective-permute-start | bytes 196616 | tf_op jit(solution)/shard_map/ppermute | solution.py:297
  25.6 4.4 %collective-permute-start.6 = (bf16[128,256]{1,0:T(8,128)(2,1)S(1)}, bf16[128,256]{1,0:T(8,128)(2,1)S(1)}, u32[]{:S(2)}, u32[]{:S(2)}) collective-permute-start(bf16[128,256]{1,0:T(8,128)(2,1)S(1)} %add_convert_fusion.3), channel_id=1, source_target_pairs={{0,4},{4,0},{8,12},{12,8},{16,20},{20,16},{24,28},{28,24},{1,5},{5... | collective-permute-start | bytes 196616 | tf_op jit(solution)/shard_map/ppermute | solution.py:297
  27.6 13.3 %collective-permute-start.9 = (bf16[1024,256]{1,0:T(8,128)(2,1)S(1)}, bf16[1024,256]{1,0:T(8,128)(2,1)S(1)}, u32[]{:S(2)}, u32[]{:S(2)}) collective-permute-start(bf16[1024,256]{1,0:T(8,128)(2,1)S(1)} %shard_map.100), channel_id=1, source_target_pairs={{0,2},{1,3},{2,0},{3,1},{4,6},{5,7},{6,4},{7,5},{8,10},{9,11},{10,... | collective-permute-start | bytes 1572872 | tf_op jit(solution)/shard_map/ppermute | solution.py:294
  30.0 10.9 %collective-permute-start.8 = (bf16[1024,256]{1,0:T(8,128)(2,1)S(1)}, bf16[1024,256]{1,0:T(8,128)(2,1)S(1)}, u32[]{:S(2)}, u32[]{:S(2)}) collective-permute-start(bf16[1024,256]{1,0:T(8,128)(2,1)S(1)} %shard_map.101), channel_id=1, source_target_pairs={{0,1},{1,0},{2,3},{3,2},{4,5},{5,4},{6,7},{7,6},{8,9},{9,8},{10,11... | collective-permute-start | bytes 1572872 | tf_op jit(solution)/shard_map/ppermute | solution.py:294
  30.1 4.5 %collective-permute-start.7 = (bf16[128,256]{1,0:T(8,128)(2,1)S(1)}, bf16[128,256]{1,0:T(8,128)(2,1)S(1)}, u32[]{:S(2)}, u32[]{:S(2)}) collective-permute-start(bf16[128,256]{1,0:T(8,128)(2,1)S(1)} %add_convert_fusion.2), channel_id=1, source_target_pairs={{0,8},{4,12},{8,0},{12,4},{16,24},{20,28},{24,16},{28,20},{1,9},{5... | collective-permute-start | bytes 196616 | tf_op jit(solution)/shard_map/ppermute | solution.py:297
  34.6 7.3 %collective-permute-start.10 = (bf16[128,256]{1,0:T(8,128)(2,1)S(1)}, bf16[128,256]{1,0:T(8,128)(2,1)S(1)}, u32[]{:S(2)}, u32[]{:S(2)}) collective-permute-start(bf16[128,256]{1,0:T(8,128)(2,1)S(1)} %add_convert_fusion.1), channel_id=1, source_target_pairs={{0,16},{4,20},{8,24},{12,28},{16,0},{20,4},{24,8},{28,12},{1,17},{... | collective-permute-start | bytes 196616 | tf_op jit(solution)/shard_map/ppermute | solution.py:297
  41.9 1.3 %collective-permute-start.11 = (bf16[128,256]{1,0:T(8,128)(2,1)S(1)}, bf16[128,256]{1,0:T(8,128)(2,1)S(1)}, u32[]{:S(2)}, u32[]{:S(2)}) collective-permute-start(bf16[128,256]{1,0:T(8,128)(2,1)S(1)} %add_convert_fusion), channel_id=1, source_target_pairs={{0,1},{1,0},{2,3},{3,2},{4,5},{5,4},{6,7},{7,6},{8,9},{9,8},{10,11... | collective-permute-start | bytes 196616 | tf_op jit(solution)/shard_map/ppermute | solution.py:294

commit v7 on v6

--- a/solution.py
+++ b/solution.py
@@ -218,7 +218,8 @@
     rows = keep_ref.shape[0]
     core = list_ref[plan.length + plan.cats + 1] & 1
     keep_ref[...] = wg[pl.ds(pl.multiple_of(core * rows, rows), rows), :]
-    send_ref[...] = wg[pl.ds(pl.multiple_of((1 - core) * rows, rows), rows), :]
+    send = wg[pl.ds(pl.multiple_of((1 - core) * rows, rows), rows), :]
+    send_ref[...] = send.astype(send_ref.dtype)
 
 
 def forward(plan, lst, tiles, xs, phases, acc=None, tail=None):
@@ -236,7 +237,7 @@
             pltpu.VMEM((blocks_dev * TILE, hid), BF16),
             jax.ShapeDtypeStruct((blocks_dev * TILE, hid), BF16),
             jax.ShapeDtypeStruct((hid // 2, hid), F32),
-            jax.ShapeDtypeStruct((hid // 2, hid), F32),
+            jax.ShapeDtypeStruct((hid // 2, hid), BF16 if plan.cats > 1 else F32),
         )
         out_specs = (VMEM,) * 4
         scratch.append(pltpu.VMEM((hid, hid), F32))
@@ -317,7 +318,7 @@
     send = swap(send, 1)
     p3 = part(3, sw)
     r3 = swap(p3, 1)
-    w = (keep + send).astype(BF16)
+    w = (keep + send.astype(F32)).astype(BF16)
     q = part(2, tie(sw, w), False, 10)
     q = add_rows(q, r3)
     q_far = swap(q, 2)

time: 44 us -> 43.9 us (level)
  starting transfers between devices: 14.5 us -> 13.7 us
  waiting for transfers between devices: 16.7 us -> 17.2 us
    ppermute x4, starting transfers between devices: 8.83 us -> 7.96 us  [fold(): other = lax.ppermute(w, axis, [(i, i ^ bit) for i in range(size)])]
where the time goes in v7:
time: 43.9 us; the launch traced here: 44 us
  waiting for transfers between devices  17.2 us (39%)
  starting transfers between devices  13.7 us (31%)
  Pallas kernels  8.08 us (18%)
  local copies, waits for them, and re-layouts  2.64 us (6%)
  between operations  1.46 us (3%)
  other arithmetic  0.81 us (2%)
    ppermute x8, waiting for transfers between devices, swap(): return lax.ppermute(x, 'grp', [(i, i ^ bit) for i in range(4)])  12.8 us
    ppermute x4, starting transfers between devices, fold(): other = lax.ppermute(w, axis, [(i, i ^ bit) for i in range(size)])  7.96 us
    ppermute x8, starting transfers between devices, swap(): return lax.ppermute(x, 'grp', [(i, i ^ bit) for i in range(4)])  5.78 us
    ppermute x4, waiting for transfers between devices, fold(): other = lax.ppermute(w, axis, [(i, i ^ bit) for i in range(size)])  4.39 us
    pallas_call x3, Pallas kernels, forward(): pl.pallas_call(body, out_shape=out, in_specs=specs, out_specs=out_specs,...  2.86 us
    unnamed x8, local copies, waits for them, and re-layouts  2.64 us
    pallas_call x4, Pallas kernels, backward(): pl.pallas_call(body, out_shape=jax.ShapeDtypeStruct((blocks * TILE, hid)...  2.29 us
    pallas_call x1, Pallas kernels, prepare(): pl.pallas_call(functools.partial(prep_body, plan, pad_col), out_shape=plt...  1.09 us
  transfers between devices with their start and end apart: 12, of which 7 were waited for; matrix products, arithmetic and copies ran while one was open for 0% of the time, Pallas kernels for 15%

profile of v7, /device:TPU:0, one launch (start us, length us, event | category | flops | bytes accessed | tf_op | source)
XLA Modules:
  0.0 44.0 jit_solution(3349485269126228413)
XLA Ops:
  0.6 0.5 %collective-permute-start.1 = (bf16[1024,256]{1,0:T(8,128)(2,1)}, bf16[1024,256]{1,0:T(8,128)(2,1)S(1)}, u32[]{:S(2)}, u32[]{:S(2)}) collective-permute-start(bf16[1024,256]{1,0:T(8,128)(2,1)} %refs_2_.1), channel_id=1, source_target_pairs={{0,1},{1,0},{2,3},{3,2},{4,5},{5,4},{6,7},{7,6},{8,9},{9,8},{10,11... | collective-permute-start | bytes 1572872 | tf_op jit(solution)/shard_map/ppermute | solution.py:295
  1.1 2.6 %collective-permute-start = (bf16[1024,256]{1,0:T(8,128)(2,1)}, bf16[1024,256]{1,0:T(8,128)(2,1)S(1)}, u32[]{:S(2)}, u32[]{:S(2)}) collective-permute-start(bf16[1024,256]{1,0:T(8,128)(2,1)} %refs_2_.1), channel_id=1, source_target_pairs={{0,2},{1,3},{2,0},{3,1},{4,6},{5,7},{6,4},{7,5},{8,10},{9,11},{10,... | collective-permute-start | bytes 1572872 | tf_op jit(solution)/shard_map/ppermute | solution.py:295
  4.4 1.1 %shard_map.94.refs_0_.list_ref = s32[134]{0:T(256)S(4)} custom-call(s32[1]{0:T(128)} %bitcast.me_ref, s32[1]{0:T(128)S(6)} %copy.10.cnt_ref, s32[64]{0:T(128)} %rows_ref.1, s32[64]{0:T(128)} %cols_ref.1), custom_call_target="tpu_custom_call" | custom-call | tf_op jit(solution)/shard_map/pallas_call | solution.py:69
  5.5 0.0 collective-permute-done.1.refs_3_
  5.5 0.0 copy-start
  5.5 1.6 %copy-done = bf16[64,128,128]{2,1,0:T(8,128)(2,1)S(1)} copy-done((bf16[64,128,128]{2,1,0:T(8,128)(2,1)S(1)}, bf16[64,128,128]{2,1,0:T(8,128)(2,1)}, u32[]{:S(2)}) %copy-start) | copy-done | bytes 2097176
  7.1 0.0 copy-start.1
  7.1 1.0 %copy-done.1 = bf16[1024,256]{1,0:T(8,128)(2,1)S(1)} copy-done((bf16[1024,256]{1,0:T(8,128)(2,1)S(1)}, bf16[1024,256]{1,0:T(8,128)(2,1)}, u32[]{:S(2)}) %copy-start.1) | copy-done | bytes 524312
  8.1 0.9 %shard_map.95.refs_3_ = f32[9,128,256]{2,1,0:T(8,128)S(1)} custom-call(s32[134]{0:T(256)S(4)} %shard_map.94.refs_0_.list_ref, bf16[64,128,128]{2,1,0:T(8,128)(2,1)S(1)} %copy-done, bf16[1024,256]{1,0:T(8,128)(2,1)S(1)} %copy-done.1, bf16[1024,256]{1,0:T(8,128)(2,1)S(1)} %collective-permute-done.1.refs_3_), custom_call_target="tpu_custom_call" | custom-call | tf_op jit(solution)/shard_map/pallas_call | solution.py:251
  9.1 0.0 copy-start.2
  9.1 0.0 copy-start.3
  9.1 7.3 %collective-permute-done.refs_2_ = bf16[1024,256]{1,0:T(8,128)(2,1)S(1)} collective-permute-done((bf16[1024,256]{1,0:T(8,128)(2,1)}, bf16[1024,256]{1,0:T(8,128)(2,1)S(1)}, u32[]{:S(2)}, u32[]{:S(2)}) %collective-permute-start) | collective-permute-done | bytes 524320 | tf_op jit(solution)/shard_map/ppermute | solution.py:295
  16.5 0.0 collective-permute-start.2
  16.5 0.5 %shard_map.96.refs_3_ = f32[9,128,256]{2,1,0:T(8,128)S(1)} custom-call(s32[134]{0:T(256)S(4)} %shard_map.94.refs_0_.list_ref, bf16[64,128,128]{2,1,0:T(8,128)(2,1)S(1)} %copy-done, bf16[1024,256]{1,0:T(8,128)(2,1)S(1)} %collective-permute-done.refs_2_, f32[9,128,256]{2,1,0:T(8,128)S(1)} %shard_map.95.refs_3_), custom_call_target="tpu_custom_call" | custom-call | tf_op jit(solution)/shard_map/pallas_call | solution.py:251
  17.0 1.4 %collective-permute-done.2.refs_2_ = bf16[1024,256]{1,0:T(8,128)(2,1)S(1)} collective-permute-done((bf16[1024,256]{1,0:T(8,128)(2,1)S(1)}, bf16[1024,256]{1,0:T(8,128)(2,1)S(1)}, u32[]{:S(2)}, u32[]{:S(2)}) %collective-permute-start.2) | collective-permute-done | bytes 524320 | tf_op jit(solution)/shard_map/ppermute | solution.py:295
  18.4 0.0 copy-done.2
  18.4 0.0 copy-done.3
  18.4 1.4 %shard_map.97 = (bf16[1024,256]{1,0:T(8,128)(2,1)S(1)}, bf16[1024,256]{1,0:T(8,128)(2,1)S(1)}, f32[128,256]{1,0:T(8,128)S(1)}, bf16[128,256]{1,0:T(8,128)(2,1)S(1)}) custom-call(s32[134]{0:T(256)S(4)} %shard_map.94.refs_0_.list_ref, bf16[64,128,128]{2,1,0:T(8,128)(2,1)S(1)} %copy-done, bf16[1024,256]{1,0:T(8,128)(2,1)S(1)} %collective-permute-done.2.refs_2_, ...), custom_call_target="tpu_custom_call" | custom-call | tf_op jit(solution)/shard_map/pallas_call | solution.py:251
  19.8 0.2 collective-permute-start.3
  20.0 0.6 %shard_map.99 = bf16[1024,256]{1,0:T(8,128)(2,1)S(1)} custom-call(s32[134]{0:T(256)S(4)} %shard_map.94.refs_0_.list_ref, bf16[64,128,128]{2,1,0:T(8,128)(2,1)S(1)} %copy-done, bf16[1024,256]{1,0:T(8,128)(2,1)S(1)} %get-tuple-element.28.s_ref), custom_call_target="tpu_custom_call" | custom-call | bytes 1024 | tf_op jit(solution)/shard_map/pallas_call | solution.py:273
  20.6 0.4 %collective-permute-start.5 = (bf16[1024,256]{1,0:T(8,128)(2,1)S(1)}, bf16[1024,256]{1,0:T(8,128)(2,1)S(1)}, u32[]{:S(2)}, u32[]{:S(2)}) collective-permute-start(bf16[1024,256]{1,0:T(8,128)(2,1)S(1)} %shard_map.99), channel_id=1, source_target_pairs={{0,1},{1,0},{2,3},{3,2},{4,5},{5,4},{6,7},{7,6},{8,9},{9,8},{10,11... | collective-permute-start | bytes 1572872 | tf_op jit(solution)/shard_map/ppermute | solution.py:295
  21.1 0.1 collective-permute-done.3
  21.1 1.8 %collective-permute-start.4 = (bf16[128,256]{1,0:T(8,128)(2,1)S(1)}, bf16[128,256]{1,0:T(8,128)(2,1)S(1)}, u32[]{:S(2)}, u32[]{:S(2)}) collective-permute-start(bf16[128,256]{1,0:T(8,128)(2,1)S(1)} %add_convert_fusion.4), channel_id=1, source_target_pairs={{0,2},{1,3},{2,0},{3,1},{4,6},{5,7},{6,4},{7,5},{8,10},{9,11},{10,... | collective-permute-start | bytes 196616 | tf_op jit(solution)/shard_map/ppermute | solution.py:298
  23.0 0.5 %shard_map.98 = f32[9,128,256]{2,1,0:T(8,128)S(1)} custom-call(s32[134]{0:T(256)S(4)} %shard_map.94.refs_0_.list_ref, bf16[64,128,128]{2,1,0:T(8,128)(2,1)S(1)} %copy-done, bf16[1024,256]{1,0:T(8,128)(2,1)S(1)} %get-tuple-element.28.s_ref), custom_call_target="tpu_custom_call" | custom-call | flops 11000000512 | bytes 1024 | tf_op jit(solution)/shard_map/pallas_call | solution.py:273
  23.5 0.0 collective-permute-done.5.refs_1_
  23.5 0.1 shard_map.100
  23.6 1.8 %collective-permute-done.4 = bf16[128,256]{1,0:T(8,128)(2,1)S(1)} collective-permute-done((bf16[128,256]{1,0:T(8,128)(2,1)S(1)}, bf16[128,256]{1,0:T(8,128)(2,1)S(1)}, u32[]{:S(2)}, u32[]{:S(2)}) %collective-permute-start.4) | collective-permute-done | bytes 65568 | tf_op jit(solution)/shard_map/ppermute | solution.py:298
  25.5 2.3 %collective-permute-start.6 = (bf16[128,256]{1,0:T(8,128)(2,1)S(1)}, bf16[128,256]{1,0:T(8,128)(2,1)S(1)}, u32[]{:S(2)}, u32[]{:S(2)}) collective-permute-start(bf16[128,256]{1,0:T(8,128)(2,1)S(1)} %add_convert_fusion.3), channel_id=1, source_target_pairs={{0,4},{4,0},{8,12},{12,8},{16,20},{20,16},{24,28},{28,24},{1,5},{5... | collective-permute-start | bytes 196616 | tf_op jit(solution)/shard_map/ppermute | solution.py:298
  27.8 1.9 %collective-permute-start.9 = (bf16[1024,256]{1,0:T(8,128)(2,1)S(1)}, bf16[1024,256]{1,0:T(8,128)(2,1)S(1)}, u32[]{:S(2)}, u32[]{:S(2)}) collective-permute-start(bf16[1024,256]{1,0:T(8,128)(2,1)S(1)} %shard_map.100), channel_id=1, source_target_pairs={{0,2},{1,3},{2,0},{3,1},{4,6},{5,7},{6,4},{7,5},{8,10},{9,11},{10,... | collective-permute-start | bytes 1572872 | tf_op jit(solution)/shard_map/ppermute | solution.py:295
  29.6 0.6 %shard_map.101 = bf16[1024,256]{1,0:T(8,128)(2,1)S(1)} custom-call(s32[134]{0:T(256)S(4)} %shard_map.94.refs_0_.list_ref, bf16[64,128,128]{2,1,0:T(8,128)(2,1)S(1)} %copy-done, bf16[1024,256]{1,0:T(8,128)(2,1)S(1)} %get-tuple-element.28.s_ref), custom_call_target="tpu_custom_call" | custom-call | bytes 1024 | tf_op jit(solution)/shard_map/pallas_call | solution.py:273
  30.3 0.0 collective-permute-done.6
  30.3 0.1 collective-permute-start.8
  30.4 1.4 %collective-permute-start.7 = (bf16[128,256]{1,0:T(8,128)(2,1)S(1)}, bf16[128,256]{1,0:T(8,128)(2,1)S(1)}, u32[]{:S(2)}, u32[]{:S(2)}) collective-permute-start(bf16[128,256]{1,0:T(8,128)(2,1)S(1)} %add_convert_fusion.2), channel_id=1, source_target_pairs={{0,8},{4,12},{8,0},{12,4},{16,24},{20,28},{24,16},{28,20},{1,9},{5... | collective-permute-start | bytes 196616 | tf_op jit(solution)/shard_map/ppermute | solution.py:298
  31.8 0.5 %shard_map.102 = f32[9,128,256]{2,1,0:T(8,128)S(1)} custom-call(s32[134]{0:T(256)S(4)} %shard_map.94.refs_0_.list_ref, bf16[64,128,128]{2,1,0:T(8,128)(2,1)S(1)} %copy-done, bf16[1024,256]{1,0:T(8,128)(2,1)S(1)} %get-tuple-element.28.s_ref), custom_call_target="tpu_custom_call" | custom-call | bytes 1024 | tf_op jit(solution)/shard_map/pallas_call | solution.py:273
  32.3 2.5 %collective-permute-done.7 = bf16[128,256]{1,0:T(8,128)(2,1)S(1)} collective-permute-done((bf16[128,256]{1,0:T(8,128)(2,1)S(1)}, bf16[128,256]{1,0:T(8,128)(2,1)S(1)}, u32[]{:S(2)}, u32[]{:S(2)}) %collective-permute-start.7) | collective-permute-done | bytes 65568 | tf_op jit(solution)/shard_map/ppermute | solution.py:298
  34.9 2.5 %collective-permute-start.10 = (bf16[128,256]{1,0:T(8,128)(2,1)S(1)}, bf16[128,256]{1,0:T(8,128)(2,1)S(1)}, u32[]{:S(2)}, u32[]{:S(2)}) collective-permute-start(bf16[128,256]{1,0:T(8,128)(2,1)S(1)} %add_convert_fusion.1), channel_id=1, source_target_pairs={{0,16},{4,20},{8,24},{12,28},{16,0},{20,4},{24,8},{28,12},{1,17},{... | collective-permute-start | bytes 196616 | tf_op jit(solution)/shard_map/ppermute | solution.py:298
  37.4 0.8 %shard_map.103 = bf16[1024,256]{1,0:T(8,128)(2,1)} custom-call(bf16[1024,256]{1,0:T(8,128)(2,1)S(1)} %get-tuple-element.30.x_ref), custom_call_target="tpu_custom_call" | custom-call | bytes 1024 | tf_op jit(solution)/shard_map/pallas_call | solution.py:107
  38.2 2.8 %collective-permute-done.9.refs_2_ = bf16[1024,256]{1,0:T(8,128)(2,1)S(1)} collective-permute-done((bf16[1024,256]{1,0:T(8,128)(2,1)S(1)}, bf16[1024,256]{1,0:T(8,128)(2,1)S(1)}, u32[]{:S(2)}, u32[]{:S(2)}) %collective-permute-start.9) | collective-permute-done | bytes 524320 | tf_op jit(solution)/shard_map/ppermute | solution.py:295
  40.9 0.0 collective-permute-done.8.refs_1_
  40.9 0.9 %shard_map.104 = bf16[1024,256]{1,0:T(8,128)(2,1)} custom-call(f32[1152,256]{1,0:T(8,128)S(1)} %bitcast.3, bf16[1024,256]{1,0:T(8,128)(2,1)S(1)} %collective-permute-done.8.refs_1_, bf16[1024,256]{1,0:T(8,128)(2,1)S(1)} %collective-permute-done.9.refs_2_), custom_call_target="tpu_custom_call" | custom-call | bytes 1024 | tf_op jit(solution)/shard_map/pallas_call | solution.py:128
  41.9 0.0 collective-permute-done.10
  41.9 0.1 collective-permute-start.11
  42.0 1.2 %collective-permute-done.11 = bf16[128,256]{1,0:T(8,128)(2,1)S(1)} collective-permute-done((bf16[128,256]{1,0:T(8,128)(2,1)S(1)}, bf16[128,256]{1,0:T(8,128)(2,1)S(1)}, u32[]{:S(2)}, u32[]{:S(2)}) %collective-permute-start.11) | collective-permute-done | bytes 65568 | tf_op jit(solution)/shard_map/ppermute | solution.py:295
  43.2 0.7 %fusion = f32[256,256]{1,0:T(8,128)} fusion(bf16[128,256]{1,0:T(8,128)(2,1)S(1)} %collective-permute-done.11, bf16[128,256]{1,0:T(8,128)(2,1)S(1)} %add_convert_fusion, pred[]{:T(512)S(6)} %eq.3), kind=kLoop, calls=%fused_computation.1 | loop fusion | flops 655360 | bytes 393217 | tf_op jit(solution)/shard_map/convert_element_type | solution.py:337
  (5 shorter events, 0.1 us)
Async XLA Ops:
  0.6 4.9 %collective-permute-start.1 = (bf16[1024,256]{1,0:T(8,128)(2,1)}, bf16[1024,256]{1,0:T(8,128)(2,1)S(1)}, u32[]{:S(2)}, u32[]{:S(2)}) collective-permute-start(bf16[1024,256]{1,0:T(8,128)(2,1)} %refs_2_.1), channel_id=1, source_target_pairs={{0,1},{1,0},{2,3},{3,2},{4,5},{5,4},{6,7},{7,6},{8,9},{9,8},{10,11... | collective-permute-start | bytes 1572872 | tf_op jit(solution)/shard_map/ppermute | solution.py:295
  1.1 15.3 %collective-permute-start = (bf16[1024,256]{1,0:T(8,128)(2,1)}, bf16[1024,256]{1,0:T(8,128)(2,1)S(1)}, u32[]{:S(2)}, u32[]{:S(2)}) collective-permute-start(bf16[1024,256]{1,0:T(8,128)(2,1)} %refs_2_.1), channel_id=1, source_target_pairs={{0,2},{1,3},{2,0},{3,1},{4,6},{5,7},{6,4},{7,5},{8,10},{9,11},{10,... | collective-permute-start | bytes 1572872 | tf_op jit(solution)/shard_map/ppermute | solution.py:295
  5.5 1.6 %copy-start = (bf16[64,128,128]{2,1,0:T(8,128)(2,1)S(1)}, bf16[64,128,128]{2,1,0:T(8,128)(2,1)}, u32[]{:S(2)}) copy-start(bf16[64,128,128]{2,1,0:T(8,128)(2,1)} %tiles_ref.7) | copy-start | bytes 6291460
  7.1 1.0 %copy-start.1 = (bf16[1024,256]{1,0:T(8,128)(2,1)S(1)}, bf16[1024,256]{1,0:T(8,128)(2,1)}, u32[]{:S(2)}) copy-start(bf16[1024,256]{1,0:T(8,128)(2,1)} %refs_2_.1) | copy-start | bytes 1572868
  9.1 9.3 %copy-start.2 = (bf16[1024,256]{1,0:T(8,128)(2,1)S(1)}, bf16[1024,256]{1,0:T(8,128)(2,1)}, u32[]{:S(2)}) copy-start(bf16[1024,256]{1,0:T(8,128)(2,1)} %refs_5_.1) | copy-start | bytes 1572868
  9.1 9.3 %copy-start.3 = (bf16[256,256]{1,0:T(8,128)(2,1)S(1)}, bf16[256,256]{1,0:T(8,128)(2,1)}, u32[]{:S(2)}) copy-start(bf16[256,256]{1,0:T(8,128)(2,1)} %refs_4_.1) | copy-start | bytes 393220
  16.5 1.9 %collective-permute-start.2 = (bf16[1024,256]{1,0:T(8,128)(2,1)S(1)}, bf16[1024,256]{1,0:T(8,128)(2,1)S(1)}, u32[]{:S(2)}, u32[]{:S(2)}) collective-permute-start(bf16[1024,256]{1,0:T(8,128)(2,1)S(1)} %collective-permute-done.refs_2_), channel_id=1, source_target_pairs={{0,1},{1,0},{2,3},{3,2},{4,5},{5,4},{6,7},{7,6},{8,9},{9,8},{10,11... | collective-permute-start | bytes 1572872 | tf_op jit(solution)/shard_map/ppermute | solution.py:295
  19.8 1.3 %collective-permute-start.3 = (bf16[128,256]{1,0:T(8,128)(2,1)S(1)}, bf16[128,256]{1,0:T(8,128)(2,1)S(1)}, u32[]{:S(2)}, u32[]{:S(2)}) collective-permute-start(bf16[128,256]{1,0:T(8,128)(2,1)S(1)} %get-tuple-element.22), channel_id=1, source_target_pairs={{0,1},{1,0},{2,3},{3,2},{4,5},{5,4},{6,7},{7,6},{8,9},{9,8},{10,11... | collective-permute-start | bytes 196616 | tf_op jit(solution)/shard_map/ppermute | solution.py:295
  20.6 2.9 %collective-permute-start.5 = (bf16[1024,256]{1,0:T(8,128)(2,1)S(1)}, bf16[1024,256]{1,0:T(8,128)(2,1)S(1)}, u32[]{:S(2)}, u32[]{:S(2)}) collective-permute-start(bf16[1024,256]{1,0:T(8,128)(2,1)S(1)} %shard_map.99), channel_id=1, source_target_pairs={{0,1},{1,0},{2,3},{3,2},{4,5},{5,4},{6,7},{7,6},{8,9},{9,8},{10,11... | collective-permute-start | bytes 1572872 | tf_op jit(solution)/shard_map/ppermute | solution.py:295
  21.1 4.3 %collective-permute-start.4 = (bf16[128,256]{1,0:T(8,128)(2,1)S(1)}, bf16[128,256]{1,0:T(8,128)(2,1)S(1)}, u32[]{:S(2)}, u32[]{:S(2)}) collective-permute-start(bf16[128,256]{1,0:T(8,128)(2,1)S(1)} %add_convert_fusion.4), channel_id=1, source_target_pairs={{0,2},{1,3},{2,0},{3,1},{4,6},{5,7},{6,4},{7,5},{8,10},{9,11},{10,... | collective-permute-start | bytes 196616 | tf_op jit(solution)/shard_map/ppermute | solution.py:298
  25.5 4.8 %collective-permute-start.6 = (bf16[128,256]{1,0:T(8,128)(2,1)S(1)}, bf16[128,256]{1,0:T(8,128)(2,1)S(1)}, u32[]{:S(2)}, u32[]{:S(2)}) collective-permute-start(bf16[128,256]{1,0:T(8,128)(2,1)S(1)} %add_convert_fusion.3), channel_id=1, source_target_pairs={{0,4},{4,0},{8,12},{12,8},{16,20},{20,16},{24,28},{28,24},{1,5},{5... | collective-permute-start | bytes 196616 | tf_op jit(solution)/shard_map/ppermute | solution.py:298
  27.8 13.2 %collective-permute-start.9 = (bf16[1024,256]{1,0:T(8,128)(2,1)S(1)}, bf16[1024,256]{1,0:T(8,128)(2,1)S(1)}, u32[]{:S(2)}, u32[]{:S(2)}) collective-permute-start(bf16[1024,256]{1,0:T(8,128)(2,1)S(1)} %shard_map.100), channel_id=1, source_target_pairs={{0,2},{1,3},{2,0},{3,1},{4,6},{5,7},{6,4},{7,5},{8,10},{9,11},{10,... | collective-permute-start | bytes 1572872 | tf_op jit(solution)/shard_map/ppermute | solution.py:295
  30.3 10.6 %collective-permute-start.8 = (bf16[1024,256]{1,0:T(8,128)(2,1)S(1)}, bf16[1024,256]{1,0:T(8,128)(2,1)S(1)}, u32[]{:S(2)}, u32[]{:S(2)}) collective-permute-start(bf16[1024,256]{1,0:T(8,128)(2,1)S(1)} %shard_map.101), channel_id=1, source_target_pairs={{0,1},{1,0},{2,3},{3,2},{4,5},{5,4},{6,7},{7,6},{8,9},{9,8},{10,11... | collective-permute-start | bytes 1572872 | tf_op jit(solution)/shard_map/ppermute | solution.py:295
  30.4 4.5 %collective-permute-start.7 = (bf16[128,256]{1,0:T(8,128)(2,1)S(1)}, bf16[128,256]{1,0:T(8,128)(2,1)S(1)}, u32[]{:S(2)}, u32[]{:S(2)}) collective-permute-start(bf16[128,256]{1,0:T(8,128)(2,1)S(1)} %add_convert_fusion.2), channel_id=1, source_target_pairs={{0,8},{4,12},{8,0},{12,4},{16,24},{20,28},{24,16},{28,20},{1,9},{5... | collective-permute-start | bytes 196616 | tf_op jit(solution)/shard_map/ppermute | solution.py:298
  34.9 7.0 %collective-permute-start.10 = (bf16[128,256]{1,0:T(8,128)(2,1)S(1)}, bf16[128,256]{1,0:T(8,128)(2,1)S(1)}, u32[]{:S(2)}, u32[]{:S(2)}) collective-permute-start(bf16[128,256]{1,0:T(8,128)(2,1)S(1)} %add_convert_fusion.1), channel_id=1, source_target_pairs={{0,16},{4,20},{8,24},{12,28},{16,0},{20,4},{24,8},{28,12},{1,17},{... | collective-permute-start | bytes 196616 | tf_op jit(solution)/shard_map/ppermute | solution.py:298
  41.9 1.3 %collective-permute-start.11 = (bf16[128,256]{1,0:T(8,128)(2,1)S(1)}, bf16[128,256]{1,0:T(8,128)(2,1)S(1)}, u32[]{:S(2)}, u32[]{:S(2)}) collective-permute-start(bf16[128,256]{1,0:T(8,128)(2,1)S(1)} %add_convert_fusion), channel_id=1, source_target_pairs={{0,1},{1,0},{2,3},{3,2},{4,5},{5,4},{6,7},{7,6},{8,9},{9,8},{10,11... | collective-permute-start | bytes 196616 | tf_op jit(solution)/shard_map/ppermute | solution.py:295
